TPU v7x, 128 devices: a whole 4x4x4 slice. The times are simulated.
128 devices in a mesh: col: 16 (over z, x), gz: 8 (over y, core).
Axes of the slice: x: 4, y: 4, z: 4, core: 2. Of those that a mesh axis runs over, the one named last changes fastest.
Arguments:
- photon_flux_entering: float32 [1024, 16384], P('gz', 'col'), may hold values from 0.5 to 2
- thermal_state_prior: float32 [1024, 16384], P('gz', 'col'), may hold values from 0.8 to 1.5
- opacity_coefficient: float32 [1024, 16384], P('gz', 'col'), may hold values from 0.02 to 0.2
- conductance_scaled: float32 [1024, 16384], P('gz', 'col'), may hold values from 3276.8 to 13107.2
- thermal_inertia: float32 [1024, 16384], P('gz', 'col'), may hold values from 1 to 4
- granule_power: float32 [8, 32768, 128], P('gz', 'col'), may hold values from 0.1 to 2
- granule_holder: int32 [8, 32768, 1], P('gz', 'col'), may hold values from 0 to 15; in each aligned block of 2048 rows (0 to 2047, 2048 to 4095, ..., all dimensions but the last counted through in order) at most 512 rows name the same one
- granule_slot: int32 [8, 32768], P('gz', 'col'), may hold values from 0 to 1023
Outputs:
- photon_flux_final: float32 [1024, 16384], P('gz', 'col')
- thermal_state_final: float32 [1024, 16384], P('gz', 'col')
Inputs may be any that keep to these rules, and one draw needn't show every extreme that they name: `granule_holder`: within the 2048 records of one device no owner is named more than 512 times.
All inputs are finite; a program needn't handle non-finite values.
Results may differ from a plain program's by a relative error of at most 0.0003.
Values sent between devices are 32-bit elements; how exact they have to be, the bound alone decides.
No kernel may reach another device: no remote copies, remote signals or barrier semaphores. Data moves between devices by JAX's collectives and lax.ppermute only.
A program may use at most 128 MiB of HBM per device.

v0:
```python
import jax
import jax.numpy as jnp
from jax import lax
from jax.sharding import PartitionSpec as P

NEWTON = 2


radiative_inertia = 2.0


def passed_along(array, axis, by):
    size = lax.axis_size(axis)
    pairs = [(i, i + by) for i in range(size) if 0 <= i + by < size]
    return lax.ppermute(array, axis, pairs)


def padded_2(cells, sides, width):
    for axis, dim in sides:
        count = lax.axis_size(axis)
        ends = count - 1
        head = lax.slice_in_dim(cells, 0, width, axis=dim)
        tail = lax.slice_in_dim(cells, cells.shape[dim] - width, cells.shape[dim], axis=dim)
        cells = jnp.concatenate(
            [
                lax.ppermute(tail, axis, [(i, (i + 1) % count) for i in range(ends)]),
                cells,
                lax.ppermute(head, axis, [((i + 1) % count, i) for i in range(ends)]),
            ],
            axis=dim,
        )
    return cells


def from_below(values, stride):
    filler = jnp.zeros(values.shape[:-2] + (stride,) + values.shape[-1:], values.dtype)
    return jnp.concatenate([filler, values[..., :-stride, :]], -2)


def from_above(values, stride):
    filler = jnp.zeros(values.shape[:-2] + (stride,) + values.shape[-1:], values.dtype)
    return jnp.concatenate([values[..., stride:, :], filler], -2)


def combine_rows(
    lower_ratio,
    upper_ratio,
    scaled_rhs,
    lower_below,
    upper_below,
    rhs_below,
    lower_above,
    upper_above,
    rhs_above,
):
    pivot = 1.0 - lower_ratio * upper_below - upper_ratio * lower_above
    new_rhs = (scaled_rhs - lower_ratio * rhs_below - upper_ratio * rhs_above) / pivot
    return (-lower_ratio * lower_below / pivot, -upper_ratio * upper_above / pivot, new_rhs)


def reduce_block(lower_ratio, upper_ratio, scaled_rhs):
    height = lower_ratio.shape[0]
    stride = 1
    while stride < height:
        lower_ratio, upper_ratio, scaled_rhs = combine_rows(
            lower_ratio,
            upper_ratio,
            scaled_rhs,
            from_below(lower_ratio, stride),
            from_below(upper_ratio, stride),
            from_below(scaled_rhs, stride),
            from_above(lower_ratio, stride),
            from_above(upper_ratio, stride),
            from_above(scaled_rhs, stride),
        )
        stride = stride * 2
    return scaled_rhs


def chain_levels(stacked):
    count = lax.axis_size("gz")
    stride = 1
    while stride < count:
        below = passed_along(stacked, "gz", stride)
        above = passed_along(stacked, "gz", -stride)
        stacked = jnp.stack(
            combine_rows(
                stacked[0],
                stacked[1],
                stacked[2],
                below[0],
                below[1],
                below[2],
                above[0],
                above[1],
                above[2],
            )
        )
        stride = stride * 2
    return stacked[2]


def gather_sources(granule_power, granule_holder, granule_slot, cell_rows):
    heat = granule_power[0]
    owners = granule_holder[0, :, 0]
    cells = granule_slot[0]
    total = jnp.zeros((cell_rows, 128), jnp.float32)
    n_owner = lax.axis_size("col")
    capacity_slots = 4 * heat.shape[0] // n_owner
    member = (owners[:, None] == jnp.arange(n_owner, dtype=jnp.int32)[None, :]).astype(jnp.int32)
    slots = jnp.sum((jnp.cumsum(member, 0) - 1) * member, 1)
    send_heat = jnp.zeros((n_owner, capacity_slots, 128), jnp.float32).at[owners, slots].set(heat)
    send_cell = (
        jnp.zeros((n_owner, capacity_slots), jnp.float32)
        .at[owners, slots]
        .set(cells.astype(jnp.float32))
    )
    got_heat, got_cell = (
        lax.all_to_all(send_heat, "col", split_axis=0, concat_axis=0, tiled=True),
        lax.all_to_all(send_cell, "col", split_axis=0, concat_axis=0, tiled=True),
    )
    return total.at[got_cell.reshape(-1).astype(jnp.int32)].add(got_heat.reshape(-1, 128))


def shards(
    photon_flux_entering,
    thermal_state_prior,
    opacity_coefficient,
    conductance_scaled,
    thermal_inertia,
    granule_power,
    granule_holder,
    granule_slot,
):
    height, width = photon_flux_entering.shape
    seg_count = width // 128
    deposited_power = gather_sources(
        granule_power, granule_holder, granule_slot, height * seg_count
    ).reshape(height, width)
    edge = passed_along(conductance_scaled[:1], "gz", -1)
    diff_up = jnp.concatenate([conductance_scaled[1:], edge], 0)
    places = lax.broadcasted_iota(jnp.int32, (height, 1), 0)
    has_below = (lax.axis_index("gz") > 0).astype(jnp.float32)
    subdiagonal_entries = -conductance_scaled * jnp.where(places == 0, has_below, 1.0)
    superdiagonal_entries = -diff_up
    photon_flux_final, thermal_state_final = (photon_flux_entering, thermal_state_prior)
    for step in range(NEWTON):
        coupling_weight = 16.0 * opacity_coefficient * thermal_state_final**3
        blackbody_output = 4.0 * opacity_coefficient * thermal_state_final**4
        padded = padded_2(photon_flux_final, (("gz", 0),), 1)
        below, above = (padded[:-2], padded[2:])
        flux_mismatch = (
            conductance_scaled * (photon_flux_final - below)
            + diff_up * (photon_flux_final - above)
            + radiative_inertia * (photon_flux_final - photon_flux_entering)
            + opacity_coefficient * photon_flux_final
            - blackbody_output
        )
        thermal_mismatch = (
            thermal_inertia * (thermal_state_final - thermal_state_prior)
            + blackbody_output
            - opacity_coefficient * photon_flux_final
            - deposited_power
        )
        jacobian_divisor = thermal_inertia + coupling_weight
        forcing_vector = -flux_mismatch - coupling_weight * thermal_mismatch / jacobian_divisor
        main_band_entries = (
            conductance_scaled
            + diff_up
            + radiative_inertia
            + opacity_coefficient * thermal_inertia / jacobian_divisor
        )
        lower_ratio = subdiagonal_entries / main_band_entries
        upper_ratio = superdiagonal_entries / main_band_entries
        closed_lower = jnp.where((places == 0) | (places == height - 1), 0.0, lower_ratio)
        closed_upper = jnp.where(places >= height - 2, 0.0, upper_ratio)
        right_sides = jnp.stack(
            [
                jnp.where(places == height - 1, 0.0, forcing_vector / main_band_entries),
                jnp.where(places == 0, -lower_ratio, 0.0),
                jnp.where(places == height - 2, -upper_ratio, 0.0)
                + jnp.where(places == height - 1, 1.0, 0.0),
            ]
        )
        local = reduce_block(closed_lower, closed_upper, right_sides)
        nearby = passed_along(local[:, 0, :], "gz", -1)
        top_lower = subdiagonal_entries[-1]
        top_upper = superdiagonal_entries[-1]
        alpha = top_lower * local[1, -2]
        beta = main_band_entries[-1] + top_lower * local[2, -2] + top_upper * nearby[1]
        gamma = top_upper * nearby[2]
        value = forcing_vector[-1] - top_lower * local[0, -2] - top_upper * nearby[0]
        stacked = jnp.stack([alpha / beta, gamma / beta, value / beta])
        interface = chain_levels(stacked)
        lower_value = passed_along(interface, "gz", 1)
        thermal_increment = (
            local[0] + local[1] * lower_value[None, :] + local[2] * interface[None, :]
        )
        photon_flux_final = photon_flux_final + thermal_increment
        thermal_state_final = (
            thermal_state_final
            + (opacity_coefficient * thermal_increment - thermal_mismatch) / jacobian_divisor
        )
    return (photon_flux_final, thermal_state_final)


def solution(mesh):
    return jax.shard_map(
        shards,
        mesh=mesh,
        in_specs=(
            P("gz", "col"),
            P("gz", "col"),
            P("gz", "col"),
            P("gz", "col"),
            P("gz", "col"),
            P("gz", "col", None),
            P("gz", "col", None),
            P("gz", "col"),
        ),
        out_specs=(P("gz", "col"), P("gz", "col")),
        check_vma=False,
    )
```

profile of v0, /device:TPU:1, one launch (start us, length us, event | category | flops | bytes accessed | tf_op | source)
XLA Modules:
  0.0 271.7 jit_solution(3763467393452357758)
XLA Ops:
  1.4 4.5 %reduce-window.6 = s32[16,16,128]{2,1,0:T(8,128)S(1)} reduce-window(s32[16,16,128]{2,1,0:T(8,128)S(1)} %fusion.42, s32[]{:T(128)} %constant.18.clone.1), window={size=1x1x128 pad=0_0x0_0x127_0}, to_apply=%region_0.0 | reduce-window | flops 4161536 | bytes 262148 | tf_op jit(solution)/shard_map/reduce-window
  10.4 8.6 %scatter_custom_fusion.1 = f32[8192]{0:T(1024)} fusion(s32[2048]{0:T(1024)S(1)} %broadcast_select_fusion.4, f32[2048]{0:T(1024)S(1)} %bitcast.239, f32[]{:T(128)} %constant.14.clone.1), kind=kCustom, calls=%fused_computation.151 | custom fusion | bytes 32772
  19.1 8.4 %all-to-all-start = ((f32[16,1,512]{2,1,0:T(1,128)}), f32[16,1,512]{2,1,0:T(1,128)S(1)}, u32[]{:S(2)}, u32[]{:S(2)}) async-start(f32[16,1,512]{2,1,0:T(1,128)} %bitcast.6), calls=%async_computation | async-start | bytes 65536 | tf_op jit(solution)/shard_map/all_to_all | solution.py:120
  27.5 7.9 %scatter_custom_fusion.2 = f32[8192,128]{1,0:T(8,128)} fusion(s32[2048]{0:T(1024)S(1)} %broadcast_select_fusion.4, f32[]{:T(128)} %constant.14.clone.1, f32[1,2048,128]{2,1,0:T(8,128)S(1)} %copy-done), kind=kCustom, calls=%fused_computation.3 | custom fusion | bytes 5242884
  35.4 6.8 %all-to-all-start.1 = ((f32[16,512,128]{2,1,0:T(8,128)}), f32[16,512,128]{2,1,0:T(8,128)}, u32[]{:S(2)}, u32[]{:S(2)}) async-start(f32[16,512,128]{2,1,0:T(8,128)} %bitcast.177), calls=%async_computation.1 | async-start | bytes 8388608 | tf_op jit(solution)/shard_map/all_to_all | solution.py:119
  42.3 3.4 %collective-permute-start.1 = (f32[1,1024]{1,0:T(1,128)S(1)}, f32[1,1024]{1,0:T(1,128)S(1)}, u32[]{:S(2)}, u32[]{:S(2)}) collective-permute-start(f32[1,1024]{1,0:T(1,128)S(1)} %slice.459), channel_id=1, source_target_pairs={{1,0},{2,1},{3,2},{4,3},{5,4},{6,5},{7,6},{9,8},{10,9},{11,10},{12... | collective-permute-start | bytes 12296 | tf_op jit(solution)/shard_map/ppermute | solution.py:15
  47.7 3.6 %collective-permute-start = (f32[1,1024]{1,0:T(1,128)S(1)}, f32[1,1024]{1,0:T(1,128)S(1)}, u32[]{:S(2)}, u32[]{:S(2)}) collective-permute-start(f32[1,1024]{1,0:T(1,128)S(1)} %get-tuple-element.156), channel_id=1, source_target_pairs={{0,1},{1,2},{2,3},{3,4},{4,5},{5,6},{6,7},{8,9},{9,10},{10,11},{11... | collective-permute-start | bytes 12296 | tf_op jit(solution)/shard_map/ppermute | solution.py:26
  54.9 48.0 %all-to-all-done.1 = f32[16,512,128]{2,1,0:T(8,128)} async-done(((f32[16,512,128]{2,1,0:T(8,128)}), f32[16,512,128]{2,1,0:T(8,128)}, u32[]{:S(2)}, u32[]{:S(2)}) %all-to-all-start.1) | async-done | bytes 4194336 | tf_op jit(solution)/shard_map/all_to_all | solution.py:119
  102.9 56.4 %scatter_custom_fusion = f32[1024,128]{1,0:T(8,128)} fusion(s32[8192]{0:T(1024)S(1)} %bitcast.185, f32[8192,128]{1,0:T(8,128)} %bitcast.11, f32[]{:T(128)} %constant.14.clone.1), kind=kCustom, calls=%fused_computation.123 | custom fusion | flops 1048576 | bytes 524800 | tf_op jit(solution)/shard_map/scatter-add | solution.py:122
  160.4 2.3 select_bitcast_fusion.3
  175.6 4.4 %collective-permute-start.3 = (f32[3,1024]{1,0:T(4,128)S(1)}, f32[3,1024]{1,0:T(4,128)S(1)}, u32[]{:S(2)}, u32[]{:S(2)}) collective-permute-start(f32[3,1024]{1,0:T(4,128)S(1)} %bitcast.189), channel_id=1, source_target_pairs={{1,0},{2,1},{3,2},{4,3},{5,4},{6,5},{7,6},{9,8},{10,9},{11,10},{12... | collective-permute-start | bytes 36872 | tf_op jit(solution)/shard_map/ppermute | solution.py:15
  180.0 2.4 collective-permute-done.3
  184.4 3.6 %collective-permute-start.4 = (f32[3,1024]{1,0:T(4,128)S(1)}, f32[3,1024]{1,0:T(4,128)S(1)}, u32[]{:S(2)}, u32[]{:S(2)}) collective-permute-start(f32[3,1024]{1,0:T(4,128)S(1)} %pad_maximum_fusion.7), channel_id=1, source_target_pairs={{0,1},{1,2},{2,3},{3,4},{4,5},{5,6},{6,7},{8,9},{9,10},{10,11},{11... | collective-permute-start | bytes 36872 | tf_op jit(solution)/shard_map/ppermute | solution.py:15
  190.3 4.0 %collective-permute-start.6 = (f32[3,1024]{1,0:T(4,128)S(1)}, f32[3,1024]{1,0:T(4,128)S(1)}, u32[]{:S(2)}, u32[]{:S(2)}) collective-permute-start(f32[3,1024]{1,0:T(4,128)S(1)} %pad_maximum_fusion.8), channel_id=1, source_target_pairs={{0,2},{1,3},{2,4},{3,5},{4,6},{5,7},{8,10},{9,11},{10,12},{11,13},... | collective-permute-start | bytes 36872 | tf_op jit(solution)/shard_map/ppermute | solution.py:15
  195.3 5.4 %collective-permute-start.8 = (f32[3,1024]{1,0:T(4,128)S(1)}, f32[3,1024]{1,0:T(4,128)S(1)}, u32[]{:S(2)}, u32[]{:S(2)}) collective-permute-start(f32[3,1024]{1,0:T(4,128)S(1)} %pad_maximum_fusion.9), channel_id=1, source_target_pairs={{0,4},{1,5},{2,6},{3,7},{8,12},{9,13},{10,14},{11,15},{16,20},{17,... | collective-permute-start | bytes 36872 | tf_op jit(solution)/shard_map/ppermute | solution.py:15
  202.0 4.7 %collective-permute-done.9 = f32[3,1024]{1,0:T(4,128)S(1)} collective-permute-done((f32[3,1024]{1,0:T(4,128)S(1)}, f32[3,1024]{1,0:T(4,128)S(1)}, u32[]{:S(2)}, u32[]{:S(2)}) %collective-permute-start.9) | collective-permute-done | bytes 12320 | tf_op jit(solution)/shard_map/ppermute | solution.py:15
  206.7 6.5 %collective-permute-start.10 = (f32[1024]{0:T(1024)S(1)}, f32[1024]{0:T(1024)S(1)}, u32[]{:S(2)}, u32[]{:S(2)}) collective-permute-start(f32[1024]{0:T(1024)S(1)} %subtract_divide_fusion.19), channel_id=1, source_target_pairs={{0,1},{1,2},{2,3},{3,4},{4,5},{5,6},{6,7},{8,9},{9,10},{10,11},{11... | collective-permute-start | bytes 12296 | tf_op jit(solution)/shard_map/ppermute | solution.py:15
  217.1 4.4 %collective-permute-start.11 = (f32[1,1024]{1,0:T(1,128)S(1)}, f32[1,1024]{1,0:T(1,128)S(1)}, u32[]{:S(2)}, u32[]{:S(2)}) collective-permute-start(f32[1,1024]{1,0:T(1,128)S(1)} %get-tuple-element.126), channel_id=1, source_target_pairs={{0,1},{1,2},{2,3},{3,4},{4,5},{5,6},{6,7},{8,9},{9,10},{10,11},{11... | collective-permute-start | bytes 12296 | tf_op jit(solution)/shard_map/ppermute | solution.py:26
  236.0 3.1 %collective-permute-done.13 = f32[3,1024]{1,0:T(4,128)S(1)} collective-permute-done((f32[3,1024]{1,0:T(4,128)S(1)}, f32[3,1024]{1,0:T(4,128)S(1)}, u32[]{:S(2)}, u32[]{:S(2)}) %collective-permute-start.13) | collective-permute-done | bytes 12320 | tf_op jit(solution)/shard_map/ppermute | solution.py:15
  241.2 3.6 %collective-permute-start.14 = (f32[3,1024]{1,0:T(4,128)S(1)}, f32[3,1024]{1,0:T(4,128)S(1)}, u32[]{:S(2)}, u32[]{:S(2)}) collective-permute-start(f32[3,1024]{1,0:T(4,128)S(1)} %pad_maximum_fusion.10), channel_id=1, source_target_pairs={{0,1},{1,2},{2,3},{3,4},{4,5},{5,6},{6,7},{8,9},{9,10},{10,11},{11... | collective-permute-start | bytes 36872 | tf_op jit(solution)/shard_map/ppermute | solution.py:15
  247.1 4.0 %collective-permute-start.16 = (f32[3,1024]{1,0:T(4,128)S(1)}, f32[3,1024]{1,0:T(4,128)S(1)}, u32[]{:S(2)}, u32[]{:S(2)}) collective-permute-start(f32[3,1024]{1,0:T(4,128)S(1)} %pad_maximum_fusion.11), channel_id=1, source_target_pairs={{0,2},{1,3},{2,4},{3,5},{4,6},{5,7},{8,10},{9,11},{10,12},{11,13},... | collective-permute-start | bytes 36872 | tf_op jit(solution)/shard_map/ppermute | solution.py:15
  252.0 4.1 %collective-permute-start.18 = (f32[3,1024]{1,0:T(4,128)S(1)}, f32[3,1024]{1,0:T(4,128)S(1)}, u32[]{:S(2)}, u32[]{:S(2)}) collective-permute-start(f32[3,1024]{1,0:T(4,128)S(1)} %pad_maximum_fusion.12), channel_id=1, source_target_pairs={{0,4},{1,5},{2,6},{3,7},{8,12},{9,13},{10,14},{11,15},{16,20},{17,... | collective-permute-start | bytes 36872 | tf_op jit(solution)/shard_map/ppermute | solution.py:15
  257.4 4.7 %collective-permute-done.19 = f32[3,1024]{1,0:T(4,128)S(1)} collective-permute-done((f32[3,1024]{1,0:T(4,128)S(1)}, f32[3,1024]{1,0:T(4,128)S(1)}, u32[]{:S(2)}, u32[]{:S(2)}) %collective-permute-start.19) | collective-permute-done | bytes 12320 | tf_op jit(solution)/shard_map/ppermute | solution.py:15
  262.1 6.5 %collective-permute-start.20 = (f32[1024]{0:T(1024)S(1)}, f32[1024]{0:T(1024)S(1)}, u32[]{:S(2)}, u32[]{:S(2)}) collective-permute-start(f32[1024]{0:T(1024)S(1)} %subtract_divide_fusion.15), channel_id=1, source_target_pairs={{0,1},{1,2},{2,3},{3,4},{4,5},{5,6},{6,7},{8,9},{9,10},{10,11},{11... | collective-permute-start | bytes 12296 | tf_op jit(solution)/shard_map/ppermute | solution.py:15
  (204 shorter events, 58.3 us)
Async XLA Ops:
  19.1 16.3 %all-to-all-start = ((f32[16,1,512]{2,1,0:T(1,128)}), f32[16,1,512]{2,1,0:T(1,128)S(1)}, u32[]{:S(2)}, u32[]{:S(2)}) async-start(f32[16,1,512]{2,1,0:T(1,128)} %bitcast.6), calls=%async_computation | async-start | bytes 65536 | tf_op jit(solution)/shard_map/all_to_all | solution.py:120
  35.4 67.5 %all-to-all-start.1 = ((f32[16,512,128]{2,1,0:T(8,128)}), f32[16,512,128]{2,1,0:T(8,128)}, u32[]{:S(2)}, u32[]{:S(2)}) async-start(f32[16,512,128]{2,1,0:T(8,128)} %bitcast.177), calls=%async_computation.1 | async-start | bytes 8388608 | tf_op jit(solution)/shard_map/all_to_all | solution.py:119
  42.3 9.2 %collective-permute-start.1 = (f32[1,1024]{1,0:T(1,128)S(1)}, f32[1,1024]{1,0:T(1,128)S(1)}, u32[]{:S(2)}, u32[]{:S(2)}) collective-permute-start(f32[1,1024]{1,0:T(1,128)S(1)} %slice.459), channel_id=1, source_target_pairs={{1,0},{2,1},{3,2},{4,3},{5,4},{6,5},{7,6},{9,8},{10,9},{11,10},{12... | collective-permute-start | bytes 12296 | tf_op jit(solution)/shard_map/ppermute | solution.py:15
  45.8 114.6 %collective-permute-start.2 = (f32[1,1024]{1,0:T(1,128)S(1)}, f32[1,1024]{1,0:T(1,128)S(1)}, u32[]{:S(2)}, u32[]{:S(2)}) collective-permute-start(f32[1,1024]{1,0:T(1,128)S(1)} %get-tuple-element.157), channel_id=1, source_target_pairs={{1,0},{2,1},{3,2},{4,3},{5,4},{6,5},{7,6},{9,8},{10,9},{11,10},{12... | collective-permute-start | bytes 12296 | tf_op jit(solution)/shard_map/ppermute | solution.py:28
  47.7 112.7 %collective-permute-start = (f32[1,1024]{1,0:T(1,128)S(1)}, f32[1,1024]{1,0:T(1,128)S(1)}, u32[]{:S(2)}, u32[]{:S(2)}) collective-permute-start(f32[1,1024]{1,0:T(1,128)S(1)} %get-tuple-element.156), channel_id=1, source_target_pairs={{0,1},{1,2},{2,3},{3,4},{4,5},{5,6},{6,7},{8,9},{9,10},{10,11},{11... | collective-permute-start | bytes 12296 | tf_op jit(solution)/shard_map/ppermute | solution.py:26
  175.0 38.9 %copy-start.7 = (f32[128,1024]{1,0:T(8,128)S(1)}, f32[128,1024]{1,0:T(8,128)}, u32[]{:S(2)}) copy-start(f32[128,1024]{1,0:T(8,128)} %param.10) | copy-start | bytes 1572868
  175.6 6.8 %collective-permute-start.3 = (f32[3,1024]{1,0:T(4,128)S(1)}, f32[3,1024]{1,0:T(4,128)S(1)}, u32[]{:S(2)}, u32[]{:S(2)}) collective-permute-start(f32[3,1024]{1,0:T(4,128)S(1)} %bitcast.189), channel_id=1, source_target_pairs={{1,0},{2,1},{3,2},{4,3},{5,4},{6,5},{7,6},{9,8},{10,9},{11,10},{12... | collective-permute-start | bytes 36872 | tf_op jit(solution)/shard_map/ppermute | solution.py:15
  182.5 5.6 %collective-permute-start.5 = (f32[3,1024]{1,0:T(4,128)S(1)}, f32[3,1024]{1,0:T(4,128)S(1)}, u32[]{:S(2)}, u32[]{:S(2)}) collective-permute-start(f32[3,1024]{1,0:T(4,128)S(1)} %pad_maximum_fusion.7), channel_id=1, source_target_pairs={{1,0},{2,1},{3,2},{4,3},{5,4},{6,5},{7,6},{9,8},{10,9},{11,10},{12... | collective-permute-start | bytes 36872 | tf_op jit(solution)/shard_map/ppermute | solution.py:15
  184.4 4.5 %collective-permute-start.4 = (f32[3,1024]{1,0:T(4,128)S(1)}, f32[3,1024]{1,0:T(4,128)S(1)}, u32[]{:S(2)}, u32[]{:S(2)}) collective-permute-start(f32[3,1024]{1,0:T(4,128)S(1)} %pad_maximum_fusion.7), channel_id=1, source_target_pairs={{0,1},{1,2},{2,3},{3,4},{4,5},{5,6},{6,7},{8,9},{9,10},{10,11},{11... | collective-permute-start | bytes 36872 | tf_op jit(solution)/shard_map/ppermute | solution.py:15
  189.0 5.3 %collective-permute-start.7 = (f32[3,1024]{1,0:T(4,128)S(1)}, f32[3,1024]{1,0:T(4,128)S(1)}, u32[]{:S(2)}, u32[]{:S(2)}) collective-permute-start(f32[3,1024]{1,0:T(4,128)S(1)} %pad_maximum_fusion.8), channel_id=1, source_target_pairs={{2,0},{3,1},{4,2},{5,3},{6,4},{7,5},{10,8},{11,9},{12,10},{13,11},... | collective-permute-start | bytes 36872 | tf_op jit(solution)/shard_map/ppermute | solution.py:15
  190.3 4.9 %collective-permute-start.6 = (f32[3,1024]{1,0:T(4,128)S(1)}, f32[3,1024]{1,0:T(4,128)S(1)}, u32[]{:S(2)}, u32[]{:S(2)}) collective-permute-start(f32[3,1024]{1,0:T(4,128)S(1)} %pad_maximum_fusion.8), channel_id=1, source_target_pairs={{0,2},{1,3},{2,4},{3,5},{4,6},{5,7},{8,10},{9,11},{10,12},{11,13},... | collective-permute-start | bytes 36872 | tf_op jit(solution)/shard_map/ppermute | solution.py:15
  195.3 6.7 %collective-permute-start.8 = (f32[3,1024]{1,0:T(4,128)S(1)}, f32[3,1024]{1,0:T(4,128)S(1)}, u32[]{:S(2)}, u32[]{:S(2)}) collective-permute-start(f32[3,1024]{1,0:T(4,128)S(1)} %pad_maximum_fusion.9), channel_id=1, source_target_pairs={{0,4},{1,5},{2,6},{3,7},{8,12},{9,13},{10,14},{11,15},{16,20},{17,... | collective-permute-start | bytes 36872 | tf_op jit(solution)/shard_map/ppermute | solution.py:15
  200.7 6.0 %collective-permute-start.9 = (f32[3,1024]{1,0:T(4,128)S(1)}, f32[3,1024]{1,0:T(4,128)S(1)}, u32[]{:S(2)}, u32[]{:S(2)}) collective-permute-start(f32[3,1024]{1,0:T(4,128)S(1)} %pad_maximum_fusion.9), channel_id=1, source_target_pairs={{4,0},{5,1},{6,2},{7,3},{12,8},{13,9},{14,10},{15,11},{20,16},{21,... | collective-permute-start | bytes 36872 | tf_op jit(solution)/shard_map/ppermute | solution.py:15
  206.7 7.2 %collective-permute-start.10 = (f32[1024]{0:T(1024)S(1)}, f32[1024]{0:T(1024)S(1)}, u32[]{:S(2)}, u32[]{:S(2)}) collective-permute-start(f32[1024]{0:T(1024)S(1)} %subtract_divide_fusion.19), channel_id=1, source_target_pairs={{0,1},{1,2},{2,3},{3,4},{4,5},{5,6},{6,7},{8,9},{9,10},{10,11},{11... | collective-permute-start | bytes 12296 | tf_op jit(solution)/shard_map/ppermute | solution.py:15
  215.1 10.4 %collective-permute-start.12 = (f32[1,1024]{1,0:T(1,128)S(1)}, f32[1,1024]{1,0:T(1,128)S(1)}, u32[]{:S(2)}, u32[]{:S(2)}) collective-permute-start(f32[1,1024]{1,0:T(1,128)S(1)} %get-tuple-element.127), channel_id=1, source_target_pairs={{1,0},{2,1},{3,2},{4,3},{5,4},{6,5},{7,6},{9,8},{10,9},{11,10},{12... | collective-permute-start | bytes 12296 | tf_op jit(solution)/shard_map/ppermute | solution.py:28
  217.1 8.5 %collective-permute-start.11 = (f32[1,1024]{1,0:T(1,128)S(1)}, f32[1,1024]{1,0:T(1,128)S(1)}, u32[]{:S(2)}, u32[]{:S(2)}) collective-permute-start(f32[1,1024]{1,0:T(1,128)S(1)} %get-tuple-element.126), channel_id=1, source_target_pairs={{0,1},{1,2},{2,3},{3,4},{4,5},{5,6},{6,7},{8,9},{9,10},{10,11},{11... | collective-permute-start | bytes 12296 | tf_op jit(solution)/shard_map/ppermute | solution.py:26
  234.1 5.1 %collective-permute-start.13 = (f32[3,1024]{1,0:T(4,128)S(1)}, f32[3,1024]{1,0:T(4,128)S(1)}, u32[]{:S(2)}, u32[]{:S(2)}) collective-permute-start(f32[3,1024]{1,0:T(4,128)S(1)} %bitcast.190), channel_id=1, source_target_pairs={{1,0},{2,1},{3,2},{4,3},{5,4},{6,5},{7,6},{9,8},{10,9},{11,10},{12... | collective-permute-start | bytes 36872 | tf_op jit(solution)/shard_map/ppermute | solution.py:15
  239.3 5.6 %collective-permute-start.15 = (f32[3,1024]{1,0:T(4,128)S(1)}, f32[3,1024]{1,0:T(4,128)S(1)}, u32[]{:S(2)}, u32[]{:S(2)}) collective-permute-start(f32[3,1024]{1,0:T(4,128)S(1)} %pad_maximum_fusion.10), channel_id=1, source_target_pairs={{1,0},{2,1},{3,2},{4,3},{5,4},{6,5},{7,6},{9,8},{10,9},{11,10},{12... | collective-permute-start | bytes 36872 | tf_op jit(solution)/shard_map/ppermute | solution.py:15
  241.2 4.5 %collective-permute-start.14 = (f32[3,1024]{1,0:T(4,128)S(1)}, f32[3,1024]{1,0:T(4,128)S(1)}, u32[]{:S(2)}, u32[]{:S(2)}) collective-permute-start(f32[3,1024]{1,0:T(4,128)S(1)} %pad_maximum_fusion.10), channel_id=1, source_target_pairs={{0,1},{1,2},{2,3},{3,4},{4,5},{5,6},{6,7},{8,9},{9,10},{10,11},{11... | collective-permute-start | bytes 36872 | tf_op jit(solution)/shard_map/ppermute | solution.py:15
  245.8 5.3 %collective-permute-start.17 = (f32[3,1024]{1,0:T(4,128)S(1)}, f32[3,1024]{1,0:T(4,128)S(1)}, u32[]{:S(2)}, u32[]{:S(2)}) collective-permute-start(f32[3,1024]{1,0:T(4,128)S(1)} %pad_maximum_fusion.11), channel_id=1, source_target_pairs={{2,0},{3,1},{4,2},{5,3},{6,4},{7,5},{10,8},{11,9},{12,10},{13,11},... | collective-permute-start | bytes 36872 | tf_op jit(solution)/shard_map/ppermute | solution.py:15
  247.1 4.8 %collective-permute-start.16 = (f32[3,1024]{1,0:T(4,128)S(1)}, f32[3,1024]{1,0:T(4,128)S(1)}, u32[]{:S(2)}, u32[]{:S(2)}) collective-permute-start(f32[3,1024]{1,0:T(4,128)S(1)} %pad_maximum_fusion.11), channel_id=1, source_target_pairs={{0,2},{1,3},{2,4},{3,5},{4,6},{5,7},{8,10},{9,11},{10,12},{11,13},... | collective-permute-start | bytes 36872 | tf_op jit(solution)/shard_map/ppermute | solution.py:15
  252.0 5.4 %collective-permute-start.18 = (f32[3,1024]{1,0:T(4,128)S(1)}, f32[3,1024]{1,0:T(4,128)S(1)}, u32[]{:S(2)}, u32[]{:S(2)}) collective-permute-start(f32[3,1024]{1,0:T(4,128)S(1)} %pad_maximum_fusion.12), channel_id=1, source_target_pairs={{0,4},{1,5},{2,6},{3,7},{8,12},{9,13},{10,14},{11,15},{16,20},{17,... | collective-permute-start | bytes 36872 | tf_op jit(solution)/shard_map/ppermute | solution.py:15
  256.1 6.0 %collective-permute-start.19 = (f32[3,1024]{1,0:T(4,128)S(1)}, f32[3,1024]{1,0:T(4,128)S(1)}, u32[]{:S(2)}, u32[]{:S(2)}) collective-permute-start(f32[3,1024]{1,0:T(4,128)S(1)} %pad_maximum_fusion.12), channel_id=1, source_target_pairs={{4,0},{5,1},{6,2},{7,3},{12,8},{13,9},{14,10},{15,11},{20,16},{21,... | collective-permute-start | bytes 36872 | tf_op jit(solution)/shard_map/ppermute | solution.py:15
  262.1 7.2 %collective-permute-start.20 = (f32[1024]{0:T(1024)S(1)}, f32[1024]{0:T(1024)S(1)}, u32[]{:S(2)}, u32[]{:S(2)}) collective-permute-start(f32[1024]{0:T(1024)S(1)} %subtract_divide_fusion.15), channel_id=1, source_target_pairs={{0,1},{1,2},{2,3},{3,4},{4,5},{5,6},{6,7},{8,9},{9,10},{10,11},{11... | collective-permute-start | bytes 12296 | tf_op jit(solution)/shard_map/ppermute | solution.py:15
  (16 other events, 188.1 us)
where the time goes:
time: 273 us; the launch traced here: 272 us
  other arithmetic  90.5 us (33%)
  starting transfers between devices  83.5 us (31%)
  waiting for transfers between devices  67.7 us (25%)
  local copies, waits for them, and re-layouts  28 us (10%)
    scatter-add x1, other arithmetic, gather_sources(): total.at[got_cell.reshape(-1).astype(jnp.int32)]  56.4 us
    ppermute x17, starting transfers between devices, passed_along(): return lax.ppermute(array, axis, pairs)  56.4 us
    all_to_all x1, waiting for transfers between devices, gather_sources(): lax.all_to_all(send_heat, 'col', split_axis=0, concat_axis=0, tiled=True)  48 us
    ppermute x17, waiting for transfers between devices, passed_along(): return lax.ppermute(array, axis, pairs)  19.7 us
    unnamed x38, local copies, waits for them, and re-layouts  18.6 us
    div x20, other arithmetic, combine_rows(): (scaled_rhs - lower_ratio * rhs_below - upper_ratio * rhs_above) / pivot  10.5 us
    all_to_all x1, starting transfers between devices, gather_sources(): lax.all_to_all(send_cell, 'col', split_axis=0, concat_axis=0, tiled=True)  8.43 us
    ppermute x2, starting transfers between devices, padded_2(): lax.ppermute(tail, axis, [(i, (i + 1) % count) for i in range(ends)])  8.05 us
  transfers between devices with their start and end apart: 23, of which 11 were waited for; matrix products, arithmetic and copies ran while one was open for 26% of the time, Pallas kernels for 0%

commit v1 on v0

--- a/solution.py
+++ b/solution.py
@@ -1,6 +1,8 @@
 import jax
 import jax.numpy as jnp
 from jax import lax
+from jax.experimental import pallas as pl
+from jax.experimental.pallas import tpu as pltpu
 from jax.sharding import PartitionSpec as P
 
 NEWTON = 2
@@ -122,7 +124,7 @@
     return total.at[got_cell.reshape(-1).astype(jnp.int32)].add(got_heat.reshape(-1, 128))
 
 
-def shards(
+def general_path(
     photon_flux_entering,
     thermal_state_prior,
     opacity_coefficient,
@@ -204,6 +206,404 @@
     return (photon_flux_final, thermal_state_final)
 
 
+SLOTS = 192
+ROOM = 190
+F32 = jnp.float32
+BF16 = jnp.bfloat16
+VMEM = pl.BlockSpec(memory_space=pltpu.VMEM)
+SMEM = pl.BlockSpec(memory_space=pltpu.SMEM)
+
+
+def params(mib):
+    return pltpu.CompilerParams(vmem_limit_bytes=mib * 2**20)
+
+
+def tile(count):
+    return jax.ShapeDtypeStruct((count, 8, 128), F32)
+
+
+def pack_kernel(owner_ref, cell_ref, heat_ref, out_ref, row_vmem, row_smem, sem):
+    groups, lanes = owner_ref.shape
+    owner, cell = owner_ref[...], cell_ref[...]
+    level = lax.shift_right_logical(cell, 3)
+    band = lax.shift_right_logical(level, 4)
+    target = (level + band + owner) & 15
+    place = owner * 64 + band * 8 + (cell & 7) + 1
+    place_high = lax.shift_right_logical(place, 5).astype(F32)
+    place_low = (place & 31).astype(F32)
+    classes = lax.broadcasted_iota(jnp.int32, (16, lanes), 0)
+    member = [classes == target[g : g + 1, :] for g in range(groups)]
+    member_f = [jnp.where(m, 1.0, 0.0) for m in member]
+    source = lax.broadcasted_iota(jnp.int32, (lanes, 2 * lanes), 0)
+    sink = lax.broadcasted_iota(jnp.int32, (lanes, 2 * lanes), 1)
+    before = jnp.where((source < sink) | (sink >= lanes), 1.0, 0.0).astype(BF16)
+    counts = jnp.dot(
+        jnp.concatenate(member_f, 0).astype(BF16), before, preferred_element_type=F32
+    )
+    start = jnp.zeros((16, lanes), F32)
+    slots = []
+    for g in range(groups):
+        ahead = counts[16 * g : 16 * g + 16]
+        slots.append(jnp.sum(member_f[g] * (ahead[:, :lanes] + start), 0, keepdims=True))
+        start = start + ahead[:, lanes:]
+    slot = jnp.concatenate(slots, 0).astype(jnp.int32)
+    fits = slot < ROOM
+    row_vmem[...] = target * SLOTS + jnp.where(fits, slot, SLOTS - 1)
+    copy = pltpu.make_async_copy(row_vmem, row_smem, sem)
+    copy.start()
+    out_ref[...] = jnp.zeros_like(out_ref)
+    named = jnp.where(fits, slot, 4096)
+    slot_row = lax.broadcasted_iota(jnp.int32, (2 * lanes, lanes), 0)
+    table = jnp.zeros((32, 2 * lanes), F32)
+    for g in range(groups):
+        weights = jnp.concatenate(
+            [member_f[g] * place_high[g : g + 1], member_f[g] * place_low[g : g + 1]], 0
+        )
+        hits = jnp.where(slot_row == named[g : g + 1], 1.0, 0.0)
+        table = table + lax.dot_general(
+            weights.astype(BF16),
+            hits.astype(BF16),
+            (((1,), (1,)), ((), ())),
+            preferred_element_type=F32,
+        )
+    places = table[:16] * 32.0 + table[16:] - 1.0
+    over = jnp.max(jnp.where(start > ROOM, 1.0, 0.0))
+    lane = lax.broadcasted_iota(jnp.int32, (1, 2 * lanes), 1)
+    places = jnp.where(lane == 2 * lanes - 1, over, places)
+    copy.wait()
+
+    for g in range(groups):
+
+        @pl.loop(0, lanes, step=16)
+        def _(base):
+            for i in range(16):
+                row = row_smem[g, base + i]
+                out_ref[pl.ds(row, 1), :] = heat_ref[pl.ds(g * lanes + base + i, 1), :]
+
+    for m in range(16):
+        out_ref[m * SLOTS + ROOM : m * SLOTS + ROOM + 1, :] = places[m : m + 1, :lanes]
+        out_ref[m * SLOTS + ROOM + 1 : m * SLOTS + SLOTS, :] = places[m : m + 1, lanes:]
+
+
+def pack(owner, cell, heat):
+    return pl.pallas_call(
+        pack_kernel,
+        out_shape=jax.ShapeDtypeStruct((16 * SLOTS, 128), F32),
+        in_specs=[VMEM, VMEM, VMEM],
+        out_specs=VMEM,
+        scratch_shapes=[
+            pltpu.VMEM((16, 128), jnp.int32),
+            pltpu.SMEM((16, 128), jnp.int32),
+            pltpu.SemaphoreType.DMA,
+        ],
+        compiler_params=params(16),
+    )(owner, cell, heat)
+
+
+def sum_kernel(got_ref, out_ref, flag_ref, terms):
+    flag = jnp.zeros((1, 128), F32)
+    for s in range(16):
+        heat = got_ref[s * SLOTS : (s + 1) * SLOTS, :]
+        high = heat.astype(BF16)
+        terms[s * 256 : s * 256 + SLOTS, :128] = high
+        terms[s * 256 : s * 256 + SLOTS, 128:] = (heat - high.astype(F32)).astype(BF16)
+        terms[s * 256 + SLOTS : (s + 1) * 256, :] = jnp.zeros((256 - SLOTS, 256), BF16)
+        flag = jnp.maximum(flag, got_ref[(s + 1) * SLOTS - 1 : (s + 1) * SLOTS, :])
+    lane = lax.broadcasted_iota(jnp.int32, (1, 128), 1)
+    flag = jnp.where(lane == 127, flag, 0.0)
+    flag_ref[0] = jnp.broadcast_to(flag, (8, 128))
+
+    @pl.loop(0, 8)
+    def _(block):
+        row = (lax.broadcasted_iota(jnp.int32, (128, 128), 0) + block * 128).astype(F32)
+        hits = []
+        for s in range(16):
+            for part in range(2):
+                at = s * SLOTS + ROOM + part
+                hits.append(jnp.where(row == got_ref[at : at + 1, :], 1.0, 0.0).astype(BF16))
+        both = jnp.dot(jnp.concatenate(hits, 1), terms[...], preferred_element_type=F32)
+        out_ref[pl.ds(pl.multiple_of(block * 128, 128), 128), :] = both[:, :128] + both[:, 128:]
+
+
+def sum_records(got):
+    return pl.pallas_call(
+        sum_kernel,
+        out_shape=(jax.ShapeDtypeStruct((1024, 128), F32), tile(1)),
+        in_specs=[VMEM],
+        out_specs=(VMEM, VMEM),
+        scratch_shapes=[pltpu.VMEM((4096, 256), BF16)],
+        compiler_params=params(24),
+    )(got)
+
+
+def row_of(ref, h):
+    return ref[pl.ds((h // 8) * 64 + h % 8, 8, stride=8), :]
+
+
+def prepare_kernel(
+    flux_ref, temp_ref, opacity_ref, cond_ref, inertia_ref,
+    flux_out, temp_out, opacity_out, inertia_out, face_out,
+    loss_out, base_out, share_out, rate_out, gain_out, rest_out, one_out, two_out, port_out,
+):
+    height = loss_out.shape[0]
+
+    def body(group, carry):
+        one, one_flow, two, two_flow = carry
+        for sub in range(8):
+            h = group * 8 + sub
+            at = pl.ds(group * 64 + sub, 8, stride=8)
+            flux, temp = flux_ref[at, :], temp_ref[at, :]
+            opacity, inertia = opacity_ref[at, :], inertia_ref[at, :]
+            face = 1.0 / cond_ref[at, :]
+            stiff = 16.0 * opacity * (temp * temp * temp)
+            emit = 0.25 * stiff * temp
+            rate = 1.0 / (inertia + stiff)
+            loss = 2.0 + opacity * inertia * rate
+            flux_out[h], temp_out[h] = 2.0 * flux, temp
+            opacity_out[h], inertia_out[h] = opacity, inertia
+            face_out[h], loss_out[h], rate_out[h] = face, loss, rate
+            base_out[h] = 2.0 * flux + emit * inertia * rate
+            share_out[h] = stiff * rate
+            gain_out[h] = opacity * rate
+            rest_out[h] = temp - emit * rate
+            one, two = one + face * one_flow, two + face * two_flow
+            one_out[h], two_out[h] = one, two
+            one_flow, two_flow = one_flow + loss * one, two_flow + loss * two
+        return one, one_flow, two, two_flow
+
+    zero = jnp.zeros((8, 128), F32)
+    one, one_flow, two, two_flow = lax.fori_loop(
+        0, height // 8, body, (zero + 1.0, zero, zero, zero + 1.0)
+    )
+    port_out[0], port_out[1], port_out[2], port_out[3] = one, two, one_flow, two_flow
+
+
+def prepare(*fields):
+    height = fields[0].shape[0] // 8
+    return pl.pallas_call(
+        prepare_kernel,
+        out_shape=(tile(height),) * 13 + (tile(4),),
+        in_specs=[VMEM] * 5,
+        out_specs=(VMEM,) * 14,
+        compiler_params=params(32),
+    )(*fields)
+
+
+def source_at(where_ref, sums_ref, h):
+    band = h // 16
+    sender = (h + band + where_ref[0]) & 15
+    return sums_ref[sender * 8 + band]
+
+
+def load_kernel(where_ref, sums_ref, base_ref, share_ref, loss_ref, face_ref, flux_out, port_out):
+    height = base_ref.shape[0]
+
+    def body(group, carry):
+        value, flow = carry
+        for sub in range(8):
+            h = group * 8 + sub
+            value = value + face_ref[h] * flow
+            flux_out[h] = value
+            load = base_ref[h] + share_ref[h] * source_at(where_ref, sums_ref, h)
+            flow = flow + (loss_ref[h] * value - load)
+        return value, flow
+
+    zero = jnp.zeros((8, 128), F32)
+    value, flow = lax.fori_loop(0, height // 8, body, (zero, zero))
+    port_out[0], port_out[1] = value, flow
+
+
+def load_blocks(where, sums, base, share, loss, face):
+    return pl.pallas_call(
+        load_kernel,
+        out_shape=(tile(base.shape[0]), tile(2)),
+        in_specs=[SMEM] + [VMEM] * 5,
+        out_specs=(VMEM, VMEM),
+        compiler_params=params(16),
+    )(where, sums, base, share, loss, face)
+
+
+def block_ends(where_ref, port_of):
+    me = where_ref[1]
+    zero = jnp.zeros((8, 128), F32)
+    drop, level = zero, zero
+    draw, feed = zero, zero
+    for step in range(8):
+        low = step
+        a, b, c, d, p, j = port_of(me, low)
+        scale = 1.0 / (c * drop + d)
+        new_drop = (a * drop + b) * scale
+        new_level = level * scale + (p - new_drop * j)
+        below = low < me
+        drop, level = jnp.where(below, new_drop, drop), jnp.where(below, new_level, level)
+        high = 7 - step
+        a, b, c, d, p, j = port_of(me, high)
+        scale = 1.0 / (d + draw * b)
+        new_draw = (c + draw * a) * scale
+        new_feed = (feed - draw * p - j) * scale
+        above = high >= me
+        draw, feed = jnp.where(above, new_draw, draw), jnp.where(above, new_feed, feed)
+    value = (level + drop * feed) / (1.0 + drop * draw)
+    return value, feed - draw * value
+
+
+def slot_of(me, block):
+    apart = me ^ block
+    return (apart & 1) * 4 + (apart & 2) + lax.shift_right_logical(apart, 2)
+
+
+def second_kernel(
+    where_ref, matrix_ref, loads_ref, flag_ref, sums_ref, one_ref, two_ref, load_ref, gain_ref, rest_ref,
+    rate_ref, flux_ref, temp_ref, opacity_ref, inertia_ref, face_ref,
+    one_out, two_out, load_out, gain_out, rest_out, port_out,
+):
+    height = one_ref.shape[0]
+
+    def port_of(me, block):
+        at = slot_of(me, block)
+        return tuple(matrix_ref[at * 4 + i] for i in range(4)) + tuple(
+            loads_ref[at * 2 + i] for i in range(2)
+        )
+
+    value, flow = block_ends(where_ref, port_of)
+
+    def body(group, carry):
+        one, one_flow, two, two_flow, load, load_flow = carry
+        for sub in range(8):
+            h = group * 8 + sub
+            source = source_at(where_ref, sums_ref, h)
+            light = one_ref[h] * value + two_ref[h] * flow + load_ref[h]
+            temp = rest_ref[h] + gain_ref[h] * light + rate_ref[h] * source
+            opacity, inertia, face = opacity_ref[h], inertia_ref[h], face_ref[h]
+            stiff = 16.0 * opacity * (temp * temp * temp)
+            emit = 0.25 * stiff * temp
+            rate = 1.0 / (inertia + stiff)
+            loss = 2.0 + opacity * inertia * rate
+            lag = inertia * (temp - temp_ref[h]) - source
+            right = flux_ref[h] + (emit * inertia - stiff * lag) * rate
+            gain_out[h] = opacity * rate
+            rest_out[h] = temp - (lag + emit) * rate
+            one, two, load = one + face * one_flow, two + face * two_flow, load + face * load_flow
+            one_out[h], two_out[h], load_out[h] = one, two, load
+            one_flow, two_flow = one_flow + loss * one, two_flow + loss * two
+            load_flow = load_flow + (loss * load - right)
+        return one, one_flow, two, two_flow, load, load_flow
+
+    zero = jnp.zeros((8, 128), F32)
+    one, one_flow, two, two_flow, load, load_flow = lax.fori_loop(
+        0, height // 8, body, (zero + 1.0, zero, zero, zero + 1.0, zero, zero)
+    )
+    port_out[0], port_out[1], port_out[2], port_out[3] = one, two, one_flow, two_flow
+    port_out[4], port_out[5], port_out[6] = load, load_flow, flag_ref[0]
+
+
+def second_step(where, *arrays):
+    height = arrays[4].shape[0]
+    return pl.pallas_call(
+        second_kernel,
+        out_shape=(tile(height),) * 5 + (tile(7),),
+        in_specs=[SMEM] + [VMEM] * len(arrays),
+        out_specs=(VMEM,) * 6,
+        compiler_params=params(32),
+    )(where, *arrays)
+
+
+def finish_kernel(where_ref, ports_ref, one_ref, two_ref, load_ref, gain_ref, rest_ref, flux_out, temp_out):
+    height = one_ref.shape[0]
+
+    def port_of(me, block):
+        at = slot_of(me, block)
+        return tuple(ports_ref[at * 7 + i] for i in range(6))
+
+    value, flow = block_ends(where_ref, port_of)
+
+    def body(group, carry):
+        for sub in range(8):
+            h = group * 8 + sub
+            at = pl.ds(group * 64 + sub, 8, stride=8)
+            light = one_ref[h] * value + two_ref[h] * flow + load_ref[h]
+            flux_out[at, :] = light
+            temp_out[at, :] = rest_ref[h] + gain_ref[h] * light
+        return carry
+
+    lax.fori_loop(0, height // 8, body, 0)
+
+
+def finish(where, *arrays):
+    height = arrays[1].shape[0]
+    return pl.pallas_call(
+        finish_kernel,
+        out_shape=(jax.ShapeDtypeStruct((height * 8, 128), F32),) * 2,
+        in_specs=[SMEM] + [VMEM] * len(arrays),
+        out_specs=(VMEM, VMEM),
+        compiler_params=params(16),
+    )(where, *arrays)
+
+
+def gathered(rows):
+    for by in (4, 2, 1):
+        rows = jnp.concatenate([rows, lax.ppermute(rows, "gz", [(i, i ^ by) for i in range(8)])], 0)
+    return rows
+
+
+def tiles_of(field):
+    height, width = field.shape
+    return field.reshape(height // 8, 8, width // 128, 128).transpose(0, 2, 1, 3).reshape(-1, 128)
+
+
+def field_of(tiles, height, width):
+    return tiles.reshape(height // 8, width // 128, 8, 128).transpose(0, 2, 1, 3).reshape(height, width)
+
+
+def shards(
+    photon_flux_entering,
+    thermal_state_prior,
+    opacity_coefficient,
+    conductance_scaled,
+    thermal_inertia,
+    granule_power,
+    granule_holder,
+    granule_slot,
+):
+    height, width = photon_flux_entering.shape
+    arguments = (
+        photon_flux_entering,
+        thermal_state_prior,
+        opacity_coefficient,
+        conductance_scaled,
+        thermal_inertia,
+        granule_power,
+        granule_holder,
+        granule_slot,
+    )
+    where = jnp.stack([lax.axis_index("col"), lax.axis_index("gz")]).astype(jnp.int32)
+    sent = pack(granule_holder.reshape(16, 128), granule_slot.reshape(16, 128), granule_power[0])
+    got = lax.all_to_all(sent.reshape(16, SLOTS, 128), "col", 0, 0, tiled=True)
+    (
+        flux, temp, opacity, inertia, face, loss, base, share, rate, gain, rest, one, two, matrix,
+    ) = prepare(*[tiles_of(x) for x in arguments[:5]])
+    matrix = gathered(matrix)
+    sums, flag = sum_records(got.reshape(16 * SLOTS, 128))
+    sums = lax.all_to_all(sums.reshape(16, 64, 128), "col", 0, 0, tiled=True).reshape(128, 8, 128)
+    load, loads = load_blocks(where, sums, base, share, loss, face)
+    loads = gathered(loads)
+    one, two, load, gain, rest, ports = second_step(
+        where, matrix, loads, flag, sums, one, two, load, gain, rest, rate, flux, temp, opacity, inertia, face
+    )
+    ports = gathered(ports)
+    crowded = jnp.max(ports.reshape(8, 7, 8, 128)[:, 6, 0, 127]) > 0.5
+
+    def quick(_):
+        return tuple(
+            field_of(x, height, width) for x in finish(where, ports, one, two, load, gain, rest)
+        )
+
+    def general(operands):
+        return general_path(*operands)
+
+    return lax.cond(crowded, general, quick, arguments)
+
+
 def solution(mesh):
     return jax.shard_map(
         shards,

time: 273 us -> 94 us (0.34)
  other arithmetic: 90.5 us -> 0.8 us
  starting transfers between devices: 83.5 us -> 19.4 us
  waiting for transfers between devices: 67.7 us -> 10.1 us
  blocking collectives: 0 us -> 30 us
  Pallas kernels: 0 us -> 22.3 us
  local copies, waits for them, and re-layouts: 28 us -> 9.52 us
    scatter-add x1 -> x0, other arithmetic: 56.4 us -> none  [gather_sources(): total.at[got_cell.reshape(-1).astype(jnp.int32)]]
    ppermute x21 -> x9, starting transfers between devices: 68.3 us -> 15.8 us  [gathered(): lax.ppermute(rows, 'gz', [(i, i ^ by) for i in range(8)])]
    all_to_all x2 -> x1, waiting for transfers between devices: 48 us -> 0.01 us  [shards(): lax.all_to_all(sums.reshape(16, 64, 128), 'col', 0, 0, tiled=True)]
    all_to_all x0 -> x1, blocking collectives: none -> 30 us  [shards(): got = lax.all_to_all(sent.reshape(16, SLOTS, 128), 'col', 0, 0, tiled=True)]
    pallas_call x0 -> x6, Pallas kernels: none -> 22.3 us  [the longest x1 7.05 us: pack(): pl.pallas_call(pack_kernel, out_shape=jax.ShapeDtypeStruct((16 * SLOTS, 1...]
    div x52 -> x0, other arithmetic: 15.7 us -> none  [the longest x20 10.5 us: combine_rows(): (scaled_rhs - lower_ratio * rhs_below - upper_ratio * rhs_above) / pivot]
    all_to_all x2 -> x1, starting transfers between devices: 15.3 us -> 3.57 us  [shards(): lax.all_to_all(sums.reshape(16, 64, 128), 'col', 0, 0, tiled=True)]
    ppermute x21 -> x9, waiting for transfers between devices: 19.7 us -> 10.1 us  [gathered(): lax.ppermute(rows, 'gz', [(i, i ^ by) for i in range(8)])]
  transfers between devices with their start and end apart: 23 -> 10, of which waited for: 11 -> 5; matrix products, arithmetic and copies ran while one was open for 26% -> 0% of each run, Pallas kernels for 0% -> 4%
where the time goes in v1:
time: 94 us; the launch traced here: 93.5 us
  blocking collectives  30 us (32%)
  Pallas kernels  22.3 us (24%)
  starting transfers between devices  19.4 us (21%)
  waiting for transfers between devices  10.1 us (11%)
  local copies, waits for them, and re-layouts  9.52 us (10%)
  between operations  1.44 us (2%)
    all_to_all x1, blocking collectives, shards(): got = lax.all_to_all(sent.reshape(16, SLOTS, 128), 'col', 0, 0, tiled=True)  30 us
    ppermute x9, starting transfers between devices, gathered(): lax.ppermute(rows, 'gz', [(i, i ^ by) for i in range(8)])  15.8 us
    ppermute x9, waiting for transfers between devices, gathered(): lax.ppermute(rows, 'gz', [(i, i ^ by) for i in range(8)])  10.1 us
    unnamed x39, local copies, waits for them, and re-layouts  9.51 us
    pallas_call x1, Pallas kernels, pack(): pl.pallas_call(pack_kernel, out_shape=jax.ShapeDtypeStruct((16 * SLOTS, 1...  7.05 us
    pallas_call x1, Pallas kernels, sum_records(): pl.pallas_call(sum_kernel, out_shape=(jax.ShapeDtypeStruct((1024, 128), F...  4.66 us
    all_to_all x1, starting transfers between devices, shards(): lax.all_to_all(sums.reshape(16, 64, 128), 'col', 0, 0, tiled=True)  3.57 us
    pallas_call x1, Pallas kernels, second_step(): pl.pallas_call(second_kernel, out_shape=(tile(height),) * 5 + (tile(7),),...  3.48 us
  transfers between devices with their start and end apart: 10, of which 5 were waited for; matrix products, arithmetic and copies ran while one was open for 0% of the time, Pallas kernels for 4%

profile of v1, /device:TPU:1, one launch (start us, length us, event | category | flops | bytes accessed | tf_op | source)
XLA Modules:
  0.0 93.5 jit_solution(9232485583963739870)
XLA Ops:
  0.6 7.1 %shard_map.100 = f32[3072,128]{1,0:T(8,128)S(1)} custom-call(s32[16,128]{1,0:T(8,128)} %bitcast.235, s32[16,128]{1,0:T(8,128)} %bitcast.241, f32[2048,128]{1,0:T(8,128)} %bitcast.232), custom_call_target="tpu_custom_call" | custom-call | tf_op jit(solution)/shard_map/pallas_call | solution.py:289
  7.7 30.0 %all_to_all.21 = f32[16,192,128]{2,1,0:T(8,128)S(1)} all-to-all(f32[16,192,128]{2,1,0:T(8,128)S(1)} %bitcast.223), channel_id=1, replica_groups=mesh['col'=16,'gz'=8] {'col'}, dimensions={0} | all-to-all | bytes 3145728 | tf_op jit(solution)/shard_map/all_to_all | solution.py:581
  37.7 4.7 %shard_map.101 = (f32[1024,128]{1,0:T(8,128)}, f32[1,8,128]{2,1,0:T(8,128)S(1)}) custom-call(f32[3072,128]{1,0:T(8,128)S(1)} %bitcast.222), custom_call_target="tpu_custom_call" | custom-call | tf_op jit(solution)/shard_map/pallas_call | solution.py:329
  42.3 3.6 %all-to-all-start.3 = ((f32[16,64,128]{2,1,0:T(8,128)}), f32[16,64,128]{2,1,0:T(8,128)S(1)}, u32[]{:S(2)}, u32[]{:S(2)}) async-start(f32[16,64,128]{2,1,0:T(8,128)} %bitcast.113), calls=%async_computation.3 | async-start | bytes 1048576 | tf_op jit(solution)/shard_map/all_to_all | solution.py:587
  45.9 2.6 %shard_map.99 = (f32[128,8,128]{2,1,0:T(8,128)S(1)}, f32[128,8,128]{2,1,0:T(8,128)S(1)}, f32[128,8,128]{2,1,0:T(8,128)S(1)}, f32[128,8,128]{2,1,0:T(8,128)S(1)},...) custom-call(f32[1024,128]{1,0:T(8,128)} %bitcast.226, ...), custom_call_target="tpu_custom_call" | custom-call | tf_op jit(solution)/shard_map/pallas_call | solution.py:383
  51.7 0.8 copy-done.8
  54.0 0.8 copy-done.14
  54.8 2.9 %collective-permute-start.21 = (f32[4,8,128]{2,1,0:T(8,128)S(1)}, f32[4,8,128]{2,1,0:T(8,128)S(1)}, u32[]{:S(2)}, u32[]{:S(2)}) collective-permute-start(f32[4,8,128]{2,1,0:T(8,128)S(1)} %get-tuple-element.73), channel_id=1, source_target_pairs={{0,4},{1,5},{2,6},{3,7},{4,0},{5,1},{6,2},{7,3},{8,12},{9,13},{10,... | collective-permute-start | bytes 49160 | tf_op jit(solution)/shard_map/ppermute | solution.py:545
  57.8 1.0 %copy-done.11 = f32[128,8,128]{2,1,0:T(8,128)S(1)} copy-done((f32[128,8,128]{2,1,0:T(8,128)S(1)}, f32[128,8,128]{2,1,0:T(8,128)}, u32[]{:S(2)}) %copy-start.11) | copy-done | bytes 524312
  58.9 1.0 %copy-done.13 = f32[128,8,128]{2,1,0:T(8,128)S(1)} copy-done((f32[128,8,128]{2,1,0:T(8,128)S(1)}, f32[128,8,128]{2,1,0:T(8,128)}, u32[]{:S(2)}) %copy-start.13) | copy-done | bytes 524312
  59.9 1.0 %copy-done.15 = f32[128,8,128]{2,1,0:T(8,128)S(1)} copy-done((f32[128,8,128]{2,1,0:T(8,128)S(1)}, f32[128,8,128]{2,1,0:T(8,128)}, u32[]{:S(2)}) %copy-start.15) | copy-done | bytes 524312
  61.0 1.5 %shard_map.102 = (f32[128,8,128]{2,1,0:T(8,128)S(1)}, f32[2,8,128]{2,1,0:T(8,128)S(1)}) custom-call(s32[2]{0:T(128)S(1)} %pad_add_fusion.1.where_ref, f32[128,8,128]{2,1,0:T(8,128)S(1)} %bitcast.224, f32[128,8,128]{2,1,0:T(8,128)S(1)} %copy-done.13, f32[128,8,128]{2,1,0:T(8,128)S(1)} %copy-done.15, f32[128,8,128]{2,1,0:T(8,128)S(1)} %copy-done.11, ...), custom_call_target="tpu_custom_call" | custom-call | tf_op jit(solution)/shard_map/pallas_call | solution.py:417
  64.0 2.6 %collective-permute-done.24 = f32[2,8,128]{2,1,0:T(8,128)S(1)} collective-permute-done((f32[2,8,128]{2,1,0:T(8,128)S(1)}, f32[2,8,128]{2,1,0:T(8,128)S(1)}, u32[]{:S(2)}, u32[]{:S(2)}) %collective-permute-start.24) | collective-permute-done | bytes 8224 | tf_op jit(solution)/shard_map/ppermute | solution.py:545
  67.0 3.8 %collective-permute-start.23 = (f32[16,8,128]{2,1,0:T(8,128)S(1)}, f32[16,8,128]{2,1,0:T(8,128)S(1)}, u32[]{:S(2)}, u32[]{:S(2)}) collective-permute-start(f32[16,8,128]{2,1,0:T(8,128)S(1)} %pad_maximum_fusion.15), channel_id=1, source_target_pairs={{0,1},{1,0},{2,3},{3,2},{4,5},{5,4},{6,7},{7,6},{8,9},{9,8},{10,11... | collective-permute-start | bytes 196616 | tf_op jit(solution)/shard_map/ppermute | solution.py:545
  70.8 3.0 %collective-permute-start.26 = (f32[8,8,128]{2,1,0:T(8,128)S(1)}, f32[8,8,128]{2,1,0:T(8,128)S(1)}, u32[]{:S(2)}, u32[]{:S(2)}) collective-permute-start(f32[8,8,128]{2,1,0:T(8,128)S(1)} %pad_maximum_fusion.19), channel_id=1, source_target_pairs={{0,1},{1,0},{2,3},{3,2},{4,5},{5,4},{6,7},{7,6},{8,9},{9,8},{10,11... | collective-permute-start | bytes 98312 | tf_op jit(solution)/shard_map/ppermute | solution.py:545
  73.8 0.8 collective-permute-done.26
  74.7 3.5 %shard_map.103 = (f32[128,8,128]{2,1,0:T(8,128)}, f32[128,8,128]{2,1,0:T(8,128)}, f32[128,8,128]{2,1,0:T(8,128)}, f32[128,8,128]{2,1,0:T(8,128)}, f32[128,8,128]{2,1,0:T(8,128)}, /*index=5*/f32[7,8,128]{2,1,0:T(8,128)S(1)}) custom-call(s32[2]{0:T(128)S(1)} %pad_add_fusion.1.where_ref, f32[32,8,128]{2,1,0:T(8,128)S(1)} %pad_maximum_fusion.13.matrix_ref, ...), custom_call_target="tpu_custom_call" | custom-call | tf_op jit(solution)/shard_map/pallas_call | solution.py:502
  78.2 1.2 %collective-permute-start.27 = (f32[7,8,128]{2,1,0:T(8,128)S(1)}, f32[7,8,128]{2,1,0:T(8,128)S(1)}, u32[]{:S(2)}, u32[]{:S(2)}) collective-permute-start(f32[7,8,128]{2,1,0:T(8,128)S(1)} %get-tuple-element.91), channel_id=1, source_target_pairs={{0,4},{1,5},{2,6},{3,7},{4,0},{5,1},{6,2},{7,3},{8,12},{9,13},{10,... | collective-permute-start | bytes 86024 | tf_op jit(solution)/shard_map/ppermute | solution.py:545
  79.4 3.0 %collective-permute-done.27 = f32[7,8,128]{2,1,0:T(8,128)S(1)} collective-permute-done((f32[7,8,128]{2,1,0:T(8,128)S(1)}, f32[7,8,128]{2,1,0:T(8,128)S(1)}, u32[]{:S(2)}, u32[]{:S(2)}) %collective-permute-start.27) | collective-permute-done | bytes 28704 | tf_op jit(solution)/shard_map/ppermute | solution.py:545
  82.8 2.6 %collective-permute-done.28 = f32[14,8,128]{2,1,0:T(8,128)S(1)} collective-permute-done((f32[14,8,128]{2,1,0:T(8,128)S(1)}, f32[14,8,128]{2,1,0:T(8,128)S(1)}, u32[]{:S(2)}, u32[]{:S(2)}) %collective-permute-start.28) | collective-permute-done | bytes 57376 | tf_op jit(solution)/shard_map/ppermute | solution.py:545
  85.5 2.7 %collective-permute-start.29 = (f32[28,8,128]{2,1,0:T(8,128)S(1)}, f32[28,8,128]{2,1,0:T(8,128)S(1)}, u32[]{:S(2)}, u32[]{:S(2)}) collective-permute-start(f32[28,8,128]{2,1,0:T(8,128)S(1)} %pad_maximum_fusion.14), channel_id=1, source_target_pairs={{0,1},{1,0},{2,3},{3,2},{4,5},{5,4},{6,7},{7,6},{8,9},{9,8},{10,11... | collective-permute-start | bytes 344072 | tf_op jit(solution)/shard_map/ppermute | solution.py:545
  88.2 1.0 %collective-permute-done.29 = f32[28,8,128]{2,1,0:T(8,128)S(1)} collective-permute-done((f32[28,8,128]{2,1,0:T(8,128)S(1)}, f32[28,8,128]{2,1,0:T(8,128)S(1)}, u32[]{:S(2)}, u32[]{:S(2)}) %collective-permute-start.29) | collective-permute-done | bytes 114720 | tf_op jit(solution)/shard_map/ppermute | solution.py:545
  90.5 3.0 %conditional.1 = (f32[128,1024]{1,0:T(8,128)}, f32[128,1024]{1,0:T(8,128)}) conditional(s32[]{:T(128)} %convert_element_type.30, (s32[2]{0:T(128)S(1)}, f32[56,8,128]{2,1,0:T(8,128)S(1)}, f32[128,8,128]{2,1,0:T(8,128)}, f32[128,8,128]{2,1,0:T(8,128)}, f32[128,8,128]{2,1,0:T(8,128)}, /*index=5*/f32[128,8,128]{2,1,0:T(8,128)}, ...), branch_computations={%region_1.0_spmd, %region_2.9_spmd} | conditional | flops 77854064 | bytes 402934976 | solution.py:604
  90.5 3.0 %branch_0_fun.1 = (f32[1024,128]{1,0:T(8,128)}, f32[1024,128]{1,0:T(8,128)}) custom-call(s32[2]{0:T(128)S(1)} %get-tuple-element.30.where_ref, f32[56,8,128]{2,1,0:T(8,128)S(1)} %get-tuple-element.31.ports_ref, f32[128,8,128]{2,1,0:T(8,128)} %get-tuple-element.32.one_ref, f32[128,8,128]{2,1,0:T(8,128)} %get-tuple-element.33.two_ref, ...), custom_call_target="tpu_custom_call" | custom-call | tf_op jit(solution)/shard_map/cond/branch_0_fun/pallas_call | solution.py:534
  (54 shorter events, 7.8 us)
Async XLA Ops:
  42.3 15.5 %all-to-all-start.3 = ((f32[16,64,128]{2,1,0:T(8,128)}), f32[16,64,128]{2,1,0:T(8,128)S(1)}, u32[]{:S(2)}, u32[]{:S(2)}) async-start(f32[16,64,128]{2,1,0:T(8,128)} %bitcast.113), calls=%async_computation.3 | async-start | bytes 1048576 | tf_op jit(solution)/shard_map/all_to_all | solution.py:587
  50.1 0.8 copy-start.4
  51.6 0.8 copy-start.8
  52.5 0.8 copy-start.10
  54.0 0.8 copy-start.14
  54.8 8.4 %collective-permute-start.21 = (f32[4,8,128]{2,1,0:T(8,128)S(1)}, f32[4,8,128]{2,1,0:T(8,128)S(1)}, u32[]{:S(2)}, u32[]{:S(2)}) collective-permute-start(f32[4,8,128]{2,1,0:T(8,128)S(1)} %get-tuple-element.73), channel_id=1, source_target_pairs={{0,4},{1,5},{2,6},{3,7},{4,0},{5,1},{6,2},{7,3},{8,12},{9,13},{10,... | collective-permute-start | bytes 49160 | tf_op jit(solution)/shard_map/ppermute | solution.py:545
  57.8 1.0 %copy-start.11 = (f32[128,8,128]{2,1,0:T(8,128)S(1)}, f32[128,8,128]{2,1,0:T(8,128)}, u32[]{:S(2)}) copy-start(f32[128,8,128]{2,1,0:T(8,128)} %copy-done.10) | copy-start | bytes 1572868
  58.9 1.0 %copy-start.13 = (f32[128,8,128]{2,1,0:T(8,128)S(1)}, f32[128,8,128]{2,1,0:T(8,128)}, u32[]{:S(2)}) copy-start(f32[128,8,128]{2,1,0:T(8,128)} %copy-done.12) | copy-start | bytes 1572868
  59.9 1.0 %copy-start.15 = (f32[128,8,128]{2,1,0:T(8,128)S(1)}, f32[128,8,128]{2,1,0:T(8,128)}, u32[]{:S(2)}) copy-start(f32[128,8,128]{2,1,0:T(8,128)} %copy-done.14) | copy-start | bytes 1572868
  61.0 13.7 %copy-start.1 = (f32[128,8,128]{2,1,0:T(8,128)S(1)}, f32[128,8,128]{2,1,0:T(8,128)}, u32[]{:S(2)}) copy-start(f32[128,8,128]{2,1,0:T(8,128)} %copy-done) | copy-start | bytes 1572868
  61.0 13.7 %copy-start.3 = (f32[128,8,128]{2,1,0:T(8,128)S(1)}, f32[128,8,128]{2,1,0:T(8,128)}, u32[]{:S(2)}) copy-start(f32[128,8,128]{2,1,0:T(8,128)} %copy-done.2) | copy-start | bytes 1572868
  61.0 13.7 %copy-start.5 = (f32[128,8,128]{2,1,0:T(8,128)S(1)}, f32[128,8,128]{2,1,0:T(8,128)}, u32[]{:S(2)}) copy-start(f32[128,8,128]{2,1,0:T(8,128)} %copy-done.4) | copy-start | bytes 1572868
  61.0 13.7 %copy-start.7 = (f32[128,8,128]{2,1,0:T(8,128)S(1)}, f32[128,8,128]{2,1,0:T(8,128)}, u32[]{:S(2)}) copy-start(f32[128,8,128]{2,1,0:T(8,128)} %copy-done.6) | copy-start | bytes 1572868
  61.0 13.7 %copy-start.9 = (f32[128,8,128]{2,1,0:T(8,128)S(1)}, f32[128,8,128]{2,1,0:T(8,128)}, u32[]{:S(2)}) copy-start(f32[128,8,128]{2,1,0:T(8,128)} %copy-done.8) | copy-start | bytes 1572868
  62.5 4.1 %collective-permute-start.24 = (f32[2,8,128]{2,1,0:T(8,128)S(1)}, f32[2,8,128]{2,1,0:T(8,128)S(1)}, u32[]{:S(2)}, u32[]{:S(2)}) collective-permute-start(f32[2,8,128]{2,1,0:T(8,128)S(1)} %get-tuple-element.79), channel_id=1, source_target_pairs={{0,4},{1,5},{2,6},{3,7},{4,0},{5,1},{6,2},{7,3},{8,12},{9,13},{10,... | collective-permute-start | bytes 24584 | tf_op jit(solution)/shard_map/ppermute | solution.py:545
  63.2 3.8 %collective-permute-start.22 = (f32[8,8,128]{2,1,0:T(8,128)S(1)}, f32[8,8,128]{2,1,0:T(8,128)S(1)}, u32[]{:S(2)}, u32[]{:S(2)}) collective-permute-start(f32[8,8,128]{2,1,0:T(8,128)S(1)} %pad_maximum_fusion.18), channel_id=1, source_target_pairs={{0,2},{1,3},{2,0},{3,1},{4,6},{5,7},{6,4},{7,5},{8,10},{9,11},{10,... | collective-permute-start | bytes 98312 | tf_op jit(solution)/shard_map/ppermute | solution.py:545
  66.6 4.2 %collective-permute-start.25 = (f32[4,8,128]{2,1,0:T(8,128)S(1)}, f32[4,8,128]{2,1,0:T(8,128)S(1)}, u32[]{:S(2)}, u32[]{:S(2)}) collective-permute-start(f32[4,8,128]{2,1,0:T(8,128)S(1)} %pad_maximum_fusion.20), channel_id=1, source_target_pairs={{0,2},{1,3},{2,0},{3,1},{4,6},{5,7},{6,4},{7,5},{8,10},{9,11},{10,... | collective-permute-start | bytes 49160 | tf_op jit(solution)/shard_map/ppermute | solution.py:545
  67.0 6.7 %collective-permute-start.23 = (f32[16,8,128]{2,1,0:T(8,128)S(1)}, f32[16,8,128]{2,1,0:T(8,128)S(1)}, u32[]{:S(2)}, u32[]{:S(2)}) collective-permute-start(f32[16,8,128]{2,1,0:T(8,128)S(1)} %pad_maximum_fusion.15), channel_id=1, source_target_pairs={{0,1},{1,0},{2,3},{3,2},{4,5},{5,4},{6,7},{7,6},{8,9},{9,8},{10,11... | collective-permute-start | bytes 196616 | tf_op jit(solution)/shard_map/ppermute | solution.py:545
  70.8 3.8 %collective-permute-start.26 = (f32[8,8,128]{2,1,0:T(8,128)S(1)}, f32[8,8,128]{2,1,0:T(8,128)S(1)}, u32[]{:S(2)}, u32[]{:S(2)}) collective-permute-start(f32[8,8,128]{2,1,0:T(8,128)S(1)} %pad_maximum_fusion.19), channel_id=1, source_target_pairs={{0,1},{1,0},{2,3},{3,2},{4,5},{5,4},{6,7},{7,6},{8,9},{9,8},{10,11... | collective-permute-start | bytes 98312 | tf_op jit(solution)/shard_map/ppermute | solution.py:545
  74.7 15.8 %copy-start.31 = (s32[1,2048,1]{1,2,0:T(1,128)S(1)}, s32[1,2048,1]{1,2,0:T(1,128)}, u32[]{:S(2)}) copy-start(s32[1,2048,1]{1,2,0:T(1,128)} %param.16) | copy-start | bytes 24580
  74.7 15.8 %copy-start.32 = (s32[1,2048]{1,0:T(1,128)S(1)}, s32[1,2048]{1,0:T(1,128)}, u32[]{:S(2)}) copy-start(s32[1,2048]{1,0:T(1,128)} %param.17) | copy-start | bytes 24580
  78.2 4.2 %collective-permute-start.27 = (f32[7,8,128]{2,1,0:T(8,128)S(1)}, f32[7,8,128]{2,1,0:T(8,128)S(1)}, u32[]{:S(2)}, u32[]{:S(2)}) collective-permute-start(f32[7,8,128]{2,1,0:T(8,128)S(1)} %get-tuple-element.91), channel_id=1, source_target_pairs={{0,4},{1,5},{2,6},{3,7},{4,0},{5,1},{6,2},{7,3},{8,12},{9,13},{10,... | collective-permute-start | bytes 86024 | tf_op jit(solution)/shard_map/ppermute | solution.py:545
  82.4 3.0 %collective-permute-start.28 = (f32[14,8,128]{2,1,0:T(8,128)S(1)}, f32[14,8,128]{2,1,0:T(8,128)S(1)}, u32[]{:S(2)}, u32[]{:S(2)}) collective-permute-start(f32[14,8,128]{2,1,0:T(8,128)S(1)} %pad_maximum_fusion.17), channel_id=1, source_target_pairs={{0,2},{1,3},{2,0},{3,1},{4,6},{5,7},{6,4},{7,5},{8,10},{9,11},{10,... | collective-permute-start | bytes 172040 | tf_op jit(solution)/shard_map/ppermute | solution.py:545
  85.5 3.7 %collective-permute-start.29 = (f32[28,8,128]{2,1,0:T(8,128)S(1)}, f32[28,8,128]{2,1,0:T(8,128)S(1)}, u32[]{:S(2)}, u32[]{:S(2)}) collective-permute-start(f32[28,8,128]{2,1,0:T(8,128)S(1)} %pad_maximum_fusion.14), channel_id=1, source_target_pairs={{0,1},{1,0},{2,3},{3,2},{4,5},{5,4},{6,7},{7,6},{8,9},{9,8},{10,11... | collective-permute-start | bytes 344072 | tf_op jit(solution)/shard_map/ppermute | solution.py:545
  (4 other events, 3.2 us)

commit v2 on v1

--- a/solution.py
+++ b/solution.py
@@ -208,21 +208,35 @@
 
 SLOTS = 192
 ROOM = 190
+PIECE = 32
 F32 = jnp.float32
 BF16 = jnp.bfloat16
 VMEM = pl.BlockSpec(memory_space=pltpu.VMEM)
 SMEM = pl.BlockSpec(memory_space=pltpu.SMEM)
+ANY = pl.BlockSpec(memory_space=pl.ANY)
+HBM = pl.BlockSpec(memory_space=pltpu.HBM)
 
 
 def params(mib):
     return pltpu.CompilerParams(vmem_limit_bytes=mib * 2**20)
 
 
-def tile(count):
-    return jax.ShapeDtypeStruct((count, 8, 128), F32)
-
-
-def pack_kernel(owner_ref, cell_ref, heat_ref, out_ref, row_vmem, row_smem, sem):
+def tile(*count):
+    return jax.ShapeDtypeStruct(count + (8, 128), F32)
+
+
+def pieces(source, sink, sems, rows):
+    return [
+        pltpu.make_async_copy(
+            source.at[pl.ds(k * rows, rows)], sink.at[pl.ds(k * rows, rows)], sems.at[k]
+        )
+        for k in range(source.shape[0] // rows)
+    ]
+
+
+def pack_kernel(owner_ref, cell_ref, heat_hbm, out_ref, heat_ref, row_vmem, row_smem, sem, heat_sem):
+    heat_copy = pltpu.make_async_copy(heat_hbm, heat_ref, heat_sem)
+    heat_copy.start()
     groups, lanes = owner_ref.shape
     owner, cell = owner_ref[...], cell_ref[...]
     level = lax.shift_right_logical(cell, 3)
@@ -232,19 +246,16 @@
     place_high = lax.shift_right_logical(place, 5).astype(F32)
     place_low = (place & 31).astype(F32)
     classes = lax.broadcasted_iota(jnp.int32, (16, lanes), 0)
-    member = [classes == target[g : g + 1, :] for g in range(groups)]
-    member_f = [jnp.where(m, 1.0, 0.0) for m in member]
+    member = [jnp.where(classes == target[g : g + 1, :], 1.0, 0.0) for g in range(groups)]
     source = lax.broadcasted_iota(jnp.int32, (lanes, 2 * lanes), 0)
     sink = lax.broadcasted_iota(jnp.int32, (lanes, 2 * lanes), 1)
     before = jnp.where((source < sink) | (sink >= lanes), 1.0, 0.0).astype(BF16)
-    counts = jnp.dot(
-        jnp.concatenate(member_f, 0).astype(BF16), before, preferred_element_type=F32
-    )
+    counts = jnp.dot(jnp.concatenate(member, 0).astype(BF16), before, preferred_element_type=F32)
     start = jnp.zeros((16, lanes), F32)
     slots = []
     for g in range(groups):
         ahead = counts[16 * g : 16 * g + 16]
-        slots.append(jnp.sum(member_f[g] * (ahead[:, :lanes] + start), 0, keepdims=True))
+        slots.append(jnp.sum(member[g] * (ahead[:, :lanes] + start), 0, keepdims=True))
         start = start + ahead[:, lanes:]
     slot = jnp.concatenate(slots, 0).astype(jnp.int32)
     fits = slot < ROOM
@@ -254,31 +265,29 @@
     out_ref[...] = jnp.zeros_like(out_ref)
     named = jnp.where(fits, slot, 4096)
     slot_row = lax.broadcasted_iota(jnp.int32, (2 * lanes, lanes), 0)
-    table = jnp.zeros((32, 2 * lanes), F32)
-    for g in range(groups):
-        weights = jnp.concatenate(
-            [member_f[g] * place_high[g : g + 1], member_f[g] * place_low[g : g + 1]], 0
-        )
-        hits = jnp.where(slot_row == named[g : g + 1], 1.0, 0.0)
-        table = table + lax.dot_general(
-            weights.astype(BF16),
-            hits.astype(BF16),
-            (((1,), (1,)), ((), ())),
-            preferred_element_type=F32,
-        )
+    weights = jnp.concatenate(
+        [
+            jnp.concatenate([member[g] * part[g : g + 1] for g in range(groups)], 1)
+            for part in (place_high, place_low)
+        ],
+        0,
+    ).astype(BF16)
+    hits = jnp.concatenate(
+        [jnp.where(slot_row == named[g : g + 1], 1.0, 0.0).astype(BF16) for g in range(groups)], 1
+    )
+    table = lax.dot_general(weights, hits, (((1,), (1,)), ((), ())), preferred_element_type=F32)
     places = table[:16] * 32.0 + table[16:] - 1.0
     over = jnp.max(jnp.where(start > ROOM, 1.0, 0.0))
     lane = lax.broadcasted_iota(jnp.int32, (1, 2 * lanes), 1)
     places = jnp.where(lane == 2 * lanes - 1, over, places)
     copy.wait()
-
-    for g in range(groups):
-
-        @pl.loop(0, lanes, step=16)
-        def _(base):
-            for i in range(16):
-                row = row_smem[g, base + i]
-                out_ref[pl.ds(row, 1), :] = heat_ref[pl.ds(g * lanes + base + i, 1), :]
+    heat_copy.wait()
+
+    @pl.loop(0, groups)
+    def _(g):
+        for i in range(lanes):
+            row = row_smem[g, i]
+            out_ref[pl.ds(row, 1), :] = heat_ref[pl.ds(g * lanes + i, 1), :]
 
     for m in range(16):
         out_ref[m * SLOTS + ROOM : m * SLOTS + ROOM + 1, :] = places[m : m + 1, :lanes]
@@ -289,104 +298,113 @@
     return pl.pallas_call(
         pack_kernel,
         out_shape=jax.ShapeDtypeStruct((16 * SLOTS, 128), F32),
-        in_specs=[VMEM, VMEM, VMEM],
+        in_specs=[VMEM, VMEM, HBM],
         out_specs=VMEM,
         scratch_shapes=[
+            pltpu.VMEM((2048, 128), F32),
             pltpu.VMEM((16, 128), jnp.int32),
             pltpu.SMEM((16, 128), jnp.int32),
+            pltpu.SemaphoreType.DMA,
             pltpu.SemaphoreType.DMA,
         ],
         compiler_params=params(16),
     )(owner, cell, heat)
 
 
-def sum_kernel(got_ref, out_ref, flag_ref, terms):
+def sum_kernel(after_ref, got_ref, out_ref, flag_ref, terms):
     flag = jnp.zeros((1, 128), F32)
     for s in range(16):
         heat = got_ref[s * SLOTS : (s + 1) * SLOTS, :]
         high = heat.astype(BF16)
-        terms[s * 256 : s * 256 + SLOTS, :128] = high
-        terms[s * 256 : s * 256 + SLOTS, 128:] = (heat - high.astype(F32)).astype(BF16)
-        terms[s * 256 + SLOTS : (s + 1) * 256, :] = jnp.zeros((256 - SLOTS, 256), BF16)
+        terms[s * SLOTS : (s + 1) * SLOTS, :128] = high
+        terms[s * SLOTS : (s + 1) * SLOTS, 128:] = (heat - high.astype(F32)).astype(BF16)
         flag = jnp.maximum(flag, got_ref[(s + 1) * SLOTS - 1 : (s + 1) * SLOTS, :])
     lane = lax.broadcasted_iota(jnp.int32, (1, 128), 1)
     flag = jnp.where(lane == 127, flag, 0.0)
     flag_ref[0] = jnp.broadcast_to(flag, (8, 128))
-
-    @pl.loop(0, 8)
-    def _(block):
-        row = (lax.broadcasted_iota(jnp.int32, (128, 128), 0) + block * 128).astype(F32)
-        hits = []
-        for s in range(16):
-            for part in range(2):
-                at = s * SLOTS + ROOM + part
-                hits.append(jnp.where(row == got_ref[at : at + 1, :], 1.0, 0.0).astype(BF16))
+    left = lane < 64
+    names = []
+    for s in range(0, 16, 2):
+        rows = [
+            got_ref[at : at + 1, :]
+            for block in (s, s + 1)
+            for at in (block * SLOTS + ROOM, block * SLOTS + ROOM + 1)
+        ]
+        turned = pltpu.roll(rows[2], 64, 1)
+        names += [
+            rows[0],
+            jnp.where(left, rows[1], turned),
+            jnp.where(left, turned, pltpu.roll(rows[3], 64, 1)),
+        ]
+    names = jnp.concatenate(names, 1)
+    row = lax.broadcasted_iota(jnp.int32, (128, 128), 0).astype(F32).astype(BF16)
+
+    for block in range(8):
+        near = (names - block * 128.0).astype(BF16)
+        hits = [
+            jnp.where(row == near[:, g * 128 : (g + 1) * 128], BF16(1.0), BF16(0.0)) for g in range(24)
+        ]
         both = jnp.dot(jnp.concatenate(hits, 1), terms[...], preferred_element_type=F32)
-        out_ref[pl.ds(pl.multiple_of(block * 128, 128), 128), :] = both[:, :128] + both[:, 128:]
-
-
-def sum_records(got):
+        out_ref[block * 128 : (block + 1) * 128, :] = both[:, :128] + both[:, 128:]
+
+
+def sum_records(after, got):
     return pl.pallas_call(
         sum_kernel,
         out_shape=(jax.ShapeDtypeStruct((1024, 128), F32), tile(1)),
-        in_specs=[VMEM],
+        in_specs=[ANY, VMEM],
         out_specs=(VMEM, VMEM),
-        scratch_shapes=[pltpu.VMEM((4096, 256), BF16)],
+        scratch_shapes=[pltpu.VMEM((16 * SLOTS, 256), BF16)],
         compiler_params=params(24),
-    )(got)
-
-
-def row_of(ref, h):
-    return ref[pl.ds((h // 8) * 64 + h % 8, 8, stride=8), :]
+    )(after, got)
+
+
+def first_balance(flux, temp, opacity, inertia):
+    stiff = 16.0 * opacity * (temp * temp * temp)
+    emit = 0.25 * stiff * temp
+    rate = 1.0 / (inertia + stiff)
+    loss = 2.0 + opacity * inertia * rate
+    return loss, 2.0 * flux + emit * inertia * rate, stiff * rate, emit, rate
 
 
 def prepare_kernel(
-    flux_ref, temp_ref, opacity_ref, cond_ref, inertia_ref,
-    flux_out, temp_out, opacity_out, inertia_out, face_out,
-    loss_out, base_out, share_out, rate_out, gain_out, rest_out, one_out, two_out, port_out,
+    after_ref, flux_ref, temp_ref, opacity_ref, cond_ref, inertia_ref, weight_out, matrix_out, base_out
 ):
-    height = loss_out.shape[0]
-
-    def body(group, carry):
-        one, one_flow, two, two_flow = carry
+    height = weight_out.shape[0]
+
+    def body(step, carry):
+        value, value_flow, flow, flow_flow, load, load_flow = carry
         for sub in range(8):
-            h = group * 8 + sub
-            at = pl.ds(group * 64 + sub, 8, stride=8)
-            flux, temp = flux_ref[at, :], temp_ref[at, :]
-            opacity, inertia = opacity_ref[at, :], inertia_ref[at, :]
+            group = height // 8 - 1 - step
+            h = group * 8 + 7 - sub
+            at = pl.ds(group * 64 + 7 - sub, 8, stride=8)
+            loss, base, share, _, _ = first_balance(
+                flux_ref[at, :], temp_ref[at, :], opacity_ref[at, :], inertia_ref[at, :]
+            )
             face = 1.0 / cond_ref[at, :]
-            stiff = 16.0 * opacity * (temp * temp * temp)
-            emit = 0.25 * stiff * temp
-            rate = 1.0 / (inertia + stiff)
-            loss = 2.0 + opacity * inertia * rate
-            flux_out[h], temp_out[h] = 2.0 * flux, temp
-            opacity_out[h], inertia_out[h] = opacity, inertia
-            face_out[h], loss_out[h], rate_out[h] = face, loss, rate
-            base_out[h] = 2.0 * flux + emit * inertia * rate
-            share_out[h] = stiff * rate
-            gain_out[h] = opacity * rate
-            rest_out[h] = temp - emit * rate
-            one, two = one + face * one_flow, two + face * two_flow
-            one_out[h], two_out[h] = one, two
-            one_flow, two_flow = one_flow + loss * one, two_flow + loss * two
-        return one, one_flow, two, two_flow
+            weight_out[h, 0], weight_out[h, 1] = value_flow * share, flow_flow * share
+            load, load_flow = load - value_flow * base, load_flow - flow_flow * base
+            value, flow = value + loss * value_flow, flow + loss * flow_flow
+            value_flow, flow_flow = value_flow + face * value, flow_flow + face * flow
+        return value, value_flow, flow, flow_flow, load, load_flow
 
     zero = jnp.zeros((8, 128), F32)
-    one, one_flow, two, two_flow = lax.fori_loop(
-        0, height // 8, body, (zero + 1.0, zero, zero, zero + 1.0)
+    value, value_flow, flow, flow_flow, load, load_flow = lax.fori_loop(
+        0, height // 8, body, (zero + 1.0, zero, zero, zero + 1.0, zero, zero)
     )
-    port_out[0], port_out[1], port_out[2], port_out[3] = one, two, one_flow, two_flow
-
-
-def prepare(*fields):
+    matrix_out[0], matrix_out[1], matrix_out[2], matrix_out[3] = value, value_flow, flow, flow_flow
+    base_out[0], base_out[1] = load, load_flow
+
+
+def prepare(after, *fields):
     height = fields[0].shape[0] // 8
     return pl.pallas_call(
         prepare_kernel,
-        out_shape=(tile(height),) * 13 + (tile(4),),
-        in_specs=[VMEM] * 5,
-        out_specs=(VMEM,) * 14,
-        compiler_params=params(32),
-    )(*fields)
+        out_shape=(tile(height, 2), tile(4), tile(2)),
+        in_specs=[ANY] + [VMEM] * 5,
+        out_specs=(VMEM,) * 3,
+        compiler_params=params(16),
+    )(after, *fields)
 
 
 def source_at(where_ref, sums_ref, h):
@@ -395,32 +413,40 @@
     return sums_ref[sender * 8 + band]
 
 
-def load_kernel(where_ref, sums_ref, base_ref, share_ref, loss_ref, face_ref, flux_out, port_out):
-    height = base_ref.shape[0]
+def load_kernel(where_ref, flag_ref, sums_ref, base_ref, weight_ref, port_out):
+    height = weight_ref.shape[0]
 
     def body(group, carry):
-        value, flow = carry
+        totals = list(carry)
         for sub in range(8):
             h = group * 8 + sub
-            value = value + face_ref[h] * flow
-            flux_out[h] = value
-            load = base_ref[h] + share_ref[h] * source_at(where_ref, sums_ref, h)
-            flow = flow + (loss_ref[h] * value - load)
-        return value, flow
+            source = source_at(where_ref, sums_ref, h)
+            for i in range(2):
+                at = i * 4 + sub % 4
+                totals[at] = totals[at] + weight_ref[h, i] * source
+        return tuple(totals)
 
     zero = jnp.zeros((8, 128), F32)
-    value, flow = lax.fori_loop(0, height // 8, body, (zero, zero))
-    port_out[0], port_out[1] = value, flow
-
-
-def load_blocks(where, sums, base, share, loss, face):
+    totals = lax.fori_loop(0, height // 8, body, (zero,) * 8)
+    for i in range(2):
+        a, b, c, d = totals[4 * i : 4 * i + 4]
+        port_out[i] = base_ref[i] - ((a + b) + (c + d))
+    port_out[2] = flag_ref[0]
+
+
+def load_blocks(where, flag, sums, base, weight):
     return pl.pallas_call(
         load_kernel,
-        out_shape=(tile(base.shape[0]), tile(2)),
-        in_specs=[SMEM] + [VMEM] * 5,
-        out_specs=(VMEM, VMEM),
-        compiler_params=params(16),
-    )(where, sums, base, share, loss, face)
+        out_shape=tile(3),
+        in_specs=[SMEM] + [VMEM] * 4,
+        out_specs=VMEM,
+        compiler_params=params(8),
+    )(where, flag, sums, base, weight)
+
+
+def slot_of(me, block):
+    steps = (lax.shift_right_logical(block, 1) - lax.shift_right_logical(me, 1)) & 3
+    return steps * 2 + ((me ^ block) & 1)
 
 
 def block_ends(where_ref, port_of):
@@ -429,15 +455,15 @@
     drop, level = zero, zero
     draw, feed = zero, zero
     for step in range(8):
-        low = step
-        a, b, c, d, p, j = port_of(me, low)
+        low = jnp.int32(step)
+        a, b, c, d, p, j = port_of(slot_of(me, low))
         scale = 1.0 / (c * drop + d)
         new_drop = (a * drop + b) * scale
         new_level = level * scale + (p - new_drop * j)
         below = low < me
         drop, level = jnp.where(below, new_drop, drop), jnp.where(below, new_level, level)
-        high = 7 - step
-        a, b, c, d, p, j = port_of(me, high)
+        high = jnp.int32(7 - step)
+        a, b, c, d, p, j = port_of(slot_of(me, high))
         scale = 1.0 / (d + draw * b)
         new_draw = (c + draw * a) * scale
         new_feed = (feed - draw * p - j) * scale
@@ -447,73 +473,86 @@
     return value, feed - draw * value
 
 
-def slot_of(me, block):
-    apart = me ^ block
-    return (apart & 1) * 4 + (apart & 2) + lax.shift_right_logical(apart, 2)
-
-
 def second_kernel(
-    where_ref, matrix_ref, loads_ref, flag_ref, sums_ref, one_ref, two_ref, load_ref, gain_ref, rest_ref,
-    rate_ref, flux_ref, temp_ref, opacity_ref, inertia_ref, face_ref,
-    one_out, two_out, load_out, gain_out, rest_out, port_out,
+    where_ref, matrix_ref, loads_ref, sums_ref, flux_ref, temp_ref, opacity_ref, cond_ref, inertia_ref,
+    kept_hbm, port_out, crowded_out, kept_ref, sems,
 ):
-    height = one_ref.shape[0]
-
-    def port_of(me, block):
-        at = slot_of(me, block)
+    height = kept_ref.shape[0]
+
+    def port_of(at):
         return tuple(matrix_ref[at * 4 + i] for i in range(4)) + tuple(
-            loads_ref[at * 2 + i] for i in range(2)
-        )
-
-    value, flow = block_ends(where_ref, port_of)
+            loads_ref[at * 3 + i] for i in range(2)
+        )
+
+    light, light_flow = block_ends(where_ref, port_of)
+    flag = loads_ref[2]
+    for block in range(1, 8):
+        flag = jnp.maximum(flag, loads_ref[block * 3 + 2])
+    crowded_out[0] = jnp.where(jnp.max(flag) > 0.5, 1, 0)
 
     def body(group, carry):
-        one, one_flow, two, two_flow, load, load_flow = carry
+        light, light_flow, one, one_flow, two, two_flow, load, load_flow = carry
         for sub in range(8):
             h = group * 8 + sub
+            at = pl.ds(group * 64 + sub, 8, stride=8)
+            flux, before = flux_ref[at, :], temp_ref[at, :]
+            opacity, inertia = opacity_ref[at, :], inertia_ref[at, :]
+            face = 1.0 / cond_ref[at, :]
             source = source_at(where_ref, sums_ref, h)
-            light = one_ref[h] * value + two_ref[h] * flow + load_ref[h]
-            temp = rest_ref[h] + gain_ref[h] * light + rate_ref[h] * source
-            opacity, inertia, face = opacity_ref[h], inertia_ref[h], face_ref[h]
+            loss, base, share, emit, rate = first_balance(flux, before, opacity, inertia)
+            light = light + face * light_flow
+            light_flow = light_flow + (loss * light - (base + share * source))
+            temp = before + (opacity * light - emit + source) * rate
             stiff = 16.0 * opacity * (temp * temp * temp)
             emit = 0.25 * stiff * temp
             rate = 1.0 / (inertia + stiff)
             loss = 2.0 + opacity * inertia * rate
-            lag = inertia * (temp - temp_ref[h]) - source
-            right = flux_ref[h] + (emit * inertia - stiff * lag) * rate
-            gain_out[h] = opacity * rate
-            rest_out[h] = temp - (lag + emit) * rate
+            lag = inertia * (temp - before) - source
+            right = 2.0 * flux + (emit * inertia - stiff * lag) * rate
             one, two, load = one + face * one_flow, two + face * two_flow, load + face * load_flow
-            one_out[h], two_out[h], load_out[h] = one, two, load
+            kept = (one, two, load, opacity * rate, temp - (lag + emit) * rate)
+            for i, item in enumerate(kept):
+                kept_ref[h, i] = item
             one_flow, two_flow = one_flow + loss * one, two_flow + loss * two
             load_flow = load_flow + (loss * load - right)
-        return one, one_flow, two, two_flow, load, load_flow
+        return light, light_flow, one, one_flow, two, two_flow, load, load_flow
 
     zero = jnp.zeros((8, 128), F32)
-    one, one_flow, two, two_flow, load, load_flow = lax.fori_loop(
-        0, height // 8, body, (zero + 1.0, zero, zero, zero + 1.0, zero, zero)
-    )
+    carry = (light, light_flow, zero + 1.0, zero, zero, zero + 1.0, zero, zero)
+    leaving = pieces(kept_ref, kept_hbm, sems, PIECE)
+    for k, copy in enumerate(leaving):
+        carry = lax.fori_loop(k * PIECE // 8, (k + 1) * PIECE // 8, body, carry)
+        copy.start()
+    _, _, one, one_flow, two, two_flow, load, load_flow = carry
     port_out[0], port_out[1], port_out[2], port_out[3] = one, two, one_flow, two_flow
-    port_out[4], port_out[5], port_out[6] = load, load_flow, flag_ref[0]
-
-
-def second_step(where, *arrays):
-    height = arrays[4].shape[0]
+    port_out[4], port_out[5] = load, load_flow
+    for copy in leaving:
+        copy.wait()
+
+
+def second_step(where, matrix, loads, sums, *fields):
+    height = fields[0].shape[0] // 8
     return pl.pallas_call(
         second_kernel,
-        out_shape=(tile(height),) * 5 + (tile(7),),
-        in_specs=[SMEM] + [VMEM] * len(arrays),
-        out_specs=(VMEM,) * 6,
-        compiler_params=params(32),
-    )(where, *arrays)
-
-
-def finish_kernel(where_ref, ports_ref, one_ref, two_ref, load_ref, gain_ref, rest_ref, flux_out, temp_out):
-    height = one_ref.shape[0]
-
-    def port_of(me, block):
-        at = slot_of(me, block)
-        return tuple(ports_ref[at * 7 + i] for i in range(6))
+        out_shape=(tile(height, 5), tile(6), jax.ShapeDtypeStruct((1,), jnp.int32)),
+        in_specs=[SMEM] + [VMEM] * 8,
+        out_specs=(HBM, VMEM, SMEM),
+        scratch_shapes=[
+            pltpu.VMEM((height, 5, 8, 128), F32),
+            pltpu.SemaphoreType.DMA((height // PIECE,)),
+        ],
+        compiler_params=params(16),
+    )(where, matrix, loads, sums, *fields)
+
+
+def finish_kernel(where_ref, ports_ref, kept_hbm, flux_hbm, temp_hbm, kept_ref, flux_ref, temp_ref, sems):
+    height = kept_ref.shape[0]
+    copies = pieces(kept_hbm, kept_ref, sems.at[0], PIECE)
+    for copy in copies:
+        copy.start()
+
+    def port_of(at):
+        return tuple(ports_ref[at * 6 + i] for i in range(6))
 
     value, flow = block_ends(where_ref, port_of)
 
@@ -521,29 +560,48 @@
         for sub in range(8):
             h = group * 8 + sub
             at = pl.ds(group * 64 + sub, 8, stride=8)
-            light = one_ref[h] * value + two_ref[h] * flow + load_ref[h]
-            flux_out[at, :] = light
-            temp_out[at, :] = rest_ref[h] + gain_ref[h] * light
+            light = kept_ref[h, 0] * value + kept_ref[h, 1] * flow + kept_ref[h, 2]
+            flux_ref[at, :] = light
+            temp_ref[at, :] = kept_ref[h, 4] + kept_ref[h, 3] * light
         return carry
 
-    lax.fori_loop(0, height // 8, body, 0)
-
-
-def finish(where, *arrays):
-    height = arrays[1].shape[0]
+    leaving = [
+        pieces(flux_ref, flux_hbm, sems.at[1], PIECE * 8),
+        pieces(temp_ref, temp_hbm, sems.at[2], PIECE * 8),
+    ]
+    for k, copy in enumerate(copies):
+        copy.wait()
+        lax.fori_loop(k * PIECE // 8, (k + 1) * PIECE // 8, body, 0)
+        for part in leaving:
+            part[k].start()
+    for part in leaving:
+        for copy in part:
+            copy.wait()
+
+
+def finish(where, ports, kept):
+    height = kept.shape[0]
     return pl.pallas_call(
         finish_kernel,
         out_shape=(jax.ShapeDtypeStruct((height * 8, 128), F32),) * 2,
-        in_specs=[SMEM] + [VMEM] * len(arrays),
-        out_specs=(VMEM, VMEM),
+        in_specs=[SMEM, VMEM, HBM],
+        out_specs=(HBM, HBM),
+        scratch_shapes=[
+            pltpu.VMEM((height, 5, 8, 128), F32),
+            pltpu.VMEM((height * 8, 128), F32),
+            pltpu.VMEM((height * 8, 128), F32),
+            pltpu.SemaphoreType.DMA((3, height // PIECE)),
+        ],
         compiler_params=params(16),
-    )(where, *arrays)
+    )(where, ports, kept)
 
 
 def gathered(rows):
-    for by in (4, 2, 1):
-        rows = jnp.concatenate([rows, lax.ppermute(rows, "gz", [(i, i ^ by) for i in range(8)])], 0)
-    return rows
+    rows = jnp.concatenate([rows, lax.ppermute(rows, "gz", [(i, i ^ 1) for i in range(8)])], 0)
+    above = [
+        lax.ppermute(rows, "gz", [(i, (i - 2 * steps) % 8) for i in range(8)]) for steps in (1, 2, 3)
+    ]
+    return jnp.concatenate([rows] + above, 0)
 
 
 def tiles_of(field):
@@ -579,29 +637,22 @@
     where = jnp.stack([lax.axis_index("col"), lax.axis_index("gz")]).astype(jnp.int32)
     sent = pack(granule_holder.reshape(16, 128), granule_slot.reshape(16, 128), granule_power[0])
     got = lax.all_to_all(sent.reshape(16, SLOTS, 128), "col", 0, 0, tiled=True)
-    (
-        flux, temp, opacity, inertia, face, loss, base, share, rate, gain, rest, one, two, matrix,
-    ) = prepare(*[tiles_of(x) for x in arguments[:5]])
+    fields = [tiles_of(x) for x in arguments[:5]]
+    weight, matrix, base = prepare(sent, *fields)
     matrix = gathered(matrix)
-    sums, flag = sum_records(got.reshape(16 * SLOTS, 128))
+    sums, flag = sum_records(matrix, got.reshape(16 * SLOTS, 128))
     sums = lax.all_to_all(sums.reshape(16, 64, 128), "col", 0, 0, tiled=True).reshape(128, 8, 128)
-    load, loads = load_blocks(where, sums, base, share, loss, face)
-    loads = gathered(loads)
-    one, two, load, gain, rest, ports = second_step(
-        where, matrix, loads, flag, sums, one, two, load, gain, rest, rate, flux, temp, opacity, inertia, face
-    )
+    loads = gathered(load_blocks(where, flag, sums, base, weight))
+    kept, ports, crowded = second_step(where, matrix, loads, sums, *fields)
     ports = gathered(ports)
-    crowded = jnp.max(ports.reshape(8, 7, 8, 128)[:, 6, 0, 127]) > 0.5
 
     def quick(_):
-        return tuple(
-            field_of(x, height, width) for x in finish(where, ports, one, two, load, gain, rest)
-        )
+        return tuple(field_of(x, height, width) for x in finish(where, ports, kept))
 
     def general(operands):
         return general_path(*operands)
 
-    return lax.cond(crowded, general, quick, arguments)
+    return lax.cond(crowded[0] > 0, general, quick, arguments)
 
 
 def solution(mesh):

time: 94 us -> 83.9 us (0.89)
  blocking collectives: 30 us -> 0 us
  waiting for transfers between devices: 10.1 us -> 34.6 us
  local copies, waits for them, and re-layouts: 9.52 us -> 0.09 us
  starting transfers between devices: 19.4 us -> 28.6 us
  Pallas kernels: 22.3 us -> 18.3 us
    all_to_all x1 -> x0, blocking collectives: 30 us -> none  [shards(): got = lax.all_to_all(sent.reshape(16, SLOTS, 128), 'col', 0, 0, tiled=True)]
    all_to_all x0 -> x1, waiting for transfers between devices: none -> 11 us  [shards(): got = lax.all_to_all(sent.reshape(16, SLOTS, 128), 'col', 0, 0, tiled=True)]
    all_to_all x1, waiting for transfers between devices: 0.01 us -> 10 us  [shards(): lax.all_to_all(sums.reshape(16, 64, 128), 'col', 0, 0, tiled=True)]
    unnamed x39 -> x22, local copies, waits for them, and re-layouts: 9.51 us -> 0.07 us
    all_to_all x0 -> x1, starting transfers between devices: none -> 8.57 us  [shards(): got = lax.all_to_all(sent.reshape(16, SLOTS, 128), 'col', 0, 0, tiled=True)]
    ppermute x9 -> x12, waiting for transfers between devices: 10.1 us -> 13.6 us  [the longest x9 11.1 us: gathered(): lax.ppermute(rows, 'gz', [(i, (i - 2 * steps) % 8) for i in range(8)])]
    pallas_call x1, Pallas kernels: 7.05 us -> 4.79 us  [pack(): pl.pallas_call(pack_kernel, out_shape=jax.ShapeDtypeStruct((16 * SLOTS, 1...]
    pallas_call x1, Pallas kernels: 4.66 us -> 2.66 us  [sum_records(): pl.pallas_call(sum_kernel, out_shape=(jax.ShapeDtypeStruct((1024, 128), F...]
  transfers between devices with their start and end apart: 10 -> 14, of which waited for: 5 -> 11; matrix products, arithmetic and copies ran while one was open for 0% -> 0% of each run, Pallas kernels for 4% -> 3%
where the time goes in v2:
time: 83.9 us; the launch traced here: 83.5 us
  waiting for transfers between devices  34.6 us (41%)
  starting transfers between devices  28.6 us (34%)
  Pallas kernels  18.3 us (22%)
  between operations  1.61 us (2%)
    ppermute x9, waiting for transfers between devices, gathered(): lax.ppermute(rows, 'gz', [(i, (i - 2 * steps) % 8) for i in range(8)])  11.1 us
    all_to_all x1, waiting for transfers between devices, shards(): got = lax.all_to_all(sent.reshape(16, SLOTS, 128), 'col', 0, 0, tiled=True)  11 us
    all_to_all x1, waiting for transfers between devices, shards(): lax.all_to_all(sums.reshape(16, 64, 128), 'col', 0, 0, tiled=True)  10 us
    ppermute x9, starting transfers between devices, gathered(): lax.ppermute(rows, 'gz', [(i, (i - 2 * steps) % 8) for i in range(8)])  9.9 us
    all_to_all x1, starting transfers between devices, shards(): got = lax.all_to_all(sent.reshape(16, SLOTS, 128), 'col', 0, 0, tiled=True)  8.57 us
    ppermute x3, starting transfers between devices, gathered(): lax.ppermute(rows, 'gz', [(i, i ^ 1) for i in range(8)])  5.4 us
    pallas_call x1, Pallas kernels, pack(): pl.pallas_call(pack_kernel, out_shape=jax.ShapeDtypeStruct((16 * SLOTS, 1...  4.79 us
    all_to_all x1, starting transfers between devices, shards(): lax.all_to_all(sums.reshape(16, 64, 128), 'col', 0, 0, tiled=True)  4.7 us
  transfers between devices with their start and end apart: 14, of which 11 were waited for; matrix products, arithmetic and copies ran while one was open for 0% of the time, Pallas kernels for 3%

profile of v2, /device:TPU:1, one launch (start us, length us, event | category | flops | bytes accessed | tf_op | source)
XLA Modules:
  0.0 83.5 jit_solution(11162790296414011844)
XLA Ops:
  0.6 4.8 %shard_map.99.after_ref = f32[3072,128]{1,0:T(8,128)} custom-call(s32[16,128]{1,0:T(8,128)} %bitcast.238, s32[16,128]{1,0:T(8,128)} %bitcast.244, f32[2048,128]{1,0:T(8,128)} %bitcast.236), custom_call_target="tpu_custom_call" | custom-call | tf_op jit(solution)/shard_map/pallas_call | solution.py:298
  5.4 8.6 %all-to-all-start.2 = ((f32[16,192,128]{2,1,0:T(8,128)}), f32[16,192,128]{2,1,0:T(8,128)S(1)}, u32[]{:S(2)}, u32[]{:S(2)}) async-start(f32[16,192,128]{2,1,0:T(8,128)} %bitcast.111), calls=%async_computation.2 | async-start | bytes 3145728 | tf_op jit(solution)/shard_map/all_to_all | solution.py:639
  14.0 2.3 %shard_map.100 = (f32[128,2,8,128]{3,2,1,0:T(8,128)S(1)}, f32[4,8,128]{2,1,0:T(8,128)S(1)}, f32[2,8,128]{2,1,0:T(8,128)S(1)}) custom-call(f32[3072,128]{1,0:T(8,128)} %shard_map.99.after_ref, f32[1024,128]{1,0:T(8,128)S(1)} %bitcast.225, f32[1024,128]{1,0:T(8,128)} %bitcast.229, f32[1024,128]{1,0:T(8,128)} %bitcast.231, f32[1024,128]{1,0:T(8,128)} %bitcast.227, ...), custom_call_target="tpu_custom_call" | custom-call | tf_op jit(solution)/shard_map/pallas_call | solution.py:401
  16.4 1.0 %collective-permute-start.21 = (f32[4,8,128]{2,1,0:T(8,128)S(1)}, f32[4,8,128]{2,1,0:T(8,128)S(1)}, u32[]{:S(2)}, u32[]{:S(2)}) collective-permute-start(f32[4,8,128]{2,1,0:T(8,128)S(1)} %get-tuple-element.45), channel_id=1, source_target_pairs={{0,1},{1,0},{2,3},{3,2},{4,5},{5,4},{6,7},{7,6},{8,9},{9,8},{10,11... | collective-permute-start | bytes 49160 | tf_op jit(solution)/shard_map/ppermute | solution.py:600
  17.4 0.8 %collective-permute-done.21 = f32[4,8,128]{2,1,0:T(8,128)S(1)} collective-permute-done((f32[4,8,128]{2,1,0:T(8,128)S(1)}, f32[4,8,128]{2,1,0:T(8,128)S(1)}, u32[]{:S(2)}, u32[]{:S(2)}) %collective-permute-start.21) | collective-permute-done | bytes 16416 | tf_op jit(solution)/shard_map/ppermute | solution.py:600
  18.3 2.7 %collective-permute-start.22 = (f32[8,8,128]{2,1,0:T(8,128)S(1)}, f32[8,8,128]{2,1,0:T(8,128)S(1)}, u32[]{:S(2)}, u32[]{:S(2)}) collective-permute-start(f32[8,8,128]{2,1,0:T(8,128)S(1)} %get-tuple-element.261), channel_id=1, source_target_pairs={{0,6},{1,7},{2,0},{3,1},{4,2},{5,3},{6,4},{7,5},{8,14},{9,15},{10,... | collective-permute-start | bytes 98312 | tf_op jit(solution)/shard_map/ppermute | solution.py:602
  22.0 3.5 %collective-permute-done.23 = f32[8,8,128]{2,1,0:T(8,128)S(1)} collective-permute-done((f32[8,8,128]{2,1,0:T(8,128)S(1)}, f32[8,8,128]{2,1,0:T(8,128)S(1)}, u32[]{:S(2)}, u32[]{:S(2)}) %collective-permute-start.23) | collective-permute-done | bytes 32800 | tf_op jit(solution)/shard_map/ppermute | solution.py:602
  25.9 11.0 %all-to-all-done.2 = f32[16,192,128]{2,1,0:T(8,128)S(1)} async-done(((f32[16,192,128]{2,1,0:T(8,128)}), f32[16,192,128]{2,1,0:T(8,128)S(1)}, u32[]{:S(2)}, u32[]{:S(2)}) %all-to-all-start.2) | async-done | bytes 1572896 | tf_op jit(solution)/shard_map/all_to_all | solution.py:639
  36.9 2.7 %shard_map.101 = (f32[1024,128]{1,0:T(8,128)}, f32[1,8,128]{2,1,0:T(8,128)S(1)}) custom-call(f32[32,8,128]{2,1,0:T(8,128)S(1)} %constant_dynamic-update-slice_fusion.2.after_ref.matrix_ref, f32[3072,128]{1,0:T(8,128)S(1)} %bitcast.222), custom_call_target="tpu_custom_call" | custom-call | tf_op jit(solution)/shard_map/pallas_call | solution.py:352
  39.6 4.7 %all-to-all-start.3 = ((f32[16,64,128]{2,1,0:T(8,128)}), f32[16,64,128]{2,1,0:T(8,128)S(1)}, u32[]{:S(2)}, u32[]{:S(2)}) async-start(f32[16,64,128]{2,1,0:T(8,128)} %bitcast.113), calls=%async_computation.3 | async-start | bytes 1048576 | tf_op jit(solution)/shard_map/all_to_all | solution.py:644
  44.3 10.0 %all-to-all-done.3 = f32[16,64,128]{2,1,0:T(8,128)S(1)} async-done(((f32[16,64,128]{2,1,0:T(8,128)}), f32[16,64,128]{2,1,0:T(8,128)S(1)}, u32[]{:S(2)}, u32[]{:S(2)}) %all-to-all-start.3) | async-done | bytes 524320 | tf_op jit(solution)/shard_map/all_to_all | solution.py:644
  54.4 1.4 %shard_map.102 = f32[3,8,128]{2,1,0:T(8,128)S(1)} custom-call(s32[2]{0:T(128)S(1)} %pad_add_fusion.1.where_ref, f32[1,8,128]{2,1,0:T(8,128)S(1)} %get-tuple-element.46.flag_ref, f32[128,8,128]{2,1,0:T(8,128)S(1)} %bitcast.223, f32[2,8,128]{2,1,0:T(8,128)S(1)} %get-tuple-element.48.base_ref, f32[128,2,8,128]{3,2,1,0:T(8,128)S(1)} %get-tuple-element.49.weight_ref), custom_call_target="tpu_custom_call" | custom-call | tf_op jit(solution)/shard_map/pallas_call | solution.py:438
  55.8 2.4 %collective-permute-start.25 = (f32[3,8,128]{2,1,0:T(8,128)S(1)}, f32[3,8,128]{2,1,0:T(8,128)S(1)}, u32[]{:S(2)}, u32[]{:S(2)}) collective-permute-start(f32[3,8,128]{2,1,0:T(8,128)S(1)} %shard_map.102), channel_id=1, source_target_pairs={{0,1},{1,0},{2,3},{3,2},{4,5},{5,4},{6,7},{7,6},{8,9},{9,8},{10,11... | collective-permute-start | bytes 36872 | tf_op jit(solution)/shard_map/ppermute | solution.py:600
  59.1 2.7 %collective-permute-start.26 = (f32[6,8,128]{2,1,0:T(8,128)S(1)}, f32[6,8,128]{2,1,0:T(8,128)S(1)}, u32[]{:S(2)}, u32[]{:S(2)}) collective-permute-start(f32[6,8,128]{2,1,0:T(8,128)S(1)} %pad_maximum_fusion.13), channel_id=1, source_target_pairs={{0,6},{1,7},{2,0},{3,1},{4,2},{5,3},{6,4},{7,5},{8,14},{9,15},{10,... | collective-permute-start | bytes 73736 | tf_op jit(solution)/shard_map/ppermute | solution.py:602
  62.9 3.1 %collective-permute-done.27 = f32[6,8,128]{2,1,0:T(8,128)S(1)} collective-permute-done((f32[6,8,128]{2,1,0:T(8,128)S(1)}, f32[6,8,128]{2,1,0:T(8,128)S(1)}, u32[]{:S(2)}, u32[]{:S(2)}) %collective-permute-start.27) | collective-permute-done | bytes 24608 | tf_op jit(solution)/shard_map/ppermute | solution.py:602
  66.4 4.4 %shard_map.103 = (f32[128,5,8,128]{3,2,1,0:T(8,128)S(1)}, f32[6,8,128]{2,1,0:T(8,128)S(1)}, s32[1]{0:T(128)}) custom-call(s32[2]{0:T(128)S(1)} %pad_add_fusion.1.where_ref, f32[32,8,128]{2,1,0:T(8,128)S(1)} %constant_dynamic-update-slice_fusion.2.after_ref.matrix_ref, f32[24,8,128]{2,1,0:T(8,128)S(1)} %constant_dynamic-update-slice_fusion.7.loads_ref, ...), custom_call_target="tpu_custom_call" | custom-call | tf_op jit(solution)/shard_map/pallas_call | solution.py:535
  70.8 1.9 %collective-permute-start.29 = (f32[6,8,128]{2,1,0:T(8,128)S(1)}, f32[6,8,128]{2,1,0:T(8,128)S(1)}, u32[]{:S(2)}, u32[]{:S(2)}) collective-permute-start(f32[6,8,128]{2,1,0:T(8,128)S(1)} %get-tuple-element.51), channel_id=1, source_target_pairs={{0,1},{1,0},{2,3},{3,2},{4,5},{5,4},{6,7},{7,6},{8,9},{9,8},{10,11... | collective-permute-start | bytes 73736 | tf_op jit(solution)/shard_map/ppermute | solution.py:600
  72.7 0.8 %collective-permute-done.29 = f32[6,8,128]{2,1,0:T(8,128)S(1)} collective-permute-done((f32[6,8,128]{2,1,0:T(8,128)S(1)}, f32[6,8,128]{2,1,0:T(8,128)S(1)}, u32[]{:S(2)}, u32[]{:S(2)}) %collective-permute-start.29) | collective-permute-done | bytes 24608 | tf_op jit(solution)/shard_map/ppermute | solution.py:600
  74.5 1.3 %collective-permute-start.31 = (f32[12,8,128]{2,1,0:T(8,128)S(1)}, f32[12,8,128]{2,1,0:T(8,128)S(1)}, u32[]{:S(2)}, u32[]{:S(2)}) collective-permute-start(f32[12,8,128]{2,1,0:T(8,128)S(1)} %get-tuple-element.257), channel_id=1, source_target_pairs={{0,4},{1,5},{2,6},{3,7},{4,0},{5,1},{6,2},{7,3},{8,12},{9,13},{10,... | collective-permute-start | bytes 147464 | tf_op jit(solution)/shard_map/ppermute | solution.py:602
  75.7 0.9 %collective-permute-start.32 = (f32[12,8,128]{2,1,0:T(8,128)S(1)}, f32[12,8,128]{2,1,0:T(8,128)S(1)}, u32[]{:S(2)}, u32[]{:S(2)}) collective-permute-start(f32[12,8,128]{2,1,0:T(8,128)S(1)} %get-tuple-element.257), channel_id=1, source_target_pairs={{0,2},{1,3},{2,4},{3,5},{4,6},{5,7},{6,0},{7,1},{8,10},{9,11},{10,... | collective-permute-start | bytes 147464 | tf_op jit(solution)/shard_map/ppermute | solution.py:602
  76.6 2.4 %collective-permute-done.31 = f32[12,8,128]{2,1,0:T(8,128)S(1)} collective-permute-done((f32[12,8,128]{2,1,0:T(8,128)S(1)}, f32[12,8,128]{2,1,0:T(8,128)S(1)}, u32[]{:S(2)}, u32[]{:S(2)}) %collective-permute-start.31) | collective-permute-done | bytes 49184 | tf_op jit(solution)/shard_map/ppermute | solution.py:602
  79.0 1.4 %collective-permute-done.32 = f32[12,8,128]{2,1,0:T(8,128)S(1)} collective-permute-done((f32[12,8,128]{2,1,0:T(8,128)S(1)}, f32[12,8,128]{2,1,0:T(8,128)S(1)}, u32[]{:S(2)}, u32[]{:S(2)}) %collective-permute-start.32) | collective-permute-done | bytes 49184 | tf_op jit(solution)/shard_map/ppermute | solution.py:602
  80.5 2.8 %conditional.1 = (f32[128,1024]{1,0:T(8,128)}, f32[128,1024]{1,0:T(8,128)}) conditional(s32[]{:T(128)} %bitcast.115, (s32[2]{0:T(128)S(1)}, f32[48,8,128]{2,1,0:T(8,128)S(1)}, f32[128,5,8,128]{3,2,1,0:T(8,128)S(1)}) %tuple.15, (f32[128,1024]{1,0:T(8,128)S(1)}, f32[128,1024]{1,0:T(8,128)S(1)}, f32[128,1024]{1,0:T(8,128)S(1)}, ...), branch_computations={%region_0.0_spmd, %region_1.8_spmd} | conditional | flops 77854064 | bytes 392449088 | solution.py:655
  80.5 2.6 %branch_0_fun.1 = (f32[1024,128]{1,0:T(8,128)}, f32[1024,128]{1,0:T(8,128)}) custom-call(s32[2]{0:T(128)S(1)} %get-tuple-element.22.where_ref, f32[48,8,128]{2,1,0:T(8,128)S(1)} %get-tuple-element.23.ports_ref, f32[128,5,8,128]{3,2,1,0:T(8,128)S(1)} %get-tuple-element.24.kept_hbm), custom_call_target="tpu_custom_call" | custom-call | tf_op jit(solution)/shard_map/cond/branch_0_fun/pallas_call | solution.py:584
  (40 shorter events, 3.9 us)
Async XLA Ops:
  5.4 8.6 %copy-start = (f32[128,1024]{1,0:T(8,128)S(1)}, f32[128,1024]{1,0:T(8,128)}, u32[]{:S(2)}) copy-start(f32[128,1024]{1,0:T(8,128)} %param.10) | copy-start | bytes 1572868
  5.4 31.5 %all-to-all-start.2 = ((f32[16,192,128]{2,1,0:T(8,128)}), f32[16,192,128]{2,1,0:T(8,128)S(1)}, u32[]{:S(2)}, u32[]{:S(2)}) async-start(f32[16,192,128]{2,1,0:T(8,128)} %bitcast.111), calls=%async_computation.2 | async-start | bytes 3145728 | tf_op jit(solution)/shard_map/all_to_all | solution.py:639
  16.4 1.9 %collective-permute-start.21 = (f32[4,8,128]{2,1,0:T(8,128)S(1)}, f32[4,8,128]{2,1,0:T(8,128)S(1)}, u32[]{:S(2)}, u32[]{:S(2)}) collective-permute-start(f32[4,8,128]{2,1,0:T(8,128)S(1)} %get-tuple-element.45), channel_id=1, source_target_pairs={{0,1},{1,0},{2,3},{3,2},{4,5},{5,4},{6,7},{7,6},{8,9},{9,8},{10,11... | collective-permute-start | bytes 49160 | tf_op jit(solution)/shard_map/ppermute | solution.py:600
  18.3 3.8 %collective-permute-start.22 = (f32[8,8,128]{2,1,0:T(8,128)S(1)}, f32[8,8,128]{2,1,0:T(8,128)S(1)}, u32[]{:S(2)}, u32[]{:S(2)}) collective-permute-start(f32[8,8,128]{2,1,0:T(8,128)S(1)} %get-tuple-element.261), channel_id=1, source_target_pairs={{0,6},{1,7},{2,0},{3,1},{4,2},{5,3},{6,4},{7,5},{8,14},{9,15},{10,... | collective-permute-start | bytes 98312 | tf_op jit(solution)/shard_map/ppermute | solution.py:602
  21.0 4.6 %collective-permute-start.23 = (f32[8,8,128]{2,1,0:T(8,128)S(1)}, f32[8,8,128]{2,1,0:T(8,128)S(1)}, u32[]{:S(2)}, u32[]{:S(2)}) collective-permute-start(f32[8,8,128]{2,1,0:T(8,128)S(1)} %get-tuple-element.261), channel_id=1, source_target_pairs={{0,4},{1,5},{2,6},{3,7},{4,0},{5,1},{6,2},{7,3},{8,12},{9,13},{10,... | collective-permute-start | bytes 98312 | tf_op jit(solution)/shard_map/ppermute | solution.py:602
  21.4 4.6 %collective-permute-start.24 = (f32[8,8,128]{2,1,0:T(8,128)S(1)}, f32[8,8,128]{2,1,0:T(8,128)S(1)}, u32[]{:S(2)}, u32[]{:S(2)}) collective-permute-start(f32[8,8,128]{2,1,0:T(8,128)S(1)} %get-tuple-element.261), channel_id=1, source_target_pairs={{0,2},{1,3},{2,4},{3,5},{4,6},{5,7},{6,0},{7,1},{8,10},{9,11},{10,... | collective-permute-start | bytes 98312 | tf_op jit(solution)/shard_map/ppermute | solution.py:602
  39.6 26.8 %copy-start.1 = (f32[128,1024]{1,0:T(8,128)S(1)}, f32[128,1024]{1,0:T(8,128)}, u32[]{:S(2)}) copy-start(f32[128,1024]{1,0:T(8,128)} %param.13) | copy-start | bytes 1572868
  39.6 14.8 %all-to-all-start.3 = ((f32[16,64,128]{2,1,0:T(8,128)}), f32[16,64,128]{2,1,0:T(8,128)S(1)}, u32[]{:S(2)}, u32[]{:S(2)}) async-start(f32[16,64,128]{2,1,0:T(8,128)} %bitcast.113), calls=%async_computation.3 | async-start | bytes 1048576 | tf_op jit(solution)/shard_map/all_to_all | solution.py:644
  55.8 3.3 %collective-permute-start.25 = (f32[3,8,128]{2,1,0:T(8,128)S(1)}, f32[3,8,128]{2,1,0:T(8,128)S(1)}, u32[]{:S(2)}, u32[]{:S(2)}) collective-permute-start(f32[3,8,128]{2,1,0:T(8,128)S(1)} %shard_map.102), channel_id=1, source_target_pairs={{0,1},{1,0},{2,3},{3,2},{4,5},{5,4},{6,7},{7,6},{8,9},{9,8},{10,11... | collective-permute-start | bytes 36872 | tf_op jit(solution)/shard_map/ppermute | solution.py:600
  59.1 3.8 %collective-permute-start.26 = (f32[6,8,128]{2,1,0:T(8,128)S(1)}, f32[6,8,128]{2,1,0:T(8,128)S(1)}, u32[]{:S(2)}, u32[]{:S(2)}) collective-permute-start(f32[6,8,128]{2,1,0:T(8,128)S(1)} %pad_maximum_fusion.13), channel_id=1, source_target_pairs={{0,6},{1,7},{2,0},{3,1},{4,2},{5,3},{6,4},{7,5},{8,14},{9,15},{10,... | collective-permute-start | bytes 73736 | tf_op jit(solution)/shard_map/ppermute | solution.py:602
  61.9 4.2 %collective-permute-start.27 = (f32[6,8,128]{2,1,0:T(8,128)S(1)}, f32[6,8,128]{2,1,0:T(8,128)S(1)}, u32[]{:S(2)}, u32[]{:S(2)}) collective-permute-start(f32[6,8,128]{2,1,0:T(8,128)S(1)} %pad_maximum_fusion.13), channel_id=1, source_target_pairs={{0,4},{1,5},{2,6},{3,7},{4,0},{5,1},{6,2},{7,3},{8,12},{9,13},{10,... | collective-permute-start | bytes 73736 | tf_op jit(solution)/shard_map/ppermute | solution.py:602
  62.2 4.1 %collective-permute-start.28 = (f32[6,8,128]{2,1,0:T(8,128)S(1)}, f32[6,8,128]{2,1,0:T(8,128)S(1)}, u32[]{:S(2)}, u32[]{:S(2)}) collective-permute-start(f32[6,8,128]{2,1,0:T(8,128)S(1)} %pad_maximum_fusion.13), channel_id=1, source_target_pairs={{0,2},{1,3},{2,4},{3,5},{4,6},{5,7},{6,0},{7,1},{8,10},{9,11},{10,... | collective-permute-start | bytes 73736 | tf_op jit(solution)/shard_map/ppermute | solution.py:602
  66.3 14.1 %copy-start.2 = (f32[128,1024]{1,0:T(8,128)S(1)}, f32[128,1024]{1,0:T(8,128)}, u32[]{:S(2)}) copy-start(f32[128,1024]{1,0:T(8,128)} %param.11) | copy-start | bytes 1572868
  66.3 14.1 %copy-start.3 = (f32[128,1024]{1,0:T(8,128)S(1)}, f32[128,1024]{1,0:T(8,128)}, u32[]{:S(2)}) copy-start(f32[128,1024]{1,0:T(8,128)} %param.12) | copy-start | bytes 1572868
  66.3 14.1 %copy-start.15 = (s32[1,2048,1]{1,2,0:T(1,128)S(1)}, s32[1,2048,1]{1,2,0:T(1,128)}, u32[]{:S(2)}) copy-start(s32[1,2048,1]{1,2,0:T(1,128)} %param.16) | copy-start | bytes 24580
  66.3 14.1 %copy-start.16 = (s32[1,2048]{1,0:T(1,128)S(1)}, s32[1,2048]{1,0:T(1,128)}, u32[]{:S(2)}) copy-start(s32[1,2048]{1,0:T(1,128)} %param.17) | copy-start | bytes 24580
  70.8 2.8 %collective-permute-start.29 = (f32[6,8,128]{2,1,0:T(8,128)S(1)}, f32[6,8,128]{2,1,0:T(8,128)S(1)}, u32[]{:S(2)}, u32[]{:S(2)}) collective-permute-start(f32[6,8,128]{2,1,0:T(8,128)S(1)} %get-tuple-element.51), channel_id=1, source_target_pairs={{0,1},{1,0},{2,3},{3,2},{4,5},{5,4},{6,7},{7,6},{8,9},{9,8},{10,11... | collective-permute-start | bytes 73736 | tf_op jit(solution)/shard_map/ppermute | solution.py:600
  73.6 3.0 %collective-permute-start.30 = (f32[12,8,128]{2,1,0:T(8,128)S(1)}, f32[12,8,128]{2,1,0:T(8,128)S(1)}, u32[]{:S(2)}, u32[]{:S(2)}) collective-permute-start(f32[12,8,128]{2,1,0:T(8,128)S(1)} %get-tuple-element.257), channel_id=1, source_target_pairs={{0,6},{1,7},{2,0},{3,1},{4,2},{5,3},{6,4},{7,5},{8,14},{9,15},{10,... | collective-permute-start | bytes 147464 | tf_op jit(solution)/shard_map/ppermute | solution.py:602
  74.5 4.5 %collective-permute-start.31 = (f32[12,8,128]{2,1,0:T(8,128)S(1)}, f32[12,8,128]{2,1,0:T(8,128)S(1)}, u32[]{:S(2)}, u32[]{:S(2)}) collective-permute-start(f32[12,8,128]{2,1,0:T(8,128)S(1)} %get-tuple-element.257), channel_id=1, source_target_pairs={{0,4},{1,5},{2,6},{3,7},{4,0},{5,1},{6,2},{7,3},{8,12},{9,13},{10,... | collective-permute-start | bytes 147464 | tf_op jit(solution)/shard_map/ppermute | solution.py:602
  75.7 4.7 %collective-permute-start.32 = (f32[12,8,128]{2,1,0:T(8,128)S(1)}, f32[12,8,128]{2,1,0:T(8,128)S(1)}, u32[]{:S(2)}, u32[]{:S(2)}) collective-permute-start(f32[12,8,128]{2,1,0:T(8,128)S(1)} %get-tuple-element.257), channel_id=1, source_target_pairs={{0,2},{1,3},{2,4},{3,5},{4,6},{5,7},{6,0},{7,1},{8,10},{9,11},{10,... | collective-permute-start | bytes 147464 | tf_op jit(solution)/shard_map/ppermute | solution.py:602

commit v3 on v2

--- a/solution.py
+++ b/solution.py
@@ -473,25 +473,13 @@
     return value, feed - draw * value
 
 
-def second_kernel(
-    where_ref, matrix_ref, loads_ref, sums_ref, flux_ref, temp_ref, opacity_ref, cond_ref, inertia_ref,
-    kept_hbm, port_out, crowded_out, kept_ref, sems,
+def middle_kernel(
+    after_ref, where_ref, sums_ref, flux_ref, temp_ref, opacity_ref, cond_ref, inertia_ref, kept_out
 ):
-    height = kept_ref.shape[0]
-
-    def port_of(at):
-        return tuple(matrix_ref[at * 4 + i] for i in range(4)) + tuple(
-            loads_ref[at * 3 + i] for i in range(2)
-        )
-
-    light, light_flow = block_ends(where_ref, port_of)
-    flag = loads_ref[2]
-    for block in range(1, 8):
-        flag = jnp.maximum(flag, loads_ref[block * 3 + 2])
-    crowded_out[0] = jnp.where(jnp.max(flag) > 0.5, 1, 0)
+    height = kept_out.shape[0]
 
     def body(group, carry):
-        light, light_flow, one, one_flow, two, two_flow, load, load_flow = carry
+        one, one_flow, two, two_flow, load, load_flow = carry
         for sub in range(8):
             h = group * 8 + sub
             at = pl.ds(group * 64 + sub, 8, stride=8)
@@ -500,56 +488,90 @@
             face = 1.0 / cond_ref[at, :]
             source = source_at(where_ref, sums_ref, h)
             loss, base, share, emit, rate = first_balance(flux, before, opacity, inertia)
-            light = light + face * light_flow
-            light_flow = light_flow + (loss * light - (base + share * source))
-            temp = before + (opacity * light - emit + source) * rate
+            one, two, load = one + face * one_flow, two + face * two_flow, load + face * load_flow
+            kept = (
+                one, two, load, face, opacity, inertia, opacity * rate,
+                before + (source - emit) * rate, inertia * before + source, 2.0 * flux,
+            )
+            for i, item in enumerate(kept):
+                kept_out[h, i] = item
+            one_flow, two_flow = one_flow + loss * one, two_flow + loss * two
+            load_flow = load_flow + (loss * load - (base + share * source))
+        return one, one_flow, two, two_flow, load, load_flow
+
+    zero = jnp.zeros((8, 128), F32)
+    lax.fori_loop(0, height // 8, body, (zero + 1.0, zero, zero, zero + 1.0, zero, zero))
+
+
+def middle(after, where, sums, *fields):
+    height = fields[0].shape[0] // 8
+    return pl.pallas_call(
+        middle_kernel,
+        out_shape=tile(height, 10),
+        in_specs=[ANY, SMEM] + [VMEM] * 6,
+        out_specs=VMEM,
+        compiler_params=params(16),
+    )(after, where, sums, *fields)
+
+
+def second_kernel(where_ref, matrix_ref, loads_ref, middle_ref, kept_out, port_out):
+    height = kept_out.shape[0]
+
+    def port_of(at):
+        return tuple(matrix_ref[at * 4 + i] for i in range(4)) + tuple(
+            loads_ref[at * 3 + i] for i in range(2)
+        )
+
+    value, flow = block_ends(where_ref, port_of)
+
+    def body(group, carry):
+        one, one_flow, two, two_flow, load, load_flow = carry
+        for sub in range(8):
+            h = group * 8 + sub
+            face, opacity, inertia = middle_ref[h, 3], middle_ref[h, 4], middle_ref[h, 5]
+            light = middle_ref[h, 0] * value + middle_ref[h, 1] * flow + middle_ref[h, 2]
+            temp = middle_ref[h, 7] + middle_ref[h, 6] * light
             stiff = 16.0 * opacity * (temp * temp * temp)
             emit = 0.25 * stiff * temp
             rate = 1.0 / (inertia + stiff)
             loss = 2.0 + opacity * inertia * rate
-            lag = inertia * (temp - before) - source
-            right = 2.0 * flux + (emit * inertia - stiff * lag) * rate
+            lag = inertia * temp - middle_ref[h, 8]
+            right = middle_ref[h, 9] + (emit * inertia - stiff * lag) * rate
             one, two, load = one + face * one_flow, two + face * two_flow, load + face * load_flow
             kept = (one, two, load, opacity * rate, temp - (lag + emit) * rate)
             for i, item in enumerate(kept):
-                kept_ref[h, i] = item
+                kept_out[h, i] = item
             one_flow, two_flow = one_flow + loss * one, two_flow + loss * two
             load_flow = load_flow + (loss * load - right)
-        return light, light_flow, one, one_flow, two, two_flow, load, load_flow
+        return one, one_flow, two, two_flow, load, load_flow
 
     zero = jnp.zeros((8, 128), F32)
-    carry = (light, light_flow, zero + 1.0, zero, zero, zero + 1.0, zero, zero)
-    leaving = pieces(kept_ref, kept_hbm, sems, PIECE)
-    for k, copy in enumerate(leaving):
-        carry = lax.fori_loop(k * PIECE // 8, (k + 1) * PIECE // 8, body, carry)
-        copy.start()
-    _, _, one, one_flow, two, two_flow, load, load_flow = carry
+    one, one_flow, two, two_flow, load, load_flow = lax.fori_loop(
+        0, height // 8, body, (zero + 1.0, zero, zero, zero + 1.0, zero, zero)
+    )
     port_out[0], port_out[1], port_out[2], port_out[3] = one, two, one_flow, two_flow
     port_out[4], port_out[5] = load, load_flow
-    for copy in leaving:
-        copy.wait()
-
-
-def second_step(where, matrix, loads, sums, *fields):
-    height = fields[0].shape[0] // 8
+
+
+def second_step(where, matrix, loads, kept):
+    height = kept.shape[0]
     return pl.pallas_call(
         second_kernel,
-        out_shape=(tile(height, 5), tile(6), jax.ShapeDtypeStruct((1,), jnp.int32)),
-        in_specs=[SMEM] + [VMEM] * 8,
-        out_specs=(HBM, VMEM, SMEM),
-        scratch_shapes=[
-            pltpu.VMEM((height, 5, 8, 128), F32),
-            pltpu.SemaphoreType.DMA((height // PIECE,)),
-        ],
+        out_shape=(tile(height, 5), tile(6)),
+        in_specs=[SMEM] + [VMEM] * 3,
+        out_specs=(VMEM, VMEM),
         compiler_params=params(16),
-    )(where, matrix, loads, sums, *fields)
-
-
-def finish_kernel(where_ref, ports_ref, kept_hbm, flux_hbm, temp_hbm, kept_ref, flux_ref, temp_ref, sems):
+    )(where, matrix, loads, kept)
+
+
+def finish_kernel(
+    where_ref, loads_ref, ports_ref, kept_ref, flux_hbm, temp_hbm, crowded_out, flux_ref, temp_ref, sems
+):
     height = kept_ref.shape[0]
-    copies = pieces(kept_hbm, kept_ref, sems.at[0], PIECE)
-    for copy in copies:
-        copy.start()
+    flag = loads_ref[2]
+    for block in range(1, 8):
+        flag = jnp.maximum(flag, loads_ref[block * 3 + 2])
+    crowded_out[0] = jnp.where(jnp.max(flag) > 0.5, 1, 0)
 
     def port_of(at):
         return tuple(ports_ref[at * 6 + i] for i in range(6))
@@ -566,11 +588,10 @@
         return carry
 
     leaving = [
-        pieces(flux_ref, flux_hbm, sems.at[1], PIECE * 8),
-        pieces(temp_ref, temp_hbm, sems.at[2], PIECE * 8),
+        pieces(flux_ref, flux_hbm, sems.at[0], PIECE * 8),
+        pieces(temp_ref, temp_hbm, sems.at[1], PIECE * 8),
     ]
-    for k, copy in enumerate(copies):
-        copy.wait()
+    for k in range(height // PIECE):
         lax.fori_loop(k * PIECE // 8, (k + 1) * PIECE // 8, body, 0)
         for part in leaving:
             part[k].start()
@@ -579,29 +600,36 @@
             copy.wait()
 
 
-def finish(where, ports, kept):
+def finish(where, loads, ports, kept):
     height = kept.shape[0]
     return pl.pallas_call(
         finish_kernel,
-        out_shape=(jax.ShapeDtypeStruct((height * 8, 128), F32),) * 2,
-        in_specs=[SMEM, VMEM, HBM],
-        out_specs=(HBM, HBM),
+        out_shape=(jax.ShapeDtypeStruct((height * 8, 128), F32),) * 2
+        + (jax.ShapeDtypeStruct((1,), jnp.int32),),
+        in_specs=[SMEM] + [VMEM] * 3,
+        out_specs=(HBM, HBM, SMEM),
         scratch_shapes=[
-            pltpu.VMEM((height, 5, 8, 128), F32),
             pltpu.VMEM((height * 8, 128), F32),
             pltpu.VMEM((height * 8, 128), F32),
-            pltpu.SemaphoreType.DMA((3, height // PIECE)),
+            pltpu.SemaphoreType.DMA((2, height // PIECE)),
         ],
         compiler_params=params(16),
-    )(where, ports, kept)
-
-
-def gathered(rows):
-    rows = jnp.concatenate([rows, lax.ppermute(rows, "gz", [(i, i ^ 1) for i in range(8)])], 0)
+    )(where, loads, ports, kept)
+
+
+def swapped(rows):
+    return jnp.concatenate([rows, lax.ppermute(rows, "gz", [(i, i ^ 1) for i in range(8)])], 0)
+
+
+def spread(rows):
     above = [
         lax.ppermute(rows, "gz", [(i, (i - 2 * steps) % 8) for i in range(8)]) for steps in (1, 2, 3)
     ]
     return jnp.concatenate([rows] + above, 0)
+
+
+def gathered(rows):
+    return spread(swapped(rows))
 
 
 def tiles_of(field):
@@ -642,17 +670,17 @@
     matrix = gathered(matrix)
     sums, flag = sum_records(matrix, got.reshape(16 * SLOTS, 128))
     sums = lax.all_to_all(sums.reshape(16, 64, 128), "col", 0, 0, tiled=True).reshape(128, 8, 128)
-    loads = gathered(load_blocks(where, flag, sums, base, weight))
-    kept, ports, crowded = second_step(where, matrix, loads, sums, *fields)
-    ports = gathered(ports)
-
-    def quick(_):
-        return tuple(field_of(x, height, width) for x in finish(where, ports, kept))
-
-    def general(operands):
-        return general_path(*operands)
-
-    return lax.cond(crowded[0] > 0, general, quick, arguments)
+    loads = swapped(load_blocks(where, flag, sums, base, weight))
+    cells = middle(loads, where, sums, *fields)
+    loads = spread(loads)
+    kept, ports = second_step(where, matrix, loads, cells)
+    flux, temp, crowded = finish(where, loads, gathered(ports), kept)
+
+    def again(state):
+        return general_path(*arguments) + (jnp.zeros_like(state[2]),)
+
+    flux, temp = field_of(flux, height, width), field_of(temp, height, width)
+    return lax.while_loop(lambda state: state[2][0] > 0, again, (flux, temp, crowded))[:2]
 
 
 def solution(mesh):

time: 83.9 us -> 81 us (0.965)
  waiting for transfers between devices: 34.6 us -> 32.5 us
    ppermute x12, waiting for transfers between devices: 13.6 us -> 11.5 us  [the longest x9 8.96 us: spread(): lax.ppermute(rows, 'gz', [(i, (i - 2 * steps) % 8) for i in range(8)])]
    pallas_call x1 -> x2, Pallas kernels: 4.45 us -> 4 us  [the longest x1 2.43 us: middle(): pl.pallas_call(middle_kernel, out_shape=tile(height, 10), in_specs=[ANY,...]
  transfers between devices with their start and end apart: 14 -> 14, of which waited for: 11 -> 12; matrix products, arithmetic and copies ran while one was open for 0% -> 0% of each run, Pallas kernels for 3% -> 6%
where the time goes in v3:
time: 81 us; the launch traced here: 80.5 us
  waiting for transfers between devices  32.5 us (40%)
  starting transfers between devices  28.5 us (35%)
  Pallas kernels  17.5 us (22%)
  between operations  0.98 us (1%)
    all_to_all x1, waiting for transfers between devices, shards(): got = lax.all_to_all(sent.reshape(16, SLOTS, 128), 'col', 0, 0, tiled=True)  11 us
    all_to_all x1, waiting for transfers between devices, shards(): lax.all_to_all(sums.reshape(16, 64, 128), 'col', 0, 0, tiled=True)  10 us
    ppermute x9, starting transfers between devices, spread(): lax.ppermute(rows, 'gz', [(i, (i - 2 * steps) % 8) for i in range(8)])  9.82 us
    ppermute x9, waiting for transfers between devices, spread(): lax.ppermute(rows, 'gz', [(i, (i - 2 * steps) % 8) for i in range(8)])  8.96 us
    all_to_all x1, starting transfers between devices, shards(): got = lax.all_to_all(sent.reshape(16, SLOTS, 128), 'col', 0, 0, tiled=True)  8.57 us
    ppermute x3, starting transfers between devices, swapped(): lax.ppermute(rows, 'gz', [(i, i ^ 1) for i in range(8)])  5.4 us
    pallas_call x1, Pallas kernels, pack(): pl.pallas_call(pack_kernel, out_shape=jax.ShapeDtypeStruct((16 * SLOTS, 1...  4.79 us
    all_to_all x1, starting transfers between devices, shards(): lax.all_to_all(sums.reshape(16, 64, 128), 'col', 0, 0, tiled=True)  4.7 us
  transfers between devices with their start and end apart: 14, of which 12 were waited for; matrix products, arithmetic and copies ran while one was open for 0% of the time, Pallas kernels for 6%

profile of v3, /device:TPU:1, one launch (start us, length us, event | category | flops | bytes accessed | tf_op | source)
XLA Modules:
  0.0 80.5 jit_solution(1200411451378034133)
XLA Ops:
  0.6 4.8 %shard_map.95.after_ref = f32[3072,128]{1,0:T(8,128)} custom-call(s32[16,128]{1,0:T(8,128)} %bitcast.317, s32[16,128]{1,0:T(8,128)} %bitcast.378, f32[2048,128]{1,0:T(8,128)} %bitcast.311), custom_call_target="tpu_custom_call" | custom-call | tf_op jit(solution)/shard_map/pallas_call | solution.py:298
  5.4 8.6 %all-to-all-start.2 = ((f32[16,192,128]{2,1,0:T(8,128)}), f32[16,192,128]{2,1,0:T(8,128)S(1)}, u32[]{:S(2)}, u32[]{:S(2)}) async-start(f32[16,192,128]{2,1,0:T(8,128)} %bitcast.107), calls=%async_computation.2 | async-start | bytes 3145728 | tf_op jit(solution)/shard_map/all_to_all | solution.py:667
  14.0 2.3 %shard_map.96 = (f32[128,2,8,128]{3,2,1,0:T(8,128)S(1)}, f32[4,8,128]{2,1,0:T(8,128)S(1)}, f32[2,8,128]{2,1,0:T(8,128)S(1)}) custom-call(f32[3072,128]{1,0:T(8,128)} %shard_map.95.after_ref, f32[1024,128]{1,0:T(8,128)} %bitcast.308, f32[1024,128]{1,0:T(8,128)} %bitcast.302, f32[1024,128]{1,0:T(8,128)} %bitcast.304, f32[1024,128]{1,0:T(8,128)S(1)} %bitcast.300, ...), custom_call_target="tpu_custom_call" | custom-call | tf_op jit(solution)/shard_map/pallas_call | solution.py:401
  16.4 1.0 %collective-permute-start.21 = (f32[4,8,128]{2,1,0:T(8,128)S(1)}, f32[4,8,128]{2,1,0:T(8,128)S(1)}, u32[]{:S(2)}, u32[]{:S(2)}) collective-permute-start(f32[4,8,128]{2,1,0:T(8,128)S(1)} %get-tuple-element.67), channel_id=1, source_target_pairs={{0,1},{1,0},{2,3},{3,2},{4,5},{5,4},{6,7},{7,6},{8,9},{9,8},{10,11... | collective-permute-start | bytes 49160 | tf_op jit(solution)/shard_map/ppermute | solution.py:621
  17.4 0.8 %collective-permute-done.21 = f32[4,8,128]{2,1,0:T(8,128)S(1)} collective-permute-done((f32[4,8,128]{2,1,0:T(8,128)S(1)}, f32[4,8,128]{2,1,0:T(8,128)S(1)}, u32[]{:S(2)}, u32[]{:S(2)}) %collective-permute-start.21) | collective-permute-done | bytes 16416 | tf_op jit(solution)/shard_map/ppermute | solution.py:621
  18.3 2.7 %collective-permute-start.22 = (f32[8,8,128]{2,1,0:T(8,128)S(1)}, f32[8,8,128]{2,1,0:T(8,128)S(1)}, u32[]{:S(2)}, u32[]{:S(2)}) collective-permute-start(f32[8,8,128]{2,1,0:T(8,128)S(1)} %get-tuple-element.317), channel_id=1, source_target_pairs={{0,6},{1,7},{2,0},{3,1},{4,2},{5,3},{6,4},{7,5},{8,14},{9,15},{10,... | collective-permute-start | bytes 98312 | tf_op jit(solution)/shard_map/ppermute | solution.py:626
  22.0 3.5 %collective-permute-done.23 = f32[8,8,128]{2,1,0:T(8,128)S(1)} collective-permute-done((f32[8,8,128]{2,1,0:T(8,128)S(1)}, f32[8,8,128]{2,1,0:T(8,128)S(1)}, u32[]{:S(2)}, u32[]{:S(2)}) %collective-permute-start.23) | collective-permute-done | bytes 32800 | tf_op jit(solution)/shard_map/ppermute | solution.py:626
  25.9 11.0 %all-to-all-done.2 = f32[16,192,128]{2,1,0:T(8,128)S(1)} async-done(((f32[16,192,128]{2,1,0:T(8,128)}), f32[16,192,128]{2,1,0:T(8,128)S(1)}, u32[]{:S(2)}, u32[]{:S(2)}) %all-to-all-start.2) | async-done | bytes 1572896 | tf_op jit(solution)/shard_map/all_to_all | solution.py:667
  36.9 2.7 %shard_map.97 = (f32[1024,128]{1,0:T(8,128)}, f32[1,8,128]{2,1,0:T(8,128)S(1)}) custom-call(f32[32,8,128]{2,1,0:T(8,128)S(1)} %constant_dynamic-update-slice_fusion.2.after_ref.matrix_ref, f32[3072,128]{1,0:T(8,128)S(1)} %bitcast.297), custom_call_target="tpu_custom_call" | custom-call | tf_op jit(solution)/shard_map/pallas_call | solution.py:352
  39.6 4.7 %all-to-all-start.3 = ((f32[16,64,128]{2,1,0:T(8,128)}), f32[16,64,128]{2,1,0:T(8,128)S(1)}, u32[]{:S(2)}, u32[]{:S(2)}) async-start(f32[16,64,128]{2,1,0:T(8,128)} %bitcast.109), calls=%async_computation.3 | async-start | bytes 1048576 | tf_op jit(solution)/shard_map/all_to_all | solution.py:672
  44.3 10.0 %all-to-all-done.3 = f32[16,64,128]{2,1,0:T(8,128)S(1)} async-done(((f32[16,64,128]{2,1,0:T(8,128)}), f32[16,64,128]{2,1,0:T(8,128)S(1)}, u32[]{:S(2)}, u32[]{:S(2)}) %all-to-all-start.3) | async-done | bytes 524320 | tf_op jit(solution)/shard_map/all_to_all | solution.py:672
  54.4 1.4 %shard_map.98 = f32[3,8,128]{2,1,0:T(8,128)S(1)} custom-call(s32[2]{0:T(128)S(1)} %pad_add_fusion.1.where_ref, f32[1,8,128]{2,1,0:T(8,128)S(1)} %get-tuple-element.68.flag_ref, f32[128,8,128]{2,1,0:T(8,128)S(1)} %bitcast.298, f32[2,8,128]{2,1,0:T(8,128)S(1)} %get-tuple-element.70.base_ref, f32[128,2,8,128]{3,2,1,0:T(8,128)S(1)} %get-tuple-element.71.weight_ref), custom_call_target="tpu_custom_call" | custom-call | tf_op jit(solution)/shard_map/pallas_call | solution.py:438
  55.8 2.4 %collective-permute-start.25 = (f32[3,8,128]{2,1,0:T(8,128)S(1)}, f32[3,8,128]{2,1,0:T(8,128)S(1)}, u32[]{:S(2)}, u32[]{:S(2)}) collective-permute-start(f32[3,8,128]{2,1,0:T(8,128)S(1)} %shard_map.98), channel_id=1, source_target_pairs={{0,1},{1,0},{2,3},{3,2},{4,5},{5,4},{6,7},{7,6},{8,9},{9,8},{10,11... | collective-permute-start | bytes 36872 | tf_op jit(solution)/shard_map/ppermute | solution.py:621
  58.3 0.8 %collective-permute-done.25 = f32[3,8,128]{2,1,0:T(8,128)S(1)} collective-permute-done((f32[3,8,128]{2,1,0:T(8,128)S(1)}, f32[3,8,128]{2,1,0:T(8,128)S(1)}, u32[]{:S(2)}, u32[]{:S(2)}) %collective-permute-start.25) | collective-permute-done | bytes 12320 | tf_op jit(solution)/shard_map/ppermute | solution.py:621
  59.1 2.7 %collective-permute-start.26 = (f32[6,8,128]{2,1,0:T(8,128)S(1)}, f32[6,8,128]{2,1,0:T(8,128)S(1)}, u32[]{:S(2)}, u32[]{:S(2)}) collective-permute-start(f32[6,8,128]{2,1,0:T(8,128)S(1)} %pad_maximum_fusion.14.after_ref), channel_id=1, source_target_pairs={{0,6},{1,7},{2,0},{3,1},{4,2},{5,3},{6,4},{7,5},{8,14},{9,15},{10,... | collective-permute-start | bytes 73736 | tf_op jit(solution)/shard_map/ppermute | solution.py:626
  62.9 2.4 %shard_map.99.middle_ref = f32[128,10,8,128]{3,2,1,0:T(8,128)S(1)} custom-call(f32[6,8,128]{2,1,0:T(8,128)S(1)} %pad_maximum_fusion.14.after_ref, s32[2]{0:T(128)S(1)} %pad_add_fusion.1.where_ref, f32[128,8,128]{2,1,0:T(8,128)S(1)} %bitcast.299, f32[1024,128]{1,0:T(8,128)} %bitcast.309, f32[1024,128]{1,0:T(8,128)S(1)} %bitcast.303, f32[1024,128]{1,0:T(8,128)} %bitcast.305, ...), custom_call_target="tpu_custom_call" | custom-call | tf_op jit(solution)/shard_map/pallas_call | solution.py:508
  66.3 1.6 %shard_map.100 = (f32[128,5,8,128]{3,2,1,0:T(8,128)S(1)}, f32[6,8,128]{2,1,0:T(8,128)S(1)}) custom-call(s32[2]{0:T(128)S(1)} %pad_add_fusion.1.where_ref, f32[32,8,128]{2,1,0:T(8,128)S(1)} %constant_dynamic-update-slice_fusion.2.after_ref.matrix_ref, f32[24,8,128]{2,1,0:T(8,128)S(1)} %constant_dynamic-update-slice_fusion.7.loads_ref, ...), custom_call_target="tpu_custom_call" | custom-call | tf_op jit(solution)/shard_map/pallas_call | solution.py:558
  67.9 1.9 %collective-permute-start.29 = (f32[6,8,128]{2,1,0:T(8,128)S(1)}, f32[6,8,128]{2,1,0:T(8,128)S(1)}, u32[]{:S(2)}, u32[]{:S(2)}) collective-permute-start(f32[6,8,128]{2,1,0:T(8,128)S(1)} %get-tuple-element.72), channel_id=1, source_target_pairs={{0,1},{1,0},{2,3},{3,2},{4,5},{5,4},{6,7},{7,6},{8,9},{9,8},{10,11... | collective-permute-start | bytes 73736 | tf_op jit(solution)/shard_map/ppermute | solution.py:621
  69.8 0.8 %collective-permute-done.29 = f32[6,8,128]{2,1,0:T(8,128)S(1)} collective-permute-done((f32[6,8,128]{2,1,0:T(8,128)S(1)}, f32[6,8,128]{2,1,0:T(8,128)S(1)}, u32[]{:S(2)}, u32[]{:S(2)}) %collective-permute-start.29) | collective-permute-done | bytes 24608 | tf_op jit(solution)/shard_map/ppermute | solution.py:621
  71.1 1.4 %collective-permute-start.31 = (f32[12,8,128]{2,1,0:T(8,128)S(1)}, f32[12,8,128]{2,1,0:T(8,128)S(1)}, u32[]{:S(2)}, u32[]{:S(2)}) collective-permute-start(f32[12,8,128]{2,1,0:T(8,128)S(1)} %get-tuple-element.313), channel_id=1, source_target_pairs={{0,4},{1,5},{2,6},{3,7},{4,0},{5,1},{6,2},{7,3},{8,12},{9,13},{10,... | collective-permute-start | bytes 147464 | tf_op jit(solution)/shard_map/ppermute | solution.py:626
  73.7 1.9 %collective-permute-done.31 = f32[12,8,128]{2,1,0:T(8,128)S(1)} collective-permute-done((f32[12,8,128]{2,1,0:T(8,128)S(1)}, f32[12,8,128]{2,1,0:T(8,128)S(1)}, u32[]{:S(2)}, u32[]{:S(2)}) %collective-permute-start.31) | collective-permute-done | bytes 49184 | tf_op jit(solution)/shard_map/ppermute | solution.py:626
  75.5 1.6 %collective-permute-done.32 = f32[12,8,128]{2,1,0:T(8,128)S(1)} collective-permute-done((f32[12,8,128]{2,1,0:T(8,128)S(1)}, f32[12,8,128]{2,1,0:T(8,128)S(1)}, u32[]{:S(2)}, u32[]{:S(2)}) %collective-permute-start.32) | collective-permute-done | bytes 49184 | tf_op jit(solution)/shard_map/ppermute | solution.py:626
  77.2 2.3 %shard_map.101 = (f32[1024,128]{1,0:T(8,128)}, f32[1024,128]{1,0:T(8,128)}, s32[1]{0:T(128)}) custom-call(s32[2]{0:T(128)S(1)} %pad_add_fusion.1.where_ref, f32[24,8,128]{2,1,0:T(8,128)S(1)} %constant_dynamic-update-slice_fusion.7.loads_ref, f32[48,8,128]{2,1,0:T(8,128)S(1)} %constant_dynamic-update-slice_fusion.14.ports_ref, ...), custom_call_target="tpu_custom_call" | custom-call | tf_op jit(solution)/shard_map/pallas_call | solution.py:605
  79.5 0.8 while.11
  (43 shorter events, 5.1 us)
Async XLA Ops:
  5.4 8.6 %copy-start = (f32[128,1024]{1,0:T(8,128)S(1)}, f32[128,1024]{1,0:T(8,128)}, u32[]{:S(2)}) copy-start(f32[128,1024]{1,0:T(8,128)} %param.13) | copy-start | bytes 1572868
  5.4 31.5 %all-to-all-start.2 = ((f32[16,192,128]{2,1,0:T(8,128)}), f32[16,192,128]{2,1,0:T(8,128)S(1)}, u32[]{:S(2)}, u32[]{:S(2)}) async-start(f32[16,192,128]{2,1,0:T(8,128)} %bitcast.107), calls=%async_computation.2 | async-start | bytes 3145728 | tf_op jit(solution)/shard_map/all_to_all | solution.py:667
  16.4 1.9 %collective-permute-start.21 = (f32[4,8,128]{2,1,0:T(8,128)S(1)}, f32[4,8,128]{2,1,0:T(8,128)S(1)}, u32[]{:S(2)}, u32[]{:S(2)}) collective-permute-start(f32[4,8,128]{2,1,0:T(8,128)S(1)} %get-tuple-element.67), channel_id=1, source_target_pairs={{0,1},{1,0},{2,3},{3,2},{4,5},{5,4},{6,7},{7,6},{8,9},{9,8},{10,11... | collective-permute-start | bytes 49160 | tf_op jit(solution)/shard_map/ppermute | solution.py:621
  18.3 3.8 %collective-permute-start.22 = (f32[8,8,128]{2,1,0:T(8,128)S(1)}, f32[8,8,128]{2,1,0:T(8,128)S(1)}, u32[]{:S(2)}, u32[]{:S(2)}) collective-permute-start(f32[8,8,128]{2,1,0:T(8,128)S(1)} %get-tuple-element.317), channel_id=1, source_target_pairs={{0,6},{1,7},{2,0},{3,1},{4,2},{5,3},{6,4},{7,5},{8,14},{9,15},{10,... | collective-permute-start | bytes 98312 | tf_op jit(solution)/shard_map/ppermute | solution.py:626
  21.0 4.6 %collective-permute-start.23 = (f32[8,8,128]{2,1,0:T(8,128)S(1)}, f32[8,8,128]{2,1,0:T(8,128)S(1)}, u32[]{:S(2)}, u32[]{:S(2)}) collective-permute-start(f32[8,8,128]{2,1,0:T(8,128)S(1)} %get-tuple-element.317), channel_id=1, source_target_pairs={{0,4},{1,5},{2,6},{3,7},{4,0},{5,1},{6,2},{7,3},{8,12},{9,13},{10,... | collective-permute-start | bytes 98312 | tf_op jit(solution)/shard_map/ppermute | solution.py:626
  21.3 4.6 %collective-permute-start.24 = (f32[8,8,128]{2,1,0:T(8,128)S(1)}, f32[8,8,128]{2,1,0:T(8,128)S(1)}, u32[]{:S(2)}, u32[]{:S(2)}) collective-permute-start(f32[8,8,128]{2,1,0:T(8,128)S(1)} %get-tuple-element.317), channel_id=1, source_target_pairs={{0,2},{1,3},{2,4},{3,5},{4,6},{5,7},{6,0},{7,1},{8,10},{9,11},{10,... | collective-permute-start | bytes 98312 | tf_op jit(solution)/shard_map/ppermute | solution.py:626
  39.6 23.3 %copy-start.1 = (f32[128,1024]{1,0:T(8,128)S(1)}, f32[128,1024]{1,0:T(8,128)}, u32[]{:S(2)}) copy-start(f32[128,1024]{1,0:T(8,128)} %param.11) | copy-start | bytes 1572868
  39.6 14.8 %all-to-all-start.3 = ((f32[16,64,128]{2,1,0:T(8,128)}), f32[16,64,128]{2,1,0:T(8,128)S(1)}, u32[]{:S(2)}, u32[]{:S(2)}) async-start(f32[16,64,128]{2,1,0:T(8,128)} %bitcast.109), calls=%async_computation.3 | async-start | bytes 1048576 | tf_op jit(solution)/shard_map/all_to_all | solution.py:672
  55.8 3.3 %collective-permute-start.25 = (f32[3,8,128]{2,1,0:T(8,128)S(1)}, f32[3,8,128]{2,1,0:T(8,128)S(1)}, u32[]{:S(2)}, u32[]{:S(2)}) collective-permute-start(f32[3,8,128]{2,1,0:T(8,128)S(1)} %shard_map.98), channel_id=1, source_target_pairs={{0,1},{1,0},{2,3},{3,2},{4,5},{5,4},{6,7},{7,6},{8,9},{9,8},{10,11... | collective-permute-start | bytes 36872 | tf_op jit(solution)/shard_map/ppermute | solution.py:621
  59.1 6.2 %collective-permute-start.26 = (f32[6,8,128]{2,1,0:T(8,128)S(1)}, f32[6,8,128]{2,1,0:T(8,128)S(1)}, u32[]{:S(2)}, u32[]{:S(2)}) collective-permute-start(f32[6,8,128]{2,1,0:T(8,128)S(1)} %pad_maximum_fusion.14.after_ref), channel_id=1, source_target_pairs={{0,6},{1,7},{2,0},{3,1},{4,2},{5,3},{6,4},{7,5},{8,14},{9,15},{10,... | collective-permute-start | bytes 73736 | tf_op jit(solution)/shard_map/ppermute | solution.py:626
  61.9 4.2 %collective-permute-start.27 = (f32[6,8,128]{2,1,0:T(8,128)S(1)}, f32[6,8,128]{2,1,0:T(8,128)S(1)}, u32[]{:S(2)}, u32[]{:S(2)}) collective-permute-start(f32[6,8,128]{2,1,0:T(8,128)S(1)} %pad_maximum_fusion.14.after_ref), channel_id=1, source_target_pairs={{0,4},{1,5},{2,6},{3,7},{4,0},{5,1},{6,2},{7,3},{8,12},{9,13},{10,... | collective-permute-start | bytes 73736 | tf_op jit(solution)/shard_map/ppermute | solution.py:626
  62.2 4.1 %collective-permute-start.28 = (f32[6,8,128]{2,1,0:T(8,128)S(1)}, f32[6,8,128]{2,1,0:T(8,128)S(1)}, u32[]{:S(2)}, u32[]{:S(2)}) collective-permute-start(f32[6,8,128]{2,1,0:T(8,128)S(1)} %pad_maximum_fusion.14.after_ref), channel_id=1, source_target_pairs={{0,2},{1,3},{2,4},{3,5},{4,6},{5,7},{6,0},{7,1},{8,10},{9,11},{10,... | collective-permute-start | bytes 73736 | tf_op jit(solution)/shard_map/ppermute | solution.py:626
  67.9 2.8 %collective-permute-start.29 = (f32[6,8,128]{2,1,0:T(8,128)S(1)}, f32[6,8,128]{2,1,0:T(8,128)S(1)}, u32[]{:S(2)}, u32[]{:S(2)}) collective-permute-start(f32[6,8,128]{2,1,0:T(8,128)S(1)} %get-tuple-element.72), channel_id=1, source_target_pairs={{0,1},{1,0},{2,3},{3,2},{4,5},{5,4},{6,7},{7,6},{8,9},{9,8},{10,11... | collective-permute-start | bytes 73736 | tf_op jit(solution)/shard_map/ppermute | solution.py:621
  70.7 2.9 %collective-permute-start.30 = (f32[12,8,128]{2,1,0:T(8,128)S(1)}, f32[12,8,128]{2,1,0:T(8,128)S(1)}, u32[]{:S(2)}, u32[]{:S(2)}) collective-permute-start(f32[12,8,128]{2,1,0:T(8,128)S(1)} %get-tuple-element.313), channel_id=1, source_target_pairs={{0,6},{1,7},{2,0},{3,1},{4,2},{5,3},{6,4},{7,5},{8,14},{9,15},{10,... | collective-permute-start | bytes 147464 | tf_op jit(solution)/shard_map/ppermute | solution.py:626
  71.1 4.4 %collective-permute-start.31 = (f32[12,8,128]{2,1,0:T(8,128)S(1)}, f32[12,8,128]{2,1,0:T(8,128)S(1)}, u32[]{:S(2)}, u32[]{:S(2)}) collective-permute-start(f32[12,8,128]{2,1,0:T(8,128)S(1)} %get-tuple-element.313), channel_id=1, source_target_pairs={{0,4},{1,5},{2,6},{3,7},{4,0},{5,1},{6,2},{7,3},{8,12},{9,13},{10,... | collective-permute-start | bytes 147464 | tf_op jit(solution)/shard_map/ppermute | solution.py:626
  72.5 4.6 %collective-permute-start.32 = (f32[12,8,128]{2,1,0:T(8,128)S(1)}, f32[12,8,128]{2,1,0:T(8,128)S(1)}, u32[]{:S(2)}, u32[]{:S(2)}) collective-permute-start(f32[12,8,128]{2,1,0:T(8,128)S(1)} %get-tuple-element.313), channel_id=1, source_target_pairs={{0,2},{1,3},{2,4},{3,5},{4,6},{5,7},{6,0},{7,1},{8,10},{9,11},{10,... | collective-permute-start | bytes 147464 | tf_op jit(solution)/shard_map/ppermute | solution.py:626
  73.6 5.8 %copy-start.2 = (f32[128,1024]{1,0:T(8,128)S(1)}, f32[128,1024]{1,0:T(8,128)}, u32[]{:S(2)}) copy-start(f32[128,1024]{1,0:T(8,128)} %param.12) | copy-start | bytes 1572868
  73.6 5.8 %copy-start.3 = (f32[128,1024]{1,0:T(8,128)S(1)}, f32[128,1024]{1,0:T(8,128)}, u32[]{:S(2)}) copy-start(f32[128,1024]{1,0:T(8,128)} %param.14) | copy-start | bytes 1572868
  73.6 5.8 %copy-start.4 = (f32[128,1024]{1,0:T(8,128)S(1)}, f32[128,1024]{1,0:T(8,128)}, u32[]{:S(2)}) copy-start(f32[128,1024]{1,0:T(8,128)} %param.10) | copy-start | bytes 1572868
  73.6 5.8 %copy-start.19 = (s32[1,2048,1]{1,2,0:T(1,128)S(1)}, s32[1,2048,1]{1,2,0:T(1,128)}, u32[]{:S(2)}) copy-start(s32[1,2048,1]{1,2,0:T(1,128)} %param.16) | copy-start | bytes 24580
  73.6 5.8 %copy-start.20 = (s32[1,2048]{1,0:T(1,128)S(1)}, s32[1,2048]{1,0:T(1,128)}, u32[]{:S(2)}) copy-start(s32[1,2048]{1,0:T(1,128)} %param.17) | copy-start | bytes 24580

commit v4 on v3

--- a/solution.py
+++ b/solution.py
@@ -208,7 +208,7 @@
 
 SLOTS = 192
 ROOM = 190
-PIECE = 32
+PIECE = 16
 F32 = jnp.float32
 BF16 = jnp.bfloat16
 VMEM = pl.BlockSpec(memory_space=pltpu.VMEM)
@@ -311,7 +311,7 @@
     )(owner, cell, heat)
 
 
-def sum_kernel(after_ref, got_ref, out_ref, flag_ref, terms):
+def sum_kernel(after_ref, got_ref, out_hbm, flag_ref, terms, out_ref, sems):
     flag = jnp.zeros((1, 128), F32)
     for s in range(16):
         heat = got_ref[s * SLOTS : (s + 1) * SLOTS, :]
@@ -338,6 +338,7 @@
         ]
     names = jnp.concatenate(names, 1)
     row = lax.broadcasted_iota(jnp.int32, (128, 128), 0).astype(F32).astype(BF16)
+    leaving = pieces(out_ref, out_hbm, sems, 128)
 
     for block in range(8):
         near = (names - block * 128.0).astype(BF16)
@@ -346,6 +347,9 @@
         ]
         both = jnp.dot(jnp.concatenate(hits, 1), terms[...], preferred_element_type=F32)
         out_ref[block * 128 : (block + 1) * 128, :] = both[:, :128] + both[:, 128:]
+        leaving[block].start()
+    for copy in leaving:
+        copy.wait()
 
 
 def sum_records(after, got):
@@ -353,8 +357,12 @@
         sum_kernel,
         out_shape=(jax.ShapeDtypeStruct((1024, 128), F32), tile(1)),
         in_specs=[ANY, VMEM],
-        out_specs=(VMEM, VMEM),
-        scratch_shapes=[pltpu.VMEM((16 * SLOTS, 256), BF16)],
+        out_specs=(HBM, VMEM),
+        scratch_shapes=[
+            pltpu.VMEM((16 * SLOTS, 256), BF16),
+            pltpu.VMEM((1024, 128), F32),
+            pltpu.SemaphoreType.DMA((8,)),
+        ],
         compiler_params=params(24),
     )(after, got)
 
@@ -427,7 +435,9 @@
         return tuple(totals)
 
     zero = jnp.zeros((8, 128), F32)
-    totals = lax.fori_loop(0, height // 8, body, (zero,) * 8)
+    totals = (zero,) * 8
+    for group in range(height // 8):
+        totals = body(group, totals)
     for i in range(2):
         a, b, c, d = totals[4 * i : 4 * i + 4]
         port_out[i] = base_ref[i] - ((a + b) + (c + d))
@@ -446,7 +456,10 @@
 
 def slot_of(me, block):
     steps = (lax.shift_right_logical(block, 1) - lax.shift_right_logical(me, 1)) & 3
-    return steps * 2 + ((me ^ block) & 1)
+    other = (me ^ block) & 1
+    core = me & 1
+    odd = jnp.where(lax.shift_right_logical(steps, 1) == core, 2 + other, 7 - other)
+    return jnp.where((steps & 1) == 1, odd, steps * 2 + other)
 
 
 def block_ends(where_ref, port_of):
@@ -500,7 +513,9 @@
         return one, one_flow, two, two_flow, load, load_flow
 
     zero = jnp.zeros((8, 128), F32)
-    lax.fori_loop(0, height // 8, body, (zero + 1.0, zero, zero, zero + 1.0, zero, zero))
+    carry = (zero + 1.0, zero, zero, zero + 1.0, zero, zero)
+    for group in range(height // 8):
+        carry = body(group, carry)
 
 
 def middle(after, where, sums, *fields):
@@ -546,9 +561,10 @@
         return one, one_flow, two, two_flow, load, load_flow
 
     zero = jnp.zeros((8, 128), F32)
-    one, one_flow, two, two_flow, load, load_flow = lax.fori_loop(
-        0, height // 8, body, (zero + 1.0, zero, zero, zero + 1.0, zero, zero)
-    )
+    carry = (zero + 1.0, zero, zero, zero + 1.0, zero, zero)
+    for group in range(height // 8):
+        carry = body(group, carry)
+    one, one_flow, two, two_flow, load, load_flow = carry
     port_out[0], port_out[1], port_out[2], port_out[3] = one, two, one_flow, two_flow
     port_out[4], port_out[5] = load, load_flow
 
@@ -578,21 +594,21 @@
 
     value, flow = block_ends(where_ref, port_of)
 
-    def body(group, carry):
+    def body(group):
         for sub in range(8):
             h = group * 8 + sub
             at = pl.ds(group * 64 + sub, 8, stride=8)
             light = kept_ref[h, 0] * value + kept_ref[h, 1] * flow + kept_ref[h, 2]
             flux_ref[at, :] = light
             temp_ref[at, :] = kept_ref[h, 4] + kept_ref[h, 3] * light
-        return carry
 
     leaving = [
         pieces(flux_ref, flux_hbm, sems.at[0], PIECE * 8),
         pieces(temp_ref, temp_hbm, sems.at[1], PIECE * 8),
     ]
     for k in range(height // PIECE):
-        lax.fori_loop(k * PIECE // 8, (k + 1) * PIECE // 8, body, 0)
+        for group in range(k * PIECE // 8, (k + 1) * PIECE // 8):
+            body(group)
         for part in leaving:
             part[k].start()
     for part in leaving:
@@ -622,10 +638,10 @@
 
 
 def spread(rows):
-    above = [
-        lax.ppermute(rows, "gz", [(i, (i - 2 * steps) % 8) for i in range(8)]) for steps in (1, 2, 3)
-    ]
-    return jnp.concatenate([rows] + above, 0)
+    across = lax.ppermute(rows, "gz", [(i, (i + 4) % 8) for i in range(8)])
+    beside = lax.ppermute(rows, "gz", [(i, (i - 2 + 4 * (i % 2)) % 8) for i in range(8)])
+    passed = lax.ppermute(beside, "gz", [(i, i ^ 1) for i in range(8)])
+    return jnp.concatenate([rows, beside, across, passed], 0)
 
 
 def gathered(rows):

time: 81 us -> 79 us (0.975)
  Pallas kernels: 17.5 us -> 16.2 us
    ppermute x9, waiting for transfers between devices: 8.96 us -> 6.45 us  [the longest x3 3.3 us: spread(): lax.ppermute(rows, 'gz', [(i, (i - 2 + 4 * (i % 2)) % 8) for i in range(8)])]
    all_to_all x1, waiting for transfers between devices: 11 us -> 12.8 us  [shards(): got = lax.all_to_all(sent.reshape(16, SLOTS, 128), 'col', 0, 0, tiled=True)]
  transfers between devices with their start and end apart: 14 -> 14, of which waited for: 12 -> 10; matrix products, arithmetic and copies ran while one was open for 0% -> 0% of each run, Pallas kernels for 6% -> 6%
where the time goes in v4:
time: 79 us; the launch traced here: 78.6 us
  waiting for transfers between devices  31.8 us (40%)
  starting transfers between devices  28.6 us (36%)
  Pallas kernels  16.2 us (21%)
  between operations  1.01 us (1%)
  loops' own time  0.8 us (1%)
    all_to_all x1, waiting for transfers between devices, shards(): got = lax.all_to_all(sent.reshape(16, SLOTS, 128), 'col', 0, 0, tiled=True)  12.8 us
    all_to_all x1, waiting for transfers between devices, shards(): lax.all_to_all(sums.reshape(16, 64, 128), 'col', 0, 0, tiled=True)  10 us
    all_to_all x1, starting transfers between devices, shards(): got = lax.all_to_all(sent.reshape(16, SLOTS, 128), 'col', 0, 0, tiled=True)  8.57 us
    ppermute x3, starting transfers between devices, spread(): across = lax.ppermute(rows, 'gz', [(i, (i + 4) % 8) for i in range(8)])  7.03 us
    ppermute x3, starting transfers between devices, swapped(): lax.ppermute(rows, 'gz', [(i, i ^ 1) for i in range(8)])  4.93 us
    pallas_call x1, Pallas kernels, pack(): pl.pallas_call(pack_kernel, out_shape=jax.ShapeDtypeStruct((16 * SLOTS, 1...  4.79 us
    all_to_all x1, starting transfers between devices, shards(): lax.all_to_all(sums.reshape(16, 64, 128), 'col', 0, 0, tiled=True)  4.71 us
    ppermute x3, waiting for transfers between devices, spread(): lax.ppermute(rows, 'gz', [(i, (i - 2 + 4 * (i % 2)) % 8) for i in range(8)])  3.3 us
  transfers between devices with their start and end apart: 14, of which 10 were waited for; matrix products, arithmetic and copies ran while one was open for 0% of the time, Pallas kernels for 6%

profile of v4, /device:TPU:1, one launch (start us, length us, event | category | flops | bytes accessed | tf_op | source)
XLA Modules:
  0.0 78.6 jit_solution(3389507376650674966)
XLA Ops:
  0.6 4.8 %shard_map.95.after_ref = f32[3072,128]{1,0:T(8,128)} custom-call(s32[16,128]{1,0:T(8,128)} %bitcast.317, s32[16,128]{1,0:T(8,128)} %bitcast.378, f32[2048,128]{1,0:T(8,128)} %bitcast.311), custom_call_target="tpu_custom_call" | custom-call | tf_op jit(solution)/shard_map/pallas_call | solution.py:298
  5.4 8.6 %all-to-all-start.2 = ((f32[16,192,128]{2,1,0:T(8,128)}), f32[16,192,128]{2,1,0:T(8,128)S(1)}, u32[]{:S(2)}, u32[]{:S(2)}) async-start(f32[16,192,128]{2,1,0:T(8,128)} %bitcast.107), calls=%async_computation.2 | async-start | bytes 3145728 | tf_op jit(solution)/shard_map/all_to_all | solution.py:683
  14.0 2.3 %shard_map.96 = (f32[128,2,8,128]{3,2,1,0:T(8,128)S(1)}, f32[4,8,128]{2,1,0:T(8,128)S(1)}, f32[2,8,128]{2,1,0:T(8,128)S(1)}) custom-call(f32[3072,128]{1,0:T(8,128)} %shard_map.95.after_ref, f32[1024,128]{1,0:T(8,128)} %bitcast.308, f32[1024,128]{1,0:T(8,128)} %bitcast.302, f32[1024,128]{1,0:T(8,128)} %bitcast.304, f32[1024,128]{1,0:T(8,128)S(1)} %bitcast.300, ...), custom_call_target="tpu_custom_call" | custom-call | tf_op jit(solution)/shard_map/pallas_call | solution.py:409
  16.4 1.0 %collective-permute-start.21 = (f32[4,8,128]{2,1,0:T(8,128)S(1)}, f32[4,8,128]{2,1,0:T(8,128)S(1)}, u32[]{:S(2)}, u32[]{:S(2)}) collective-permute-start(f32[4,8,128]{2,1,0:T(8,128)S(1)} %get-tuple-element.67), channel_id=1, source_target_pairs={{0,1},{1,0},{2,3},{3,2},{4,5},{5,4},{6,7},{7,6},{8,9},{9,8},{10,11... | collective-permute-start | bytes 49160 | tf_op jit(solution)/shard_map/ppermute | solution.py:637
  17.4 0.8 %collective-permute-done.21 = f32[4,8,128]{2,1,0:T(8,128)S(1)} collective-permute-done((f32[4,8,128]{2,1,0:T(8,128)S(1)}, f32[4,8,128]{2,1,0:T(8,128)S(1)}, u32[]{:S(2)}, u32[]{:S(2)}) %collective-permute-start.21) | collective-permute-done | bytes 16416 | tf_op jit(solution)/shard_map/ppermute | solution.py:637
  18.3 1.3 %collective-permute-start.22 = (f32[8,8,128]{2,1,0:T(8,128)S(1)}, f32[8,8,128]{2,1,0:T(8,128)S(1)}, u32[]{:S(2)}, u32[]{:S(2)}) collective-permute-start(f32[8,8,128]{2,1,0:T(8,128)S(1)} %get-tuple-element.317), channel_id=1, source_target_pairs={{0,6},{1,3},{2,0},{3,5},{4,2},{5,7},{6,4},{7,1},{8,14},{9,11},{10,... | collective-permute-start | bytes 98312 | tf_op jit(solution)/shard_map/ppermute | solution.py:642
  19.6 2.6 %collective-permute-start.23 = (f32[8,8,128]{2,1,0:T(8,128)S(1)}, f32[8,8,128]{2,1,0:T(8,128)S(1)}, u32[]{:S(2)}, u32[]{:S(2)}) collective-permute-start(f32[8,8,128]{2,1,0:T(8,128)S(1)} %get-tuple-element.317), channel_id=1, source_target_pairs={{0,4},{1,5},{2,6},{3,7},{4,0},{5,1},{6,2},{7,3},{8,12},{9,13},{10,... | collective-permute-start | bytes 98312 | tf_op jit(solution)/shard_map/ppermute | solution.py:641
  23.2 0.9 %collective-permute-done.23 = f32[8,8,128]{2,1,0:T(8,128)S(1)} collective-permute-done((f32[8,8,128]{2,1,0:T(8,128)S(1)}, f32[8,8,128]{2,1,0:T(8,128)S(1)}, u32[]{:S(2)}, u32[]{:S(2)}) %collective-permute-start.23) | collective-permute-done | bytes 32800 | tf_op jit(solution)/shard_map/ppermute | solution.py:641
  24.1 12.8 %all-to-all-done.2 = f32[16,192,128]{2,1,0:T(8,128)S(1)} async-done(((f32[16,192,128]{2,1,0:T(8,128)}), f32[16,192,128]{2,1,0:T(8,128)S(1)}, u32[]{:S(2)}, u32[]{:S(2)}) %all-to-all-start.2) | async-done | bytes 1572896 | tf_op jit(solution)/shard_map/all_to_all | solution.py:683
  36.9 2.6 %shard_map.97 = (f32[1024,128]{1,0:T(8,128)}, f32[1,8,128]{2,1,0:T(8,128)S(1)}) custom-call(f32[32,8,128]{2,1,0:T(8,128)S(1)} %constant_dynamic-update-slice_fusion.2.after_ref.matrix_ref, f32[3072,128]{1,0:T(8,128)S(1)} %bitcast.297), custom_call_target="tpu_custom_call" | custom-call | tf_op jit(solution)/shard_map/pallas_call | solution.py:356
  39.5 4.7 %all-to-all-start.3 = ((f32[16,64,128]{2,1,0:T(8,128)}), f32[16,64,128]{2,1,0:T(8,128)S(1)}, u32[]{:S(2)}, u32[]{:S(2)}) async-start(f32[16,64,128]{2,1,0:T(8,128)} %bitcast.109), calls=%async_computation.3 | async-start | bytes 1048576 | tf_op jit(solution)/shard_map/all_to_all | solution.py:688
  44.3 10.0 %all-to-all-done.3 = f32[16,64,128]{2,1,0:T(8,128)S(1)} async-done(((f32[16,64,128]{2,1,0:T(8,128)}), f32[16,64,128]{2,1,0:T(8,128)S(1)}, u32[]{:S(2)}, u32[]{:S(2)}) %all-to-all-start.3) | async-done | bytes 524320 | tf_op jit(solution)/shard_map/all_to_all | solution.py:688
  55.1 2.4 %collective-permute-start.25 = (f32[3,8,128]{2,1,0:T(8,128)S(1)}, f32[3,8,128]{2,1,0:T(8,128)S(1)}, u32[]{:S(2)}, u32[]{:S(2)}) collective-permute-start(f32[3,8,128]{2,1,0:T(8,128)S(1)} %shard_map.98), channel_id=1, source_target_pairs={{0,1},{1,0},{2,3},{3,2},{4,5},{5,4},{6,7},{7,6},{8,9},{9,8},{10,11... | collective-permute-start | bytes 36872 | tf_op jit(solution)/shard_map/ppermute | solution.py:637
  58.4 1.3 %collective-permute-start.26 = (f32[6,8,128]{2,1,0:T(8,128)S(1)}, f32[6,8,128]{2,1,0:T(8,128)S(1)}, u32[]{:S(2)}, u32[]{:S(2)}) collective-permute-start(f32[6,8,128]{2,1,0:T(8,128)S(1)} %pad_maximum_fusion.14.after_ref), channel_id=1, source_target_pairs={{0,6},{1,3},{2,0},{3,5},{4,2},{5,7},{6,4},{7,1},{8,14},{9,11},{10,... | collective-permute-start | bytes 73736 | tf_op jit(solution)/shard_map/ppermute | solution.py:642
  59.7 2.6 %collective-permute-start.27 = (f32[6,8,128]{2,1,0:T(8,128)S(1)}, f32[6,8,128]{2,1,0:T(8,128)S(1)}, u32[]{:S(2)}, u32[]{:S(2)}) collective-permute-start(f32[6,8,128]{2,1,0:T(8,128)S(1)} %pad_maximum_fusion.14.after_ref), channel_id=1, source_target_pairs={{0,4},{1,5},{2,6},{3,7},{4,0},{5,1},{6,2},{7,3},{8,12},{9,13},{10,... | collective-permute-start | bytes 73736 | tf_op jit(solution)/shard_map/ppermute | solution.py:641
  62.3 2.1 %shard_map.99.middle_ref = f32[128,10,8,128]{3,2,1,0:T(8,128)S(1)} custom-call(f32[6,8,128]{2,1,0:T(8,128)S(1)} %pad_maximum_fusion.14.after_ref, s32[2]{0:T(128)S(1)} %pad_add_fusion.1.where_ref, f32[128,8,128]{2,1,0:T(8,128)S(1)} %bitcast.299, f32[1024,128]{1,0:T(8,128)} %bitcast.309, f32[1024,128]{1,0:T(8,128)S(1)} %bitcast.303, f32[1024,128]{1,0:T(8,128)} %bitcast.305, ...), custom_call_target="tpu_custom_call" | custom-call | tf_op jit(solution)/shard_map/pallas_call | solution.py:523
  64.6 1.1 %collective-permute-done.28 = f32[6,8,128]{2,1,0:T(8,128)S(1)} collective-permute-done((f32[6,8,128]{2,1,0:T(8,128)S(1)}, f32[6,8,128]{2,1,0:T(8,128)S(1)}, u32[]{:S(2)}, u32[]{:S(2)}) %collective-permute-start.28) | collective-permute-done | bytes 24608 | tf_op jit(solution)/shard_map/ppermute | solution.py:643
  65.7 1.3 %shard_map.100 = (f32[128,5,8,128]{3,2,1,0:T(8,128)S(1)}, f32[6,8,128]{2,1,0:T(8,128)S(1)}) custom-call(s32[2]{0:T(128)S(1)} %pad_add_fusion.1.where_ref, f32[32,8,128]{2,1,0:T(8,128)S(1)} %constant_dynamic-update-slice_fusion.2.after_ref.matrix_ref, f32[24,8,128]{2,1,0:T(8,128)S(1)} %constant_dynamic-update-slice_fusion.7.loads_ref, ...), custom_call_target="tpu_custom_call" | custom-call | tf_op jit(solution)/shard_map/pallas_call | solution.py:574
  67.0 1.5 %collective-permute-start.29 = (f32[6,8,128]{2,1,0:T(8,128)S(1)}, f32[6,8,128]{2,1,0:T(8,128)S(1)}, u32[]{:S(2)}, u32[]{:S(2)}) collective-permute-start(f32[6,8,128]{2,1,0:T(8,128)S(1)} %get-tuple-element.72), channel_id=1, source_target_pairs={{0,1},{1,0},{2,3},{3,2},{4,5},{5,4},{6,7},{7,6},{8,9},{9,8},{10,11... | collective-permute-start | bytes 73736 | tf_op jit(solution)/shard_map/ppermute | solution.py:637
  68.5 0.8 %collective-permute-done.29 = f32[6,8,128]{2,1,0:T(8,128)S(1)} collective-permute-done((f32[6,8,128]{2,1,0:T(8,128)S(1)}, f32[6,8,128]{2,1,0:T(8,128)S(1)}, u32[]{:S(2)}, u32[]{:S(2)}) %collective-permute-start.29) | collective-permute-done | bytes 24608 | tf_op jit(solution)/shard_map/ppermute | solution.py:637
  69.3 1.8 %collective-permute-start.31 = (f32[12,8,128]{2,1,0:T(8,128)S(1)}, f32[12,8,128]{2,1,0:T(8,128)S(1)}, u32[]{:S(2)}, u32[]{:S(2)}) collective-permute-start(f32[12,8,128]{2,1,0:T(8,128)S(1)} %get-tuple-element.313), channel_id=1, source_target_pairs={{0,4},{1,5},{2,6},{3,7},{4,0},{5,1},{6,2},{7,3},{8,12},{9,13},{10,... | collective-permute-start | bytes 147464 | tf_op jit(solution)/shard_map/ppermute | solution.py:641
  71.1 2.9 %collective-permute-done.30 = f32[12,8,128]{2,1,0:T(8,128)S(1)} collective-permute-done((f32[12,8,128]{2,1,0:T(8,128)S(1)}, f32[12,8,128]{2,1,0:T(8,128)S(1)}, u32[]{:S(2)}, u32[]{:S(2)}) %collective-permute-start.30) | collective-permute-done | bytes 49184 | tf_op jit(solution)/shard_map/ppermute | solution.py:642
  74.1 1.1 %collective-permute-done.32 = f32[12,8,128]{2,1,0:T(8,128)S(1)} collective-permute-done((f32[12,8,128]{2,1,0:T(8,128)S(1)}, f32[12,8,128]{2,1,0:T(8,128)S(1)}, u32[]{:S(2)}, u32[]{:S(2)}) %collective-permute-start.32) | collective-permute-done | bytes 49184 | tf_op jit(solution)/shard_map/ppermute | solution.py:643
  75.3 2.3 %shard_map.101 = (f32[1024,128]{1,0:T(8,128)}, f32[1024,128]{1,0:T(8,128)}, s32[1]{0:T(128)}) custom-call(s32[2]{0:T(128)S(1)} %pad_add_fusion.1.where_ref, f32[24,8,128]{2,1,0:T(8,128)S(1)} %constant_dynamic-update-slice_fusion.7.loads_ref, f32[48,8,128]{2,1,0:T(8,128)S(1)} %constant_dynamic-update-slice_fusion.14.ports_ref, ...), custom_call_target="tpu_custom_call" | custom-call | tf_op jit(solution)/shard_map/pallas_call | solution.py:621
  (43 shorter events, 3.7 us)
Async XLA Ops:
  5.4 8.6 %copy-start = (f32[128,1024]{1,0:T(8,128)S(1)}, f32[128,1024]{1,0:T(8,128)}, u32[]{:S(2)}) copy-start(f32[128,1024]{1,0:T(8,128)} %param.13) | copy-start | bytes 1572868
  5.4 31.5 %all-to-all-start.2 = ((f32[16,192,128]{2,1,0:T(8,128)}), f32[16,192,128]{2,1,0:T(8,128)S(1)}, u32[]{:S(2)}, u32[]{:S(2)}) async-start(f32[16,192,128]{2,1,0:T(8,128)} %bitcast.107), calls=%async_computation.2 | async-start | bytes 3145728 | tf_op jit(solution)/shard_map/all_to_all | solution.py:683
  16.4 1.9 %collective-permute-start.21 = (f32[4,8,128]{2,1,0:T(8,128)S(1)}, f32[4,8,128]{2,1,0:T(8,128)S(1)}, u32[]{:S(2)}, u32[]{:S(2)}) collective-permute-start(f32[4,8,128]{2,1,0:T(8,128)S(1)} %get-tuple-element.67), channel_id=1, source_target_pairs={{0,1},{1,0},{2,3},{3,2},{4,5},{5,4},{6,7},{7,6},{8,9},{9,8},{10,11... | collective-permute-start | bytes 49160 | tf_op jit(solution)/shard_map/ppermute | solution.py:637
  18.3 4.3 %collective-permute-start.22 = (f32[8,8,128]{2,1,0:T(8,128)S(1)}, f32[8,8,128]{2,1,0:T(8,128)S(1)}, u32[]{:S(2)}, u32[]{:S(2)}) collective-permute-start(f32[8,8,128]{2,1,0:T(8,128)S(1)} %get-tuple-element.317), channel_id=1, source_target_pairs={{0,6},{1,3},{2,0},{3,5},{4,2},{5,7},{6,4},{7,1},{8,14},{9,11},{10,... | collective-permute-start | bytes 98312 | tf_op jit(solution)/shard_map/ppermute | solution.py:642
  19.6 4.6 %collective-permute-start.23 = (f32[8,8,128]{2,1,0:T(8,128)S(1)}, f32[8,8,128]{2,1,0:T(8,128)S(1)}, u32[]{:S(2)}, u32[]{:S(2)}) collective-permute-start(f32[8,8,128]{2,1,0:T(8,128)S(1)} %get-tuple-element.317), channel_id=1, source_target_pairs={{0,4},{1,5},{2,6},{3,7},{4,0},{5,1},{6,2},{7,3},{8,12},{9,13},{10,... | collective-permute-start | bytes 98312 | tf_op jit(solution)/shard_map/ppermute | solution.py:641
  22.6 1.5 %collective-permute-start.24 = (f32[8,8,128]{2,1,0:T(8,128)S(1)}, f32[8,8,128]{2,1,0:T(8,128)S(1)}, u32[]{:S(2)}, u32[]{:S(2)}) collective-permute-start(f32[8,8,128]{2,1,0:T(8,128)S(1)} %collective-permute-done.22), channel_id=1, source_target_pairs={{0,1},{1,0},{2,3},{3,2},{4,5},{5,4},{6,7},{7,6},{8,9},{9,8},{10,11... | collective-permute-start | bytes 98312 | tf_op jit(solution)/shard_map/ppermute | solution.py:643
  39.5 22.8 %copy-start.1 = (f32[128,1024]{1,0:T(8,128)S(1)}, f32[128,1024]{1,0:T(8,128)}, u32[]{:S(2)}) copy-start(f32[128,1024]{1,0:T(8,128)} %param.11) | copy-start | bytes 1572868
  39.5 14.8 %all-to-all-start.3 = ((f32[16,64,128]{2,1,0:T(8,128)}), f32[16,64,128]{2,1,0:T(8,128)S(1)}, u32[]{:S(2)}, u32[]{:S(2)}) async-start(f32[16,64,128]{2,1,0:T(8,128)} %bitcast.109), calls=%async_computation.3 | async-start | bytes 1048576 | tf_op jit(solution)/shard_map/all_to_all | solution.py:688
  55.1 3.3 %collective-permute-start.25 = (f32[3,8,128]{2,1,0:T(8,128)S(1)}, f32[3,8,128]{2,1,0:T(8,128)S(1)}, u32[]{:S(2)}, u32[]{:S(2)}) collective-permute-start(f32[3,8,128]{2,1,0:T(8,128)S(1)} %shard_map.98), channel_id=1, source_target_pairs={{0,1},{1,0},{2,3},{3,2},{4,5},{5,4},{6,7},{7,6},{8,9},{9,8},{10,11... | collective-permute-start | bytes 36872 | tf_op jit(solution)/shard_map/ppermute | solution.py:637
  58.4 6.0 %collective-permute-start.26 = (f32[6,8,128]{2,1,0:T(8,128)S(1)}, f32[6,8,128]{2,1,0:T(8,128)S(1)}, u32[]{:S(2)}, u32[]{:S(2)}) collective-permute-start(f32[6,8,128]{2,1,0:T(8,128)S(1)} %pad_maximum_fusion.14.after_ref), channel_id=1, source_target_pairs={{0,6},{1,3},{2,0},{3,5},{4,2},{5,7},{6,4},{7,1},{8,14},{9,11},{10,... | collective-permute-start | bytes 73736 | tf_op jit(solution)/shard_map/ppermute | solution.py:642
  59.7 4.9 %collective-permute-start.27 = (f32[6,8,128]{2,1,0:T(8,128)S(1)}, f32[6,8,128]{2,1,0:T(8,128)S(1)}, u32[]{:S(2)}, u32[]{:S(2)}) collective-permute-start(f32[6,8,128]{2,1,0:T(8,128)S(1)} %pad_maximum_fusion.14.after_ref), channel_id=1, source_target_pairs={{0,4},{1,5},{2,6},{3,7},{4,0},{5,1},{6,2},{7,3},{8,12},{9,13},{10,... | collective-permute-start | bytes 73736 | tf_op jit(solution)/shard_map/ppermute | solution.py:641
  64.4 1.3 %collective-permute-start.28 = (f32[6,8,128]{2,1,0:T(8,128)S(1)}, f32[6,8,128]{2,1,0:T(8,128)S(1)}, u32[]{:S(2)}, u32[]{:S(2)}) collective-permute-start(f32[6,8,128]{2,1,0:T(8,128)S(1)} %collective-permute-done.26), channel_id=1, source_target_pairs={{0,1},{1,0},{2,3},{3,2},{4,5},{5,4},{6,7},{7,6},{8,9},{9,8},{10,11... | collective-permute-start | bytes 73736 | tf_op jit(solution)/shard_map/ppermute | solution.py:643
  67.0 2.3 %collective-permute-start.29 = (f32[6,8,128]{2,1,0:T(8,128)S(1)}, f32[6,8,128]{2,1,0:T(8,128)S(1)}, u32[]{:S(2)}, u32[]{:S(2)}) collective-permute-start(f32[6,8,128]{2,1,0:T(8,128)S(1)} %get-tuple-element.72), channel_id=1, source_target_pairs={{0,1},{1,0},{2,3},{3,2},{4,5},{5,4},{6,7},{7,6},{8,9},{9,8},{10,11... | collective-permute-start | bytes 73736 | tf_op jit(solution)/shard_map/ppermute | solution.py:637
  69.3 4.7 %collective-permute-start.30 = (f32[12,8,128]{2,1,0:T(8,128)S(1)}, f32[12,8,128]{2,1,0:T(8,128)S(1)}, u32[]{:S(2)}, u32[]{:S(2)}) collective-permute-start(f32[12,8,128]{2,1,0:T(8,128)S(1)} %get-tuple-element.313), channel_id=1, source_target_pairs={{0,6},{1,3},{2,0},{3,5},{4,2},{5,7},{6,4},{7,1},{8,14},{9,11},{10,... | collective-permute-start | bytes 147464 | tf_op jit(solution)/shard_map/ppermute | solution.py:642
  69.3 4.7 %collective-permute-start.31 = (f32[12,8,128]{2,1,0:T(8,128)S(1)}, f32[12,8,128]{2,1,0:T(8,128)S(1)}, u32[]{:S(2)}, u32[]{:S(2)}) collective-permute-start(f32[12,8,128]{2,1,0:T(8,128)S(1)} %get-tuple-element.313), channel_id=1, source_target_pairs={{0,4},{1,5},{2,6},{3,7},{4,0},{5,1},{6,2},{7,3},{8,12},{9,13},{10,... | collective-permute-start | bytes 147464 | tf_op jit(solution)/shard_map/ppermute | solution.py:641
  74.0 1.2 %collective-permute-start.32 = (f32[12,8,128]{2,1,0:T(8,128)S(1)}, f32[12,8,128]{2,1,0:T(8,128)S(1)}, u32[]{:S(2)}, u32[]{:S(2)}) collective-permute-start(f32[12,8,128]{2,1,0:T(8,128)S(1)} %collective-permute-done.30), channel_id=1, source_target_pairs={{0,1},{1,0},{2,3},{3,2},{4,5},{5,4},{6,7},{7,6},{8,9},{9,8},{10,11... | collective-permute-start | bytes 147464 | tf_op jit(solution)/shard_map/ppermute | solution.py:643
  74.0 3.5 %copy-start.2 = (f32[128,1024]{1,0:T(8,128)S(1)}, f32[128,1024]{1,0:T(8,128)}, u32[]{:S(2)}) copy-start(f32[128,1024]{1,0:T(8,128)} %param.12) | copy-start | bytes 1572868
  74.0 3.5 %copy-start.3 = (f32[128,1024]{1,0:T(8,128)S(1)}, f32[128,1024]{1,0:T(8,128)}, u32[]{:S(2)}) copy-start(f32[128,1024]{1,0:T(8,128)} %param.14) | copy-start | bytes 1572868
  74.1 3.5 %copy-start.4 = (f32[128,1024]{1,0:T(8,128)S(1)}, f32[128,1024]{1,0:T(8,128)}, u32[]{:S(2)}) copy-start(f32[128,1024]{1,0:T(8,128)} %param.10) | copy-start | bytes 1572868
  74.1 3.5 %copy-start.19 = (s32[1,2048,1]{1,2,0:T(1,128)S(1)}, s32[1,2048,1]{1,2,0:T(1,128)}, u32[]{:S(2)}) copy-start(s32[1,2048,1]{1,2,0:T(1,128)} %param.16) | copy-start | bytes 24580
  74.1 3.5 %copy-start.20 = (s32[1,2048]{1,0:T(1,128)S(1)}, s32[1,2048]{1,0:T(1,128)}, u32[]{:S(2)}) copy-start(s32[1,2048]{1,0:T(1,128)} %param.17) | copy-start | bytes 24580

commit v5 on v4

--- a/solution.py
+++ b/solution.py
@@ -283,11 +283,10 @@
     copy.wait()
     heat_copy.wait()
 
-    @pl.loop(0, groups)
-    def _(g):
+    for g in range(groups):
         for i in range(lanes):
             row = row_smem[g, i]
-            out_ref[pl.ds(row, 1), :] = heat_ref[pl.ds(g * lanes + i, 1), :]
+            out_ref[pl.ds(row, 1), :] = heat_ref[g * lanes + i : g * lanes + i + 1, :]
 
     for m in range(16):
         out_ref[m * SLOTS + ROOM : m * SLOTS + ROOM + 1, :] = places[m : m + 1, :lanes]
@@ -457,9 +456,9 @@
 def slot_of(me, block):
     steps = (lax.shift_right_logical(block, 1) - lax.shift_right_logical(me, 1)) & 3
     other = (me ^ block) & 1
-    core = me & 1
-    odd = jnp.where(lax.shift_right_logical(steps, 1) == core, 2 + other, 7 - other)
-    return jnp.where((steps & 1) == 1, odd, steps * 2 + other)
+    odd = jnp.where(lax.shift_right_logical(steps, 1) == (me & 1), 2 + other, 6 - other)
+    even = jnp.where(steps == 0, other, 4 + 3 * other)
+    return jnp.where((steps & 1) == 1, odd, even)
 
 
 def block_ends(where_ref, port_of):
@@ -633,19 +632,20 @@
     )(where, loads, ports, kept)
 
 
-def swapped(rows):
+def chip_rows(rows):
     return jnp.concatenate([rows, lax.ppermute(rows, "gz", [(i, i ^ 1) for i in range(8)])], 0)
 
 
-def spread(rows):
+def spread(rows, both):
     across = lax.ppermute(rows, "gz", [(i, (i + 4) % 8) for i in range(8)])
-    beside = lax.ppermute(rows, "gz", [(i, (i - 2 + 4 * (i % 2)) % 8) for i in range(8)])
-    passed = lax.ppermute(beside, "gz", [(i, i ^ 1) for i in range(8)])
-    return jnp.concatenate([rows, beside, across, passed], 0)
+    beside = lax.ppermute(both, "gz", [(i, (i - 2 + 4 * (i % 2)) % 8) for i in range(8)])
+    fetched = jnp.concatenate([beside, across], 0)
+    passed = lax.ppermute(fetched, "gz", [(i, i ^ 1) for i in range(8)])
+    return jnp.concatenate([both, fetched, passed], 0)
 
 
 def gathered(rows):
-    return spread(swapped(rows))
+    return spread(rows, chip_rows(rows))
 
 
 def tiles_of(field):
@@ -686,9 +686,10 @@
     matrix = gathered(matrix)
     sums, flag = sum_records(matrix, got.reshape(16 * SLOTS, 128))
     sums = lax.all_to_all(sums.reshape(16, 64, 128), "col", 0, 0, tiled=True).reshape(128, 8, 128)
-    loads = swapped(load_blocks(where, flag, sums, base, weight))
-    cells = middle(loads, where, sums, *fields)
-    loads = spread(loads)
+    loads = load_blocks(where, flag, sums, base, weight)
+    both = chip_rows(loads)
+    cells = middle(both, where, sums, *fields)
+    loads = spread(loads, both)
     kept, ports = second_step(where, matrix, loads, cells)
     flux, temp, crowded = finish(where, loads, gathered(ports), kept)
 

time: 79 us -> 77.3 us (0.978)
  starting transfers between devices: 28.6 us -> 27.2 us
    all_to_all x1, waiting for transfers between devices: 12.8 us -> 11 us  [shards(): got = lax.all_to_all(sent.reshape(16, SLOTS, 128), 'col', 0, 0, tiled=True)]
    ppermute x9, starting transfers between devices: 8.3 us -> 6.74 us  [the longest x3 3.86 us: chip_rows(): lax.ppermute(rows, 'gz', [(i, i ^ 1) for i in range(8)])]
    ppermute x3, waiting for transfers between devices: 0.9 us -> 2.24 us  [spread(): across = lax.ppermute(rows, 'gz', [(i, (i + 4) % 8) for i in range(8)])]
where the time goes in v5:
time: 77.3 us; the launch traced here: 76.9 us
  waiting for transfers between devices  32.1 us (42%)
  starting transfers between devices  27.2 us (35%)
  Pallas kernels  15.6 us (20%)
  between operations  1.01 us (1%)
  loops' own time  0.86 us (1%)
    all_to_all x1, waiting for transfers between devices, shards(): got = lax.all_to_all(sent.reshape(16, SLOTS, 128), 'col', 0, 0, tiled=True)  11 us
    all_to_all x1, waiting for transfers between devices, shards(): lax.all_to_all(sums.reshape(16, 64, 128), 'col', 0, 0, tiled=True)  10 us
    all_to_all x1, starting transfers between devices, shards(): got = lax.all_to_all(sent.reshape(16, SLOTS, 128), 'col', 0, 0, tiled=True)  8.57 us
    ppermute x3, starting transfers between devices, spread(): across = lax.ppermute(rows, 'gz', [(i, (i + 4) % 8) for i in range(8)])  7.15 us
    ppermute x3, waiting for transfers between devices, spread(): lax.ppermute(both, 'gz', [(i, (i - 2 + 4 * (i % 2)) % 8) for i in range(8)])  5.86 us
    all_to_all x1, starting transfers between devices, shards(): lax.all_to_all(sums.reshape(16, 64, 128), 'col', 0, 0, tiled=True)  4.71 us
    pallas_call x1, Pallas kernels, pack(): pl.pallas_call(pack_kernel, out_shape=jax.ShapeDtypeStruct((16 * SLOTS, 1...  4.19 us
    ppermute x3, starting transfers between devices, chip_rows(): lax.ppermute(rows, 'gz', [(i, i ^ 1) for i in range(8)])  3.86 us
  transfers between devices with their start and end apart: 14, of which 10 were waited for; matrix products, arithmetic and copies ran while one was open for 0% of the time, Pallas kernels for 6%

profile of v5, /device:TPU:1, one launch (start us, length us, event | category | flops | bytes accessed | tf_op | source)
XLA Modules:
  0.0 76.9 jit_solution(16803560700119070575)
XLA Ops:
  0.6 4.2 %shard_map.95.after_ref = f32[3072,128]{1,0:T(8,128)} custom-call(s32[16,128]{1,0:T(8,128)} %bitcast.317, s32[16,128]{1,0:T(8,128)} %bitcast.378, f32[2048,128]{1,0:T(8,128)} %bitcast.311), custom_call_target="tpu_custom_call" | custom-call | tf_op jit(solution)/shard_map/pallas_call | solution.py:297
  4.8 8.6 %all-to-all-start.2 = ((f32[16,192,128]{2,1,0:T(8,128)}), f32[16,192,128]{2,1,0:T(8,128)S(1)}, u32[]{:S(2)}, u32[]{:S(2)}) async-start(f32[16,192,128]{2,1,0:T(8,128)} %bitcast.107), calls=%async_computation.2 | async-start | bytes 3145728 | tf_op jit(solution)/shard_map/all_to_all | solution.py:683
  13.4 2.3 %shard_map.96 = (f32[128,2,8,128]{3,2,1,0:T(8,128)S(1)}, f32[4,8,128]{2,1,0:T(8,128)S(1)}, f32[2,8,128]{2,1,0:T(8,128)S(1)}) custom-call(f32[3072,128]{1,0:T(8,128)} %shard_map.95.after_ref, f32[1024,128]{1,0:T(8,128)} %bitcast.308, f32[1024,128]{1,0:T(8,128)} %bitcast.302, f32[1024,128]{1,0:T(8,128)} %bitcast.304, f32[1024,128]{1,0:T(8,128)S(1)} %bitcast.300, ...), custom_call_target="tpu_custom_call" | custom-call | tf_op jit(solution)/shard_map/pallas_call | solution.py:408
  15.8 1.0 %collective-permute-start.21 = (f32[4,8,128]{2,1,0:T(8,128)S(1)}, f32[4,8,128]{2,1,0:T(8,128)S(1)}, u32[]{:S(2)}, u32[]{:S(2)}) collective-permute-start(f32[4,8,128]{2,1,0:T(8,128)S(1)} %get-tuple-element.67), channel_id=1, source_target_pairs={{0,1},{1,0},{2,3},{3,2},{4,5},{5,4},{6,7},{7,6},{8,9},{9,8},{10,11... | collective-permute-start | bytes 49160 | tf_op jit(solution)/shard_map/ppermute | solution.py:636
  16.8 2.9 %collective-permute-start.23 = (f32[4,8,128]{2,1,0:T(8,128)S(1)}, f32[4,8,128]{2,1,0:T(8,128)S(1)}, u32[]{:S(2)}, u32[]{:S(2)}) collective-permute-start(f32[4,8,128]{2,1,0:T(8,128)S(1)} %get-tuple-element.67), channel_id=1, source_target_pairs={{0,4},{1,5},{2,6},{3,7},{4,0},{5,1},{6,2},{7,3},{8,12},{9,13},{10,... | collective-permute-start | bytes 49160 | tf_op jit(solution)/shard_map/ppermute | solution.py:640
  20.9 3.2 %collective-permute-done.22 = f32[8,8,128]{2,1,0:T(8,128)S(1)} collective-permute-done((f32[8,8,128]{2,1,0:T(8,128)S(1)}, f32[8,8,128]{2,1,0:T(8,128)S(1)}, u32[]{:S(2)}, u32[]{:S(2)}) %collective-permute-start.22) | collective-permute-done | bytes 32800 | tf_op jit(solution)/shard_map/ppermute | solution.py:641
  24.1 1.2 %collective-permute-done.24 = f32[12,8,128]{2,1,0:T(8,128)S(1)} collective-permute-done((f32[12,8,128]{2,1,0:T(8,128)S(1)}, f32[12,8,128]{2,1,0:T(8,128)S(1)}, u32[]{:S(2)}, u32[]{:S(2)}) %collective-permute-start.24) | collective-permute-done | bytes 49184 | tf_op jit(solution)/shard_map/ppermute | solution.py:643
  25.3 11.0 %all-to-all-done.2 = f32[16,192,128]{2,1,0:T(8,128)S(1)} async-done(((f32[16,192,128]{2,1,0:T(8,128)}), f32[16,192,128]{2,1,0:T(8,128)S(1)}, u32[]{:S(2)}, u32[]{:S(2)}) %all-to-all-start.2) | async-done | bytes 1572896 | tf_op jit(solution)/shard_map/all_to_all | solution.py:683
  36.3 2.6 %shard_map.97 = (f32[1024,128]{1,0:T(8,128)}, f32[1,8,128]{2,1,0:T(8,128)S(1)}) custom-call(f32[32,8,128]{2,1,0:T(8,128)S(1)} %constant_dynamic-update-slice_fusion.after_ref.matrix_ref, f32[3072,128]{1,0:T(8,128)S(1)} %bitcast.297), custom_call_target="tpu_custom_call" | custom-call | tf_op jit(solution)/shard_map/pallas_call | solution.py:355
  38.9 4.7 %all-to-all-start.3 = ((f32[16,64,128]{2,1,0:T(8,128)}), f32[16,64,128]{2,1,0:T(8,128)S(1)}, u32[]{:S(2)}, u32[]{:S(2)}) async-start(f32[16,64,128]{2,1,0:T(8,128)} %bitcast.109), calls=%async_computation.3 | async-start | bytes 1048576 | tf_op jit(solution)/shard_map/all_to_all | solution.py:688
  43.7 10.0 %all-to-all-done.3 = f32[16,64,128]{2,1,0:T(8,128)S(1)} async-done(((f32[16,64,128]{2,1,0:T(8,128)}), f32[16,64,128]{2,1,0:T(8,128)S(1)}, u32[]{:S(2)}, u32[]{:S(2)}) %all-to-all-start.3) | async-done | bytes 524320 | tf_op jit(solution)/shard_map/all_to_all | solution.py:688
  54.5 2.4 %collective-permute-start.25 = (f32[3,8,128]{2,1,0:T(8,128)S(1)}, f32[3,8,128]{2,1,0:T(8,128)S(1)}, u32[]{:S(2)}, u32[]{:S(2)}) collective-permute-start(f32[3,8,128]{2,1,0:T(8,128)S(1)} %shard_map.98), channel_id=1, source_target_pairs={{0,1},{1,0},{2,3},{3,2},{4,5},{5,4},{6,7},{7,6},{8,9},{9,8},{10,11... | collective-permute-start | bytes 36872 | tf_op jit(solution)/shard_map/ppermute | solution.py:636
  56.9 2.9 %collective-permute-start.27 = (f32[3,8,128]{2,1,0:T(8,128)S(1)}, f32[3,8,128]{2,1,0:T(8,128)S(1)}, u32[]{:S(2)}, u32[]{:S(2)}) collective-permute-start(f32[3,8,128]{2,1,0:T(8,128)S(1)} %shard_map.98), channel_id=1, source_target_pairs={{0,4},{1,5},{2,6},{3,7},{4,0},{5,1},{6,2},{7,3},{8,12},{9,13},{10,... | collective-permute-start | bytes 36872 | tf_op jit(solution)/shard_map/ppermute | solution.py:640
  60.3 2.1 %shard_map.99.middle_ref = f32[128,10,8,128]{3,2,1,0:T(8,128)S(1)} custom-call(f32[6,8,128]{2,1,0:T(8,128)S(1)} %pad_maximum_fusion.19.after_ref, s32[2]{0:T(128)S(1)} %pad_add_fusion.1.where_ref, f32[128,8,128]{2,1,0:T(8,128)S(1)} %bitcast.299, f32[1024,128]{1,0:T(8,128)} %bitcast.309, f32[1024,128]{1,0:T(8,128)S(1)} %bitcast.303, f32[1024,128]{1,0:T(8,128)} %bitcast.305, ...), custom_call_target="tpu_custom_call" | custom-call | tf_op jit(solution)/shard_map/pallas_call | solution.py:522
  62.4 1.4 %collective-permute-done.26 = f32[6,8,128]{2,1,0:T(8,128)S(1)} collective-permute-done((f32[6,8,128]{2,1,0:T(8,128)S(1)}, f32[6,8,128]{2,1,0:T(8,128)S(1)}, u32[]{:S(2)}, u32[]{:S(2)}) %collective-permute-start.26) | collective-permute-done | bytes 24608 | tf_op jit(solution)/shard_map/ppermute | solution.py:641
  64.1 0.9 %collective-permute-done.28 = f32[9,8,128]{2,1,0:T(8,128)S(1)} collective-permute-done((f32[9,8,128]{2,1,0:T(8,128)S(1)}, f32[9,8,128]{2,1,0:T(8,128)S(1)}, u32[]{:S(2)}, u32[]{:S(2)}) %collective-permute-start.28) | collective-permute-done | bytes 36896 | tf_op jit(solution)/shard_map/ppermute | solution.py:643
  65.0 1.3 %shard_map.100 = (f32[128,5,8,128]{3,2,1,0:T(8,128)S(1)}, f32[6,8,128]{2,1,0:T(8,128)S(1)}) custom-call(s32[2]{0:T(128)S(1)} %pad_add_fusion.1.where_ref, f32[32,8,128]{2,1,0:T(8,128)S(1)} %constant_dynamic-update-slice_fusion.after_ref.matrix_ref, f32[24,8,128]{2,1,0:T(8,128)S(1)} %constant_dynamic-update-slice_fusion.5.loads_ref, ...), custom_call_target="tpu_custom_call" | custom-call | tf_op jit(solution)/shard_map/pallas_call | solution.py:573
  66.7 1.3 %collective-permute-start.31 = (f32[6,8,128]{2,1,0:T(8,128)S(1)}, f32[6,8,128]{2,1,0:T(8,128)S(1)}, u32[]{:S(2)}, u32[]{:S(2)}) collective-permute-start(f32[6,8,128]{2,1,0:T(8,128)S(1)} %get-tuple-element.72), channel_id=1, source_target_pairs={{0,4},{1,5},{2,6},{3,7},{4,0},{5,1},{6,2},{7,3},{8,12},{9,13},{10,... | collective-permute-start | bytes 73736 | tf_op jit(solution)/shard_map/ppermute | solution.py:640
  68.0 1.3 %collective-permute-start.30 = (f32[12,8,128]{2,1,0:T(8,128)S(1)}, f32[12,8,128]{2,1,0:T(8,128)S(1)}, u32[]{:S(2)}, u32[]{:S(2)}) collective-permute-start(f32[12,8,128]{2,1,0:T(8,128)S(1)} %pad_maximum_fusion.16), channel_id=1, source_target_pairs={{0,6},{1,3},{2,0},{3,5},{4,2},{5,7},{6,4},{7,1},{8,14},{9,11},{10,... | collective-permute-start | bytes 147464 | tf_op jit(solution)/shard_map/ppermute | solution.py:641
  69.3 1.5 %collective-permute-done.31 = f32[6,8,128]{2,1,0:T(8,128)S(1)} collective-permute-done((f32[6,8,128]{2,1,0:T(8,128)S(1)}, f32[6,8,128]{2,1,0:T(8,128)S(1)}, u32[]{:S(2)}, u32[]{:S(2)}) %collective-permute-start.31) | collective-permute-done | bytes 24608 | tf_op jit(solution)/shard_map/ppermute | solution.py:640
  70.9 1.3 %collective-permute-done.30 = f32[12,8,128]{2,1,0:T(8,128)S(1)} collective-permute-done((f32[12,8,128]{2,1,0:T(8,128)S(1)}, f32[12,8,128]{2,1,0:T(8,128)S(1)}, u32[]{:S(2)}, u32[]{:S(2)}) %collective-permute-start.30) | collective-permute-done | bytes 49184 | tf_op jit(solution)/shard_map/ppermute | solution.py:641
  72.7 0.8 %collective-permute-done.32 = f32[18,8,128]{2,1,0:T(8,128)S(1)} collective-permute-done((f32[18,8,128]{2,1,0:T(8,128)S(1)}, f32[18,8,128]{2,1,0:T(8,128)S(1)}, u32[]{:S(2)}, u32[]{:S(2)}) %collective-permute-start.32) | collective-permute-done | bytes 73760 | tf_op jit(solution)/shard_map/ppermute | solution.py:643
  73.5 2.3 %shard_map.101 = (f32[1024,128]{1,0:T(8,128)}, f32[1024,128]{1,0:T(8,128)}, s32[1]{0:T(128)}) custom-call(s32[2]{0:T(128)S(1)} %pad_add_fusion.1.where_ref, f32[24,8,128]{2,1,0:T(8,128)S(1)} %constant_dynamic-update-slice_fusion.5.loads_ref, f32[48,8,128]{2,1,0:T(8,128)S(1)} %constant_dynamic-update-slice_fusion.10.ports_ref, ...), custom_call_target="tpu_custom_call" | custom-call | tf_op jit(solution)/shard_map/pallas_call | solution.py:620
  75.9 0.9 %while.11 = (f32[128,1024]{1,0:T(8,128)}, f32[128,1024]{1,0:T(8,128)}, s32[1]{0:T(128)}, f32[128,1024]{1,0:T(8,128)S(1)}, f32[128,1024]{1,0:T(8,128)S(1)}, /*ind...) while((f32[128,1024]{1,0:T(8,128)}, ...), condition=%region_7.8_spmd, body=%region_0.7_spmd | while | flops 85194096 | bytes 417096704 | solution.py:700
  (48 shorter events, 3.6 us)
Async XLA Ops:
  4.8 8.6 %copy-start = (f32[128,1024]{1,0:T(8,128)S(1)}, f32[128,1024]{1,0:T(8,128)}, u32[]{:S(2)}) copy-start(f32[128,1024]{1,0:T(8,128)} %param.13) | copy-start | bytes 1572868
  4.8 31.5 %all-to-all-start.2 = ((f32[16,192,128]{2,1,0:T(8,128)}), f32[16,192,128]{2,1,0:T(8,128)S(1)}, u32[]{:S(2)}, u32[]{:S(2)}) async-start(f32[16,192,128]{2,1,0:T(8,128)} %bitcast.107), calls=%async_computation.2 | async-start | bytes 3145728 | tf_op jit(solution)/shard_map/all_to_all | solution.py:683
  15.8 4.0 %collective-permute-start.21 = (f32[4,8,128]{2,1,0:T(8,128)S(1)}, f32[4,8,128]{2,1,0:T(8,128)S(1)}, u32[]{:S(2)}, u32[]{:S(2)}) collective-permute-start(f32[4,8,128]{2,1,0:T(8,128)S(1)} %get-tuple-element.67), channel_id=1, source_target_pairs={{0,1},{1,0},{2,3},{3,2},{4,5},{5,4},{6,7},{7,6},{8,9},{9,8},{10,11... | collective-permute-start | bytes 49160 | tf_op jit(solution)/shard_map/ppermute | solution.py:636
  16.8 4.1 %collective-permute-start.23 = (f32[4,8,128]{2,1,0:T(8,128)S(1)}, f32[4,8,128]{2,1,0:T(8,128)S(1)}, u32[]{:S(2)}, u32[]{:S(2)}) collective-permute-start(f32[4,8,128]{2,1,0:T(8,128)S(1)} %get-tuple-element.67), channel_id=1, source_target_pairs={{0,4},{1,5},{2,6},{3,7},{4,0},{5,1},{6,2},{7,3},{8,12},{9,13},{10,... | collective-permute-start | bytes 49160 | tf_op jit(solution)/shard_map/ppermute | solution.py:640
  19.8 4.3 %collective-permute-start.22 = (f32[8,8,128]{2,1,0:T(8,128)S(1)}, f32[8,8,128]{2,1,0:T(8,128)S(1)}, u32[]{:S(2)}, u32[]{:S(2)}) collective-permute-start(f32[8,8,128]{2,1,0:T(8,128)S(1)} %pad_maximum_fusion.18), channel_id=1, source_target_pairs={{0,6},{1,3},{2,0},{3,5},{4,2},{5,7},{6,4},{7,1},{8,14},{9,11},{10,... | collective-permute-start | bytes 98312 | tf_op jit(solution)/shard_map/ppermute | solution.py:641
  24.1 1.2 %collective-permute-start.24 = (f32[12,8,128]{2,1,0:T(8,128)S(1)}, f32[12,8,128]{2,1,0:T(8,128)S(1)}, u32[]{:S(2)}, u32[]{:S(2)}) collective-permute-start(f32[12,8,128]{2,1,0:T(8,128)S(1)} %pad_maximum_fusion.15), channel_id=1, source_target_pairs={{0,1},{1,0},{2,3},{3,2},{4,5},{5,4},{6,7},{7,6},{8,9},{9,8},{10,11... | collective-permute-start | bytes 147464 | tf_op jit(solution)/shard_map/ppermute | solution.py:643
  38.9 21.4 %copy-start.1 = (f32[128,1024]{1,0:T(8,128)S(1)}, f32[128,1024]{1,0:T(8,128)}, u32[]{:S(2)}) copy-start(f32[128,1024]{1,0:T(8,128)} %param.11) | copy-start | bytes 1572868
  38.9 14.8 %all-to-all-start.3 = ((f32[16,64,128]{2,1,0:T(8,128)}), f32[16,64,128]{2,1,0:T(8,128)S(1)}, u32[]{:S(2)}, u32[]{:S(2)}) async-start(f32[16,64,128]{2,1,0:T(8,128)} %bitcast.109), calls=%async_computation.3 | async-start | bytes 1048576 | tf_op jit(solution)/shard_map/all_to_all | solution.py:688
  54.5 5.4 %collective-permute-start.25 = (f32[3,8,128]{2,1,0:T(8,128)S(1)}, f32[3,8,128]{2,1,0:T(8,128)S(1)}, u32[]{:S(2)}, u32[]{:S(2)}) collective-permute-start(f32[3,8,128]{2,1,0:T(8,128)S(1)} %shard_map.98), channel_id=1, source_target_pairs={{0,1},{1,0},{2,3},{3,2},{4,5},{5,4},{6,7},{7,6},{8,9},{9,8},{10,11... | collective-permute-start | bytes 36872 | tf_op jit(solution)/shard_map/ppermute | solution.py:636
  56.9 5.5 %collective-permute-start.27 = (f32[3,8,128]{2,1,0:T(8,128)S(1)}, f32[3,8,128]{2,1,0:T(8,128)S(1)}, u32[]{:S(2)}, u32[]{:S(2)}) collective-permute-start(f32[3,8,128]{2,1,0:T(8,128)S(1)} %shard_map.98), channel_id=1, source_target_pairs={{0,4},{1,5},{2,6},{3,7},{4,0},{5,1},{6,2},{7,3},{8,12},{9,13},{10,... | collective-permute-start | bytes 36872 | tf_op jit(solution)/shard_map/ppermute | solution.py:640
  59.9 3.9 %collective-permute-start.26 = (f32[6,8,128]{2,1,0:T(8,128)S(1)}, f32[6,8,128]{2,1,0:T(8,128)S(1)}, u32[]{:S(2)}, u32[]{:S(2)}) collective-permute-start(f32[6,8,128]{2,1,0:T(8,128)S(1)} %pad_maximum_fusion.19.after_ref), channel_id=1, source_target_pairs={{0,6},{1,3},{2,0},{3,5},{4,2},{5,7},{6,4},{7,1},{8,14},{9,11},{10,... | collective-permute-start | bytes 73736 | tf_op jit(solution)/shard_map/ppermute | solution.py:641
  63.7 1.2 %collective-permute-start.28 = (f32[9,8,128]{2,1,0:T(8,128)S(1)}, f32[9,8,128]{2,1,0:T(8,128)S(1)}, u32[]{:S(2)}, u32[]{:S(2)}) collective-permute-start(f32[9,8,128]{2,1,0:T(8,128)S(1)} %pad_maximum_fusion.17), channel_id=1, source_target_pairs={{0,1},{1,0},{2,3},{3,2},{4,5},{5,4},{6,7},{7,6},{8,9},{9,8},{10,11... | collective-permute-start | bytes 110600 | tf_op jit(solution)/shard_map/ppermute | solution.py:643
  66.3 1.7 %collective-permute-start.29 = (f32[6,8,128]{2,1,0:T(8,128)S(1)}, f32[6,8,128]{2,1,0:T(8,128)S(1)}, u32[]{:S(2)}, u32[]{:S(2)}) collective-permute-start(f32[6,8,128]{2,1,0:T(8,128)S(1)} %get-tuple-element.72), channel_id=1, source_target_pairs={{0,1},{1,0},{2,3},{3,2},{4,5},{5,4},{6,7},{7,6},{8,9},{9,8},{10,11... | collective-permute-start | bytes 73736 | tf_op jit(solution)/shard_map/ppermute | solution.py:636
  66.7 4.2 %collective-permute-start.31 = (f32[6,8,128]{2,1,0:T(8,128)S(1)}, f32[6,8,128]{2,1,0:T(8,128)S(1)}, u32[]{:S(2)}, u32[]{:S(2)}) collective-permute-start(f32[6,8,128]{2,1,0:T(8,128)S(1)} %get-tuple-element.72), channel_id=1, source_target_pairs={{0,4},{1,5},{2,6},{3,7},{4,0},{5,1},{6,2},{7,3},{8,12},{9,13},{10,... | collective-permute-start | bytes 73736 | tf_op jit(solution)/shard_map/ppermute | solution.py:640
  68.0 4.2 %collective-permute-start.30 = (f32[12,8,128]{2,1,0:T(8,128)S(1)}, f32[12,8,128]{2,1,0:T(8,128)S(1)}, u32[]{:S(2)}, u32[]{:S(2)}) collective-permute-start(f32[12,8,128]{2,1,0:T(8,128)S(1)} %pad_maximum_fusion.16), channel_id=1, source_target_pairs={{0,6},{1,3},{2,0},{3,5},{4,2},{5,7},{6,4},{7,1},{8,14},{9,11},{10,... | collective-permute-start | bytes 147464 | tf_op jit(solution)/shard_map/ppermute | solution.py:641
  72.2 1.3 %collective-permute-start.32 = (f32[18,8,128]{2,1,0:T(8,128)S(1)}, f32[18,8,128]{2,1,0:T(8,128)S(1)}, u32[]{:S(2)}, u32[]{:S(2)}) collective-permute-start(f32[18,8,128]{2,1,0:T(8,128)S(1)} %pad_maximum_fusion.14), channel_id=1, source_target_pairs={{0,1},{1,0},{2,3},{3,2},{4,5},{5,4},{6,7},{7,6},{8,9},{9,8},{10,11... | collective-permute-start | bytes 221192 | tf_op jit(solution)/shard_map/ppermute | solution.py:643
  72.6 3.2 %copy-start.2 = (f32[128,1024]{1,0:T(8,128)S(1)}, f32[128,1024]{1,0:T(8,128)}, u32[]{:S(2)}) copy-start(f32[128,1024]{1,0:T(8,128)} %param.12) | copy-start | bytes 1572868
  72.6 3.2 %copy-start.3 = (f32[128,1024]{1,0:T(8,128)S(1)}, f32[128,1024]{1,0:T(8,128)}, u32[]{:S(2)}) copy-start(f32[128,1024]{1,0:T(8,128)} %param.14) | copy-start | bytes 1572868
  72.6 3.2 %copy-start.4 = (f32[128,1024]{1,0:T(8,128)S(1)}, f32[128,1024]{1,0:T(8,128)}, u32[]{:S(2)}) copy-start(f32[128,1024]{1,0:T(8,128)} %param.10) | copy-start | bytes 1572868
  72.6 3.2 %copy-start.19 = (s32[1,2048,1]{1,2,0:T(1,128)S(1)}, s32[1,2048,1]{1,2,0:T(1,128)}, u32[]{:S(2)}) copy-start(s32[1,2048,1]{1,2,0:T(1,128)} %param.16) | copy-start | bytes 24580
  72.6 3.2 %copy-start.20 = (s32[1,2048]{1,0:T(1,128)S(1)}, s32[1,2048]{1,0:T(1,128)}, u32[]{:S(2)}) copy-start(s32[1,2048]{1,0:T(1,128)} %param.17) | copy-start | bytes 24580

commit v6 on v5

--- a/solution.py
+++ b/solution.py
@@ -697,7 +697,7 @@
         return general_path(*arguments) + (jnp.zeros_like(state[2]),)
 
     flux, temp = field_of(flux, height, width), field_of(temp, height, width)
-    return lax.while_loop(lambda state: state[2][0] > 0, again, (flux, temp, crowded))[:2]
+    return lax.while_loop(lambda state: state[2] > 0, again, (flux, temp, crowded.reshape(())))[:2]
 
 
 def solution(mesh):

time: 77.3 us -> 77.3 us (level)
  no operation moved by 1% of the time
where the time goes in v6:
time: 77.3 us; the launch traced here: 76.8 us
  waiting for transfers between devices  32.1 us (42%)
  starting transfers between devices  27.2 us (35%)
  Pallas kernels  15.6 us (20%)
  between operations  1.01 us (1%)
  loops' own time  0.82 us (1%)
    all_to_all x1, waiting for transfers between devices, shards(): got = lax.all_to_all(sent.reshape(16, SLOTS, 128), 'col', 0, 0, tiled=True)  11 us
    all_to_all x1, waiting for transfers between devices, shards(): lax.all_to_all(sums.reshape(16, 64, 128), 'col', 0, 0, tiled=True)  10 us
    all_to_all x1, starting transfers between devices, shards(): got = lax.all_to_all(sent.reshape(16, SLOTS, 128), 'col', 0, 0, tiled=True)  8.57 us
    ppermute x3, starting transfers between devices, spread(): across = lax.ppermute(rows, 'gz', [(i, (i + 4) % 8) for i in range(8)])  7.15 us
    ppermute x3, waiting for transfers between devices, spread(): lax.ppermute(both, 'gz', [(i, (i - 2 + 4 * (i % 2)) % 8) for i in range(8)])  5.86 us
    all_to_all x1, starting transfers between devices, shards(): lax.all_to_all(sums.reshape(16, 64, 128), 'col', 0, 0, tiled=True)  4.71 us
    pallas_call x1, Pallas kernels, pack(): pl.pallas_call(pack_kernel, out_shape=jax.ShapeDtypeStruct((16 * SLOTS, 1...  4.19 us
    ppermute x3, starting transfers between devices, chip_rows(): lax.ppermute(rows, 'gz', [(i, i ^ 1) for i in range(8)])  3.86 us
  transfers between devices with their start and end apart: 14, of which 10 were waited for; matrix products, arithmetic and copies ran while one was open for 0% of the time, Pallas kernels for 6%

profile of v6, /device:TPU:1, one launch (start us, length us, event | category | flops | bytes accessed | tf_op | source)
XLA Modules:
  0.0 76.8 jit_solution(5056284451625737985)
XLA Ops:
  0.6 4.2 %shard_map.95.after_ref = f32[3072,128]{1,0:T(8,128)} custom-call(s32[16,128]{1,0:T(8,128)} %bitcast.317, s32[16,128]{1,0:T(8,128)} %bitcast.378, f32[2048,128]{1,0:T(8,128)} %bitcast.311), custom_call_target="tpu_custom_call" | custom-call | tf_op jit(solution)/shard_map/pallas_call | solution.py:297
  4.8 8.6 %all-to-all-start.2 = ((f32[16,192,128]{2,1,0:T(8,128)}), f32[16,192,128]{2,1,0:T(8,128)S(1)}, u32[]{:S(2)}, u32[]{:S(2)}) async-start(f32[16,192,128]{2,1,0:T(8,128)} %bitcast.106), calls=%async_computation.2 | async-start | bytes 3145728 | tf_op jit(solution)/shard_map/all_to_all | solution.py:683
  13.4 2.3 %shard_map.96 = (f32[128,2,8,128]{3,2,1,0:T(8,128)S(1)}, f32[4,8,128]{2,1,0:T(8,128)S(1)}, f32[2,8,128]{2,1,0:T(8,128)S(1)}) custom-call(f32[3072,128]{1,0:T(8,128)} %shard_map.95.after_ref, f32[1024,128]{1,0:T(8,128)} %bitcast.308, f32[1024,128]{1,0:T(8,128)} %bitcast.302, f32[1024,128]{1,0:T(8,128)} %bitcast.304, f32[1024,128]{1,0:T(8,128)S(1)} %bitcast.300, ...), custom_call_target="tpu_custom_call" | custom-call | tf_op jit(solution)/shard_map/pallas_call | solution.py:408
  15.8 1.0 %collective-permute-start.21 = (f32[4,8,128]{2,1,0:T(8,128)S(1)}, f32[4,8,128]{2,1,0:T(8,128)S(1)}, u32[]{:S(2)}, u32[]{:S(2)}) collective-permute-start(f32[4,8,128]{2,1,0:T(8,128)S(1)} %get-tuple-element.67), channel_id=1, source_target_pairs={{0,1},{1,0},{2,3},{3,2},{4,5},{5,4},{6,7},{7,6},{8,9},{9,8},{10,11... | collective-permute-start | bytes 49160 | tf_op jit(solution)/shard_map/ppermute | solution.py:636
  16.8 2.9 %collective-permute-start.23 = (f32[4,8,128]{2,1,0:T(8,128)S(1)}, f32[4,8,128]{2,1,0:T(8,128)S(1)}, u32[]{:S(2)}, u32[]{:S(2)}) collective-permute-start(f32[4,8,128]{2,1,0:T(8,128)S(1)} %get-tuple-element.67), channel_id=1, source_target_pairs={{0,4},{1,5},{2,6},{3,7},{4,0},{5,1},{6,2},{7,3},{8,12},{9,13},{10,... | collective-permute-start | bytes 49160 | tf_op jit(solution)/shard_map/ppermute | solution.py:640
  20.9 3.2 %collective-permute-done.22 = f32[8,8,128]{2,1,0:T(8,128)S(1)} collective-permute-done((f32[8,8,128]{2,1,0:T(8,128)S(1)}, f32[8,8,128]{2,1,0:T(8,128)S(1)}, u32[]{:S(2)}, u32[]{:S(2)}) %collective-permute-start.22) | collective-permute-done | bytes 32800 | tf_op jit(solution)/shard_map/ppermute | solution.py:641
  24.1 1.2 %collective-permute-done.24 = f32[12,8,128]{2,1,0:T(8,128)S(1)} collective-permute-done((f32[12,8,128]{2,1,0:T(8,128)S(1)}, f32[12,8,128]{2,1,0:T(8,128)S(1)}, u32[]{:S(2)}, u32[]{:S(2)}) %collective-permute-start.24) | collective-permute-done | bytes 49184 | tf_op jit(solution)/shard_map/ppermute | solution.py:643
  25.3 11.0 %all-to-all-done.2 = f32[16,192,128]{2,1,0:T(8,128)S(1)} async-done(((f32[16,192,128]{2,1,0:T(8,128)}), f32[16,192,128]{2,1,0:T(8,128)S(1)}, u32[]{:S(2)}, u32[]{:S(2)}) %all-to-all-start.2) | async-done | bytes 1572896 | tf_op jit(solution)/shard_map/all_to_all | solution.py:683
  36.3 2.6 %shard_map.97 = (f32[1024,128]{1,0:T(8,128)}, f32[1,8,128]{2,1,0:T(8,128)S(1)}) custom-call(f32[32,8,128]{2,1,0:T(8,128)S(1)} %constant_dynamic-update-slice_fusion.after_ref.matrix_ref, f32[3072,128]{1,0:T(8,128)S(1)} %bitcast.297), custom_call_target="tpu_custom_call" | custom-call | tf_op jit(solution)/shard_map/pallas_call | solution.py:355
  38.9 4.7 %all-to-all-start.3 = ((f32[16,64,128]{2,1,0:T(8,128)}), f32[16,64,128]{2,1,0:T(8,128)S(1)}, u32[]{:S(2)}, u32[]{:S(2)}) async-start(f32[16,64,128]{2,1,0:T(8,128)} %bitcast.108), calls=%async_computation.3 | async-start | bytes 1048576 | tf_op jit(solution)/shard_map/all_to_all | solution.py:688
  43.7 10.0 %all-to-all-done.3 = f32[16,64,128]{2,1,0:T(8,128)S(1)} async-done(((f32[16,64,128]{2,1,0:T(8,128)}), f32[16,64,128]{2,1,0:T(8,128)S(1)}, u32[]{:S(2)}, u32[]{:S(2)}) %all-to-all-start.3) | async-done | bytes 524320 | tf_op jit(solution)/shard_map/all_to_all | solution.py:688
  54.5 2.4 %collective-permute-start.25 = (f32[3,8,128]{2,1,0:T(8,128)S(1)}, f32[3,8,128]{2,1,0:T(8,128)S(1)}, u32[]{:S(2)}, u32[]{:S(2)}) collective-permute-start(f32[3,8,128]{2,1,0:T(8,128)S(1)} %shard_map.98), channel_id=1, source_target_pairs={{0,1},{1,0},{2,3},{3,2},{4,5},{5,4},{6,7},{7,6},{8,9},{9,8},{10,11... | collective-permute-start | bytes 36872 | tf_op jit(solution)/shard_map/ppermute | solution.py:636
  56.9 2.9 %collective-permute-start.27 = (f32[3,8,128]{2,1,0:T(8,128)S(1)}, f32[3,8,128]{2,1,0:T(8,128)S(1)}, u32[]{:S(2)}, u32[]{:S(2)}) collective-permute-start(f32[3,8,128]{2,1,0:T(8,128)S(1)} %shard_map.98), channel_id=1, source_target_pairs={{0,4},{1,5},{2,6},{3,7},{4,0},{5,1},{6,2},{7,3},{8,12},{9,13},{10,... | collective-permute-start | bytes 36872 | tf_op jit(solution)/shard_map/ppermute | solution.py:640
  60.3 2.1 %shard_map.99.middle_ref = f32[128,10,8,128]{3,2,1,0:T(8,128)S(1)} custom-call(f32[6,8,128]{2,1,0:T(8,128)S(1)} %pad_maximum_fusion.19.after_ref, s32[2]{0:T(128)S(1)} %pad_add_fusion.1.where_ref, f32[128,8,128]{2,1,0:T(8,128)S(1)} %bitcast.299, f32[1024,128]{1,0:T(8,128)} %bitcast.309, f32[1024,128]{1,0:T(8,128)S(1)} %bitcast.303, f32[1024,128]{1,0:T(8,128)} %bitcast.305, ...), custom_call_target="tpu_custom_call" | custom-call | tf_op jit(solution)/shard_map/pallas_call | solution.py:522
  62.4 1.4 %collective-permute-done.26 = f32[6,8,128]{2,1,0:T(8,128)S(1)} collective-permute-done((f32[6,8,128]{2,1,0:T(8,128)S(1)}, f32[6,8,128]{2,1,0:T(8,128)S(1)}, u32[]{:S(2)}, u32[]{:S(2)}) %collective-permute-start.26) | collective-permute-done | bytes 24608 | tf_op jit(solution)/shard_map/ppermute | solution.py:641
  64.1 0.9 %collective-permute-done.28 = f32[9,8,128]{2,1,0:T(8,128)S(1)} collective-permute-done((f32[9,8,128]{2,1,0:T(8,128)S(1)}, f32[9,8,128]{2,1,0:T(8,128)S(1)}, u32[]{:S(2)}, u32[]{:S(2)}) %collective-permute-start.28) | collective-permute-done | bytes 36896 | tf_op jit(solution)/shard_map/ppermute | solution.py:643
  65.0 1.3 %shard_map.100 = (f32[128,5,8,128]{3,2,1,0:T(8,128)S(1)}, f32[6,8,128]{2,1,0:T(8,128)S(1)}) custom-call(s32[2]{0:T(128)S(1)} %pad_add_fusion.1.where_ref, f32[32,8,128]{2,1,0:T(8,128)S(1)} %constant_dynamic-update-slice_fusion.after_ref.matrix_ref, f32[24,8,128]{2,1,0:T(8,128)S(1)} %constant_dynamic-update-slice_fusion.5.loads_ref, ...), custom_call_target="tpu_custom_call" | custom-call | tf_op jit(solution)/shard_map/pallas_call | solution.py:573
  66.7 1.3 %collective-permute-start.31 = (f32[6,8,128]{2,1,0:T(8,128)S(1)}, f32[6,8,128]{2,1,0:T(8,128)S(1)}, u32[]{:S(2)}, u32[]{:S(2)}) collective-permute-start(f32[6,8,128]{2,1,0:T(8,128)S(1)} %get-tuple-element.72), channel_id=1, source_target_pairs={{0,4},{1,5},{2,6},{3,7},{4,0},{5,1},{6,2},{7,3},{8,12},{9,13},{10,... | collective-permute-start | bytes 73736 | tf_op jit(solution)/shard_map/ppermute | solution.py:640
  68.0 1.3 %collective-permute-start.30 = (f32[12,8,128]{2,1,0:T(8,128)S(1)}, f32[12,8,128]{2,1,0:T(8,128)S(1)}, u32[]{:S(2)}, u32[]{:S(2)}) collective-permute-start(f32[12,8,128]{2,1,0:T(8,128)S(1)} %pad_maximum_fusion.16), channel_id=1, source_target_pairs={{0,6},{1,3},{2,0},{3,5},{4,2},{5,7},{6,4},{7,1},{8,14},{9,11},{10,... | collective-permute-start | bytes 147464 | tf_op jit(solution)/shard_map/ppermute | solution.py:641
  69.3 1.5 %collective-permute-done.31 = f32[6,8,128]{2,1,0:T(8,128)S(1)} collective-permute-done((f32[6,8,128]{2,1,0:T(8,128)S(1)}, f32[6,8,128]{2,1,0:T(8,128)S(1)}, u32[]{:S(2)}, u32[]{:S(2)}) %collective-permute-start.31) | collective-permute-done | bytes 24608 | tf_op jit(solution)/shard_map/ppermute | solution.py:640
  70.9 1.3 %collective-permute-done.30 = f32[12,8,128]{2,1,0:T(8,128)S(1)} collective-permute-done((f32[12,8,128]{2,1,0:T(8,128)S(1)}, f32[12,8,128]{2,1,0:T(8,128)S(1)}, u32[]{:S(2)}, u32[]{:S(2)}) %collective-permute-start.30) | collective-permute-done | bytes 49184 | tf_op jit(solution)/shard_map/ppermute | solution.py:641
  72.7 0.8 %collective-permute-done.32 = f32[18,8,128]{2,1,0:T(8,128)S(1)} collective-permute-done((f32[18,8,128]{2,1,0:T(8,128)S(1)}, f32[18,8,128]{2,1,0:T(8,128)S(1)}, u32[]{:S(2)}, u32[]{:S(2)}) %collective-permute-start.32) | collective-permute-done | bytes 73760 | tf_op jit(solution)/shard_map/ppermute | solution.py:643
  73.5 2.3 %shard_map.101 = (f32[1024,128]{1,0:T(8,128)}, f32[1024,128]{1,0:T(8,128)}, s32[1]{0:T(128)}) custom-call(s32[2]{0:T(128)S(1)} %pad_add_fusion.1.where_ref, f32[24,8,128]{2,1,0:T(8,128)S(1)} %constant_dynamic-update-slice_fusion.5.loads_ref, f32[48,8,128]{2,1,0:T(8,128)S(1)} %constant_dynamic-update-slice_fusion.10.ports_ref, ...), custom_call_target="tpu_custom_call" | custom-call | tf_op jit(solution)/shard_map/pallas_call | solution.py:620
  75.9 0.8 %while.11 = (f32[128,1024]{1,0:T(8,128)}, f32[128,1024]{1,0:T(8,128)}, s32[]{:T(128)}, f32[128,1024]{1,0:T(8,128)S(1)}, f32[128,1024]{1,0:T(8,128)S(1)}, /*index...) while((f32[128,1024]{1,0:T(8,128)}, ...), condition=%region_7.8_spmd, body=%region_0.7_spmd | while | flops 85193968 | bytes 417096736 | solution.py:700
  (48 shorter events, 3.6 us)
Async XLA Ops:
  4.8 8.6 %copy-start = (f32[128,1024]{1,0:T(8,128)S(1)}, f32[128,1024]{1,0:T(8,128)}, u32[]{:S(2)}) copy-start(f32[128,1024]{1,0:T(8,128)} %param.13) | copy-start | bytes 1572868
  4.8 31.5 %all-to-all-start.2 = ((f32[16,192,128]{2,1,0:T(8,128)}), f32[16,192,128]{2,1,0:T(8,128)S(1)}, u32[]{:S(2)}, u32[]{:S(2)}) async-start(f32[16,192,128]{2,1,0:T(8,128)} %bitcast.106), calls=%async_computation.2 | async-start | bytes 3145728 | tf_op jit(solution)/shard_map/all_to_all | solution.py:683
  15.8 4.0 %collective-permute-start.21 = (f32[4,8,128]{2,1,0:T(8,128)S(1)}, f32[4,8,128]{2,1,0:T(8,128)S(1)}, u32[]{:S(2)}, u32[]{:S(2)}) collective-permute-start(f32[4,8,128]{2,1,0:T(8,128)S(1)} %get-tuple-element.67), channel_id=1, source_target_pairs={{0,1},{1,0},{2,3},{3,2},{4,5},{5,4},{6,7},{7,6},{8,9},{9,8},{10,11... | collective-permute-start | bytes 49160 | tf_op jit(solution)/shard_map/ppermute | solution.py:636
  16.8 4.1 %collective-permute-start.23 = (f32[4,8,128]{2,1,0:T(8,128)S(1)}, f32[4,8,128]{2,1,0:T(8,128)S(1)}, u32[]{:S(2)}, u32[]{:S(2)}) collective-permute-start(f32[4,8,128]{2,1,0:T(8,128)S(1)} %get-tuple-element.67), channel_id=1, source_target_pairs={{0,4},{1,5},{2,6},{3,7},{4,0},{5,1},{6,2},{7,3},{8,12},{9,13},{10,... | collective-permute-start | bytes 49160 | tf_op jit(solution)/shard_map/ppermute | solution.py:640
  19.8 4.3 %collective-permute-start.22 = (f32[8,8,128]{2,1,0:T(8,128)S(1)}, f32[8,8,128]{2,1,0:T(8,128)S(1)}, u32[]{:S(2)}, u32[]{:S(2)}) collective-permute-start(f32[8,8,128]{2,1,0:T(8,128)S(1)} %pad_maximum_fusion.18), channel_id=1, source_target_pairs={{0,6},{1,3},{2,0},{3,5},{4,2},{5,7},{6,4},{7,1},{8,14},{9,11},{10,... | collective-permute-start | bytes 98312 | tf_op jit(solution)/shard_map/ppermute | solution.py:641
  24.1 1.2 %collective-permute-start.24 = (f32[12,8,128]{2,1,0:T(8,128)S(1)}, f32[12,8,128]{2,1,0:T(8,128)S(1)}, u32[]{:S(2)}, u32[]{:S(2)}) collective-permute-start(f32[12,8,128]{2,1,0:T(8,128)S(1)} %pad_maximum_fusion.15), channel_id=1, source_target_pairs={{0,1},{1,0},{2,3},{3,2},{4,5},{5,4},{6,7},{7,6},{8,9},{9,8},{10,11... | collective-permute-start | bytes 147464 | tf_op jit(solution)/shard_map/ppermute | solution.py:643
  38.9 21.4 %copy-start.1 = (f32[128,1024]{1,0:T(8,128)S(1)}, f32[128,1024]{1,0:T(8,128)}, u32[]{:S(2)}) copy-start(f32[128,1024]{1,0:T(8,128)} %param.11) | copy-start | bytes 1572868
  38.9 14.8 %all-to-all-start.3 = ((f32[16,64,128]{2,1,0:T(8,128)}), f32[16,64,128]{2,1,0:T(8,128)S(1)}, u32[]{:S(2)}, u32[]{:S(2)}) async-start(f32[16,64,128]{2,1,0:T(8,128)} %bitcast.108), calls=%async_computation.3 | async-start | bytes 1048576 | tf_op jit(solution)/shard_map/all_to_all | solution.py:688
  54.5 5.4 %collective-permute-start.25 = (f32[3,8,128]{2,1,0:T(8,128)S(1)}, f32[3,8,128]{2,1,0:T(8,128)S(1)}, u32[]{:S(2)}, u32[]{:S(2)}) collective-permute-start(f32[3,8,128]{2,1,0:T(8,128)S(1)} %shard_map.98), channel_id=1, source_target_pairs={{0,1},{1,0},{2,3},{3,2},{4,5},{5,4},{6,7},{7,6},{8,9},{9,8},{10,11... | collective-permute-start | bytes 36872 | tf_op jit(solution)/shard_map/ppermute | solution.py:636
  56.9 5.5 %collective-permute-start.27 = (f32[3,8,128]{2,1,0:T(8,128)S(1)}, f32[3,8,128]{2,1,0:T(8,128)S(1)}, u32[]{:S(2)}, u32[]{:S(2)}) collective-permute-start(f32[3,8,128]{2,1,0:T(8,128)S(1)} %shard_map.98), channel_id=1, source_target_pairs={{0,4},{1,5},{2,6},{3,7},{4,0},{5,1},{6,2},{7,3},{8,12},{9,13},{10,... | collective-permute-start | bytes 36872 | tf_op jit(solution)/shard_map/ppermute | solution.py:640
  59.9 3.9 %collective-permute-start.26 = (f32[6,8,128]{2,1,0:T(8,128)S(1)}, f32[6,8,128]{2,1,0:T(8,128)S(1)}, u32[]{:S(2)}, u32[]{:S(2)}) collective-permute-start(f32[6,8,128]{2,1,0:T(8,128)S(1)} %pad_maximum_fusion.19.after_ref), channel_id=1, source_target_pairs={{0,6},{1,3},{2,0},{3,5},{4,2},{5,7},{6,4},{7,1},{8,14},{9,11},{10,... | collective-permute-start | bytes 73736 | tf_op jit(solution)/shard_map/ppermute | solution.py:641
  63.7 1.2 %collective-permute-start.28 = (f32[9,8,128]{2,1,0:T(8,128)S(1)}, f32[9,8,128]{2,1,0:T(8,128)S(1)}, u32[]{:S(2)}, u32[]{:S(2)}) collective-permute-start(f32[9,8,128]{2,1,0:T(8,128)S(1)} %pad_maximum_fusion.17), channel_id=1, source_target_pairs={{0,1},{1,0},{2,3},{3,2},{4,5},{5,4},{6,7},{7,6},{8,9},{9,8},{10,11... | collective-permute-start | bytes 110600 | tf_op jit(solution)/shard_map/ppermute | solution.py:643
  66.3 1.7 %collective-permute-start.29 = (f32[6,8,128]{2,1,0:T(8,128)S(1)}, f32[6,8,128]{2,1,0:T(8,128)S(1)}, u32[]{:S(2)}, u32[]{:S(2)}) collective-permute-start(f32[6,8,128]{2,1,0:T(8,128)S(1)} %get-tuple-element.72), channel_id=1, source_target_pairs={{0,1},{1,0},{2,3},{3,2},{4,5},{5,4},{6,7},{7,6},{8,9},{9,8},{10,11... | collective-permute-start | bytes 73736 | tf_op jit(solution)/shard_map/ppermute | solution.py:636
  66.7 4.2 %collective-permute-start.31 = (f32[6,8,128]{2,1,0:T(8,128)S(1)}, f32[6,8,128]{2,1,0:T(8,128)S(1)}, u32[]{:S(2)}, u32[]{:S(2)}) collective-permute-start(f32[6,8,128]{2,1,0:T(8,128)S(1)} %get-tuple-element.72), channel_id=1, source_target_pairs={{0,4},{1,5},{2,6},{3,7},{4,0},{5,1},{6,2},{7,3},{8,12},{9,13},{10,... | collective-permute-start | bytes 73736 | tf_op jit(solution)/shard_map/ppermute | solution.py:640
  68.0 4.2 %collective-permute-start.30 = (f32[12,8,128]{2,1,0:T(8,128)S(1)}, f32[12,8,128]{2,1,0:T(8,128)S(1)}, u32[]{:S(2)}, u32[]{:S(2)}) collective-permute-start(f32[12,8,128]{2,1,0:T(8,128)S(1)} %pad_maximum_fusion.16), channel_id=1, source_target_pairs={{0,6},{1,3},{2,0},{3,5},{4,2},{5,7},{6,4},{7,1},{8,14},{9,11},{10,... | collective-permute-start | bytes 147464 | tf_op jit(solution)/shard_map/ppermute | solution.py:641
  72.2 1.3 %collective-permute-start.32 = (f32[18,8,128]{2,1,0:T(8,128)S(1)}, f32[18,8,128]{2,1,0:T(8,128)S(1)}, u32[]{:S(2)}, u32[]{:S(2)}) collective-permute-start(f32[18,8,128]{2,1,0:T(8,128)S(1)} %pad_maximum_fusion.14), channel_id=1, source_target_pairs={{0,1},{1,0},{2,3},{3,2},{4,5},{5,4},{6,7},{7,6},{8,9},{9,8},{10,11... | collective-permute-start | bytes 221192 | tf_op jit(solution)/shard_map/ppermute | solution.py:643
  72.6 3.2 %copy-start.2 = (f32[128,1024]{1,0:T(8,128)S(1)}, f32[128,1024]{1,0:T(8,128)}, u32[]{:S(2)}) copy-start(f32[128,1024]{1,0:T(8,128)} %param.12) | copy-start | bytes 1572868
  72.6 3.2 %copy-start.3 = (f32[128,1024]{1,0:T(8,128)S(1)}, f32[128,1024]{1,0:T(8,128)}, u32[]{:S(2)}) copy-start(f32[128,1024]{1,0:T(8,128)} %param.14) | copy-start | bytes 1572868
  72.6 3.2 %copy-start.4 = (f32[128,1024]{1,0:T(8,128)S(1)}, f32[128,1024]{1,0:T(8,128)}, u32[]{:S(2)}) copy-start(f32[128,1024]{1,0:T(8,128)} %param.10) | copy-start | bytes 1572868
  72.6 3.2 %copy-start.19 = (s32[1,2048,1]{1,2,0:T(1,128)S(1)}, s32[1,2048,1]{1,2,0:T(1,128)}, u32[]{:S(2)}) copy-start(s32[1,2048,1]{1,2,0:T(1,128)} %param.16) | copy-start | bytes 24580
  72.6 3.2 %copy-start.20 = (s32[1,2048]{1,0:T(1,128)S(1)}, s32[1,2048]{1,0:T(1,128)}, u32[]{:S(2)}) copy-start(s32[1,2048]{1,0:T(1,128)} %param.17) | copy-start | bytes 24580
